TPU v7x, 32 devices: a whole 2x2x4 slice. The times are simulated.
32 devices in a mesh: grp: 2 (over y), dp: 4 (over z), query: 2 (over x), proj: 2 (over core).
Axes of the slice: x: 2, y: 2, z: 4, core: 2. Of those that a mesh axis runs over, the one named last changes fastest.
Arguments:
- activations: bfloat16 [8192, 4096], P(('grp', 'dp', 'query'), 'proj'), parts along dimension 0
- out_grads: bfloat16 [8192, 14336], P(('grp', 'dp', 'query'), 'proj'), parts along dimension 0
- proj_in: bfloat16 [4096, 32], P('proj'), may hold values from -0.09375 to 0.09375
- proj_out: bfloat16 [14336, 32], P('proj'), may hold values from -0.046875 to 0.046875
- lengths: int32 [16, 17], P(('grp', 'dp', 'query')), parts along dimension 0, may hold values from 1 to 128, 512 in all within a row
- queries: float32 [2, 512, 1024], P('query', 'dp'), may hold values from -6 to 6
Outputs:
- scores: float32 [256, 1024], P(('grp', 'dp'), 'query'), parts along dimension 0
There are 2 independent parts, one for each index of `grp`. A program takes and returns all parts, laid end to end along the dimension named above; an argument that names none is the same for every part. Nothing has to cross between parts.
Inputs may be any that keep to these rules, and one draw needn't show every extreme that they name: `lengths`: each row sums to 512; some entry equals 128.
All inputs are finite; a program needn't handle non-finite values.
Results may differ from a plain program's by a relative error of at most 0.0003.
Values sent between devices are 32-bit elements; how exact they have to be, the bound alone decides.
No kernel may reach another device: no remote copies, remote signals or barrier semaphores. Data moves between devices by JAX's collectives and lax.ppermute only.
A program may use at most 64 MiB of HBM per device.

v0:
```python
import jax
import jax.numpy as jnp
from jax import lax
from jax.sharding import PartitionSpec as P


def membership(lengths, slots):
    counts = lengths[:, :-1]
    ends = jnp.cumsum(counts, axis=1)
    starts = ends - counts
    positions = jnp.arange(slots, dtype=jnp.int32)
    inside = (positions[None, None, :] >= starts[:, :, None]) & (
        positions[None, None, :] < ends[:, :, None]
    )
    member = inside.astype(jnp.float32)
    live = jnp.sum(member, axis=1)
    return (member, live, counts.astype(jnp.float32))


def precondition(input_fisher, output_fisher, grads):
    width = input_fisher.shape[0]
    identity = jnp.eye(width, dtype=jnp.float32)

    def inverse(fisher):
        scaled = fisher * (width / jnp.trace(fisher)) + 1.0 * identity
        factor = jnp.linalg.cholesky(scaled)
        return jax.scipy.linalg.cho_solve((factor, True), identity)

    in_inverse = inverse(input_fisher)
    out_inverse = inverse(output_fisher)
    left_side = jnp.einsum("ik,nkl->nil", out_inverse, grads, precision=lax.Precision.HIGHEST)
    both_sides = jnp.einsum("nil,lj->nij", left_side, in_inverse, precision=lax.Precision.HIGHEST)
    return both_sides.reshape(grads.shape[0], width * width)


def score_block(left, right, width):
    return jnp.einsum("ek,nk->en", left, right, precision=lax.Precision.HIGHEST) / width


def body(activations, out_grads, proj_in, proj_out, lengths, queries):
    width = proj_in.shape[1]
    slots = activations.shape[0]
    input_part = jnp.dot(activations, proj_in, preferred_element_type=jnp.float32)
    output_part = jnp.dot(out_grads, proj_out, preferred_element_type=jnp.float32)
    input_proj, output_proj = lax.psum((input_part, output_part), "proj")
    member, live, counts = membership(lengths, slots)
    outer = (output_proj[:, :, None] * input_proj[:, None, :]).reshape(slots, width * width)
    summed = jnp.dot(
        member[0], outer, precision=lax.Precision.HIGHEST, preferred_element_type=jnp.float32
    )
    example_grads = summed / counts[0][:, None]
    masked_in = input_proj * live[0][:, None]
    masked_out = output_proj * live[0][:, None]
    local_in = jnp.einsum("ti,tj->ij", masked_in, input_proj, precision=lax.Precision.HIGHEST)
    local_out = jnp.einsum("ti,tj->ij", masked_out, output_proj, precision=lax.Precision.HIGHEST)
    input_fisher, output_fisher = lax.psum((local_in, local_out), ("dp", "query"))
    conditioned = precondition(input_fisher, output_fisher, queries[0].reshape(-1, width, width))
    row_grads = lax.all_gather(example_grads, "query", axis=0, tiled=True)
    return score_block(
        row_grads, lax.all_gather(conditioned[None], "dp", axis=1, tiled=True)[0], width
    )


def solution(mesh):
    in_specs = (
        P(("grp", "dp", "query"), "proj"),
        P(("grp", "dp", "query"), "proj"),
        P("proj", None),
        P("proj", None),
        P(("grp", "dp", "query"), None),
        P("query", "dp", None),
    )
    out_specs = P(("grp", "dp"), "query")
    return jax.shard_map(body, mesh=mesh, in_specs=in_specs, out_specs=out_specs, check_vma=False)
```

profile of v0, /device:TPU:0, one launch (start us, length us, event | category | flops | bytes accessed | tf_op | source)
XLA Modules:
  0.0 150.7 jit_solution(12989239694949339405)
XLA Ops:
  6.5 1.6 %copy-done = bf16[512,2048]{1,0:T(8,128)(2,1)S(1)} copy-done((bf16[512,2048]{1,0:T(8,128)(2,1)S(1)}, bf16[512,2048]{1,0:T(8,128)(2,1)}, u32[]{:S(2)}) %copy-start) | copy-done | bytes 2097176
  8.1 2.3 %fusion.32 = f32[512,32]{0,1:T(8,128)} fusion(bf16[512,2048]{1,0:T(8,128)(2,1)S(1)} %copy-done, bf16[2048,32]{0,1:T(8,128)(2,1)} %param.11), kind=kOutput, calls=%fused_computation.56 | convolution fusion | flops 67108864 | bytes 2293760 | tf_op jit(solution)/shard_map/dot_general | solution.py:43
  10.4 6.1 %fusion.31 = f32[512,32]{0,1:T(8,128)} fusion(bf16[512,7168]{1,0:T(8,128)(2,1)} %param.10, bf16[7168,32]{0,1:T(8,128)(2,1)S(1)} %copy-done.4), kind=kOutput, calls=%fused_computation.55 | convolution fusion | flops 234881024 | bytes 7864320 | tf_op jit(solution)/shard_map/dot_general | solution.py:44
  17.0 20.3 %all-reduce.4.cloned.1.call-done = (f32[512,32]{0,1:T(8,128)}, f32[512,32]{0,1:T(8,128)}) async-done(((f32[512,32]{0,1:T(8,128)}, f32[512,32]{0,1:T(8,128)}), (f32[512,32]{0,1:T(8,128)}, f32[512,32]{0,1:T(8,128)})) %all-reduce.4.cloned.1.call-update) | async-done | bytes 131088 | tf_op jit(solution)/shard_map/psum | solution.py:45
  37.3 1.2 fusion.8
  38.5 1.1 fusion.10
  39.6 37.3 %all-reduce = (f32[32,32]{0,1:T(8,128)S(1)}, f32[32,32]{0,1:T(8,128)S(1)}) all-reduce(f32[32,32]{0,1:T(8,128)S(1)} %fusion.8, f32[32,32]{0,1:T(8,128)S(1)} %fusion.10), channel_id=1, replica_groups=mesh['grp'=2,'dp'=4,'query'=2,'proj'=2] {'dp','query'}, use_global_device_ids=true, to_apply=%region_8.11 | all-reduce | flops 2048 | bytes 16384 | tf_op jit(solution)/shard_map/psum | solution.py:56
  77.0 0.6 select_reduce_fusion.2
  77.6 0.7 select_reduce_fusion.3
  79.8 2.9 %cholesky.55 = f32[32,32]{1,0:T(8,128)S(1)} custom-call(f32[32,32]{1,0:T(8,128)S(1)} %fusion.25), custom_call_target="Cholesky" | custom-call | tf_op jit(solution)/shard_map/jit(cholesky)/cholesky | solution.py:26
  82.7 0.6 compare_reduce_fusion
  83.4 0.7 fusion.22
  84.0 2.5 %custom-call.9 = f32[1,32,32]{1,2,0:T(8,128)S(1)} custom-call(f32[1,32,32]{2,1,0:T(8,128)S(1)} %fusion.22), custom_call_target="InvertDiagBlocksLowerTriangular" | custom-call | tf_op jit(solution)/shard_map/jit(_cho_solve)/triangular_solve | solution.py:27
  87.0 2.9 %cholesky.44 = f32[32,32]{1,0:T(8,128)S(1)} custom-call(f32[32,32]{1,0:T(8,128)S(1)} %fusion.28), custom_call_target="Cholesky" | custom-call | tf_op jit(solution)/shard_map/jit(cholesky)/cholesky | solution.py:26
  90.0 0.6 compare_reduce_fusion.1
  90.6 0.7 fusion.21
  91.3 2.5 %custom-call.8 = f32[1,32,32]{1,2,0:T(8,128)S(1)} custom-call(f32[1,32,32]{2,1,0:T(8,128)S(1)} %fusion.21), custom_call_target="InvertDiagBlocksLowerTriangular" | custom-call | tf_op jit(solution)/shard_map/jit(_cho_solve)/triangular_solve | solution.py:27
  94.1 0.9 convolution_bitcast_fusion
  95.0 1.7 %fusion.5 = f32[128,32,32]{0,2,1:T(8,128)} fusion(f32[32,32,1]{0,1,2:T(8,128)S(1)} %convolution_bitcast_fusion.1, f32[128,32,32]{0,1,2:T(8,128)S(1)} %convolution_bitcast_fusion), kind=kOutput, calls=%fused_computation.8 | convolution fusion | flops 50331648 | bytes 1052672 | tf_op jit(solution)/shard_map/nil,lj->nij/dot_general | solution.py:32
  96.7 0.3 broadcast_multiply_fusion
  97.0 1.1 convolution_divide_fusion
  98.1 4.9 %all_gather.6 = f32[32,1024]{1,0:T(8,128)S(1)} all-gather(f32[16,1024]{1,0:T(8,128)S(1)} %convolution_divide_fusion), channel_id=1, replica_groups=mesh['grp'=2,'dp'=4,'query'=2,'proj'=2] {'query'}, dimensions={0}, use_global_device_ids=true | all-gather | bytes 196608 | tf_op jit(solution)/shard_map/all_gather | solution.py:58
  103.0 37.3 %all-gather.2.cloned.1.call-done = f32[1,512,1024]{1,2,0:T(8,128)} async-done(((f32[1,128,1024]{1,2,0:T(8,128)}), f32[1,512,1024]{1,2,0:T(8,128)}) %all-gather.2.cloned.1.call-update) | async-done | bytes 2097168 | tf_op jit(solution)/shard_map/all_gather | solution.py:60
  140.3 3.5 %fusion.2 = f32[32,512]{1,0:T(8,128)} fusion(f32[32,1024]{1,0:T(8,128)S(1)} %all_gather.6, f32[1,512,1024]{1,2,0:T(8,128)} %all-gather.2.cloned.1.call-done), kind=kOutput, calls=%fused_computation.4 | convolution fusion | flops 201342976 | bytes 2293760 | tf_op jit(solution)/shard_map/ek,nk->en/dot_general | solution.py:37
  (30 shorter events, 1.6 us)
Async XLA Ops:
  6.5 1.6 %copy-start = (bf16[512,2048]{1,0:T(8,128)(2,1)S(1)}, bf16[512,2048]{1,0:T(8,128)(2,1)}, u32[]{:S(2)}) copy-start(bf16[512,2048]{1,0:T(8,128)(2,1)} %param.9) | copy-start | bytes 6291460
  6.5 3.9 %copy-start.4 = (bf16[7168,32]{0,1:T(8,128)(2,1)S(1)}, bf16[7168,32]{0,1:T(8,128)(2,1)}, u32[]{:S(2)}) copy-start(bf16[7168,32]{0,1:T(8,128)(2,1)} %param.12) | copy-start | bytes 1376260
  6.5 30.8 %all-reduce.4.cloned.1.call-start = ((), (), s32[]{:S(2)}) async-start(), calls=%async_computation.1 | async-start | bytes 262144 | tf_op jit(solution)/shard_map/psum | solution.py:45
  10.4 6.1 %copy-start.5 = (s32[1,17]{1,0:T(1,128)S(1)}, s32[1,17]{1,0:T(1,128)}, u32[]{:S(2)}) copy-start(s32[1,17]{1,0:T(1,128)} %param.13) | copy-start | bytes 208
  10.4 6.3 %copy-start.3 = (f32[1,128,1024]{2,1,0:T(8,128)S(1)}, f32[1,128,1024]{2,1,0:T(8,128)}, u32[]{:S(2)}) copy-start(f32[1,128,1024]{2,1,0:T(8,128)} %param.14) | copy-start | bytes 1572868
  16.5 123.8 %all-gather.2.cloned.1.call-start = ((), (), s32[]{:S(2)}) async-start(), calls=%async_computation | async-start | bytes 2621440 | tf_op jit(solution)/shard_map/all_gather | solution.py:60
  37.3 59.4 %copy-start.1 = (f32[512,32]{0,1:T(8,128)S(1)}, f32[512,32]{0,1:T(8,128)}, u32[]{:S(2)}) copy-start(f32[512,32]{0,1:T(8,128)} %get-tuple-element.9) | copy-start | bytes 196612
  37.3 59.4 %copy-start.2 = (f32[512,32]{0,1:T(8,128)S(1)}, f32[512,32]{0,1:T(8,128)}, u32[]{:S(2)}) copy-start(f32[512,32]{0,1:T(8,128)} %get-tuple-element.10) | copy-start | bytes 196612
Sparse Core Ops, SparseCore 0:
  16.6 20.6 all-reduce.3
  96.8 43.4 all-gather.1
where the time goes:
time: 151 us
  waiting for transfers between devices  57.6 us (38%)
  blocking collectives  42.3 us (28%)
  matrix products  18.6 us (12%)
  other arithmetic  15.3 us (10%)
  between operations  14.9 us (10%)
  local copies, waits for them, and re-layouts  1.94 us (1%)
    psum x1, blocking collectives, body(): lax.psum((local_in, local_out), ('dp', 'query'))  37.3 us
    all_gather x1, waiting for transfers between devices, body(): lax.all_gather(conditioned[None], 'dp', axis=1, tiled=True)[0]  37.3 us
    psum x1, waiting for transfers between devices, body(): input_proj, output_proj = lax.psum((input_part, output_part), 'proj')  20.3 us
    another operation x6, other arithmetic, inverse(): factor = jnp.linalg.cholesky(scaled)  7.19 us
    another operation x4, other arithmetic, inverse(): return jax.scipy.linalg.cho_solve((factor, True), identity)  6.22 us
    dot_general x1, matrix products, body(): jnp.dot(out_grads, proj_out, preferred_element_type=jnp.float32)  6.06 us
    all_gather x1, blocking collectives, body(): row_grads = lax.all_gather(example_grads, 'query', axis=0, tiled=True)  4.94 us
    dot_general x1, matrix products, score_block(): jnp.einsum('ek,nk->en', left, right, precision=lax.Precision.HIGHEST)  3.51 us
  transfers between devices with their start and end apart: 2, of which 2 were waited for; matrix products, arithmetic and copies ran while one was open for 1% of the time, Pallas kernels for 0%

commit v1 on v0

v1 whole, which is shorter than its diff:
```python
import functools

import jax
import jax.numpy as jnp
from jax import lax
from jax.experimental import pallas as pl
from jax.experimental.pallas import tpu as pltpu
from jax.sharding import PartitionSpec as P

F32 = jnp.float32
BF16 = jnp.bfloat16
HIGHEST = lax.Precision.HIGHEST
NT = (((1,), (1,)), ((), ()))
AXES = ("dp", "query", "proj")
MIB = 2**20


def swap(value, mesh, mask):
    count = mesh.shape["dp"] * mesh.shape["query"] * mesh.shape["proj"]
    return lax.ppermute(value, AXES, [(i, i ^ mask) for i in range(count)])


def bits_of(size):
    return [1 << b for b in range(size.bit_length() - 1)]


def project_kernel(plan, a_hbm, g_hbm, p_in_hbm, p_out_hbm, out_ref, a_buf, g_buf, p_in, p_out, sems, p_sems):
    width = p_in.shape[0]
    p_copies = {
        "a": pltpu.make_async_copy(p_in_hbm, p_in, p_sems.at[0]),
        "g": pltpu.make_async_copy(p_out_hbm, p_out, p_sems.at[1]),
    }
    source, buffer, proj = {"a": a_hbm, "g": g_hbm}, {"a": a_buf, "g": g_buf}, {"a": p_in, "g": p_out}
    steps, seen = [], set()
    for i, (name, start, size) in enumerate(plan):
        cols = pl.ds(start, size)
        copy = pltpu.make_async_copy(source[name].at[:, cols], buffer[name].at[:, cols], sems.at[i])
        if name not in seen:
            seen.add(name)
            p_copies[name].start()
        copy.start()
        steps.append((name, slice(start, start + size), copy))
    waited, total = set(), {}
    for name, cols, copy in steps:
        if name not in waited:
            waited.add(name)
            p_copies[name].wait()
        copy.wait()
        part = lax.dot_general(proj[name][:, cols], buffer[name][:, cols], NT, preferred_element_type=F32)
        total[name] = part if name not in total else total[name] + part
    out_ref[0:width, :] = total["a"]
    out_ref[width : 2 * width, :] = total["g"]


def project(activations, out_grads, proj_in, proj_out):
    slots, d = activations.shape
    ff = out_grads.shape[1]
    width = proj_in.shape[1]
    quarter = ff // 4
    plan = tuple(("g", i * quarter, quarter) for i in range(4)) + (("a", 0, d),)
    return pl.pallas_call(
        functools.partial(project_kernel, plan),
        out_shape=jax.ShapeDtypeStruct((2 * width, slots), F32),
        in_specs=[pl.BlockSpec(memory_space=pl.ANY)] * 4,
        out_specs=pl.BlockSpec(memory_space=pltpu.VMEM),
        scratch_shapes=[
            pltpu.VMEM((slots, d), BF16),
            pltpu.VMEM((slots, ff), BF16),
            pltpu.VMEM((width, d), BF16),
            pltpu.VMEM((width, ff), BF16),
            pltpu.SemaphoreType.DMA((len(plan),)),
            pltpu.SemaphoreType.DMA((2,)),
        ],
        compiler_params=pltpu.CompilerParams(vmem_limit_bytes=60 * MIB),
        name="project",
    )(activations, out_grads, proj_in.T, proj_out.T)


def fisher_kernel(lengths_ref, own_ref, other_ref, out_ref):
    width = out_ref.shape[0]
    both = own_ref[...] + other_ref[...]
    live_slots = lax.fori_loop(0, lengths_ref.shape[1] - 1, lambda e, n: n + lengths_ref[0, e], jnp.int32(0))
    slot = lax.broadcasted_iota(jnp.int32, both.shape, 1)
    live = jnp.where(slot < live_slots, both, 0.0)
    gram = lax.dot_general(live, both, NT, precision=HIGHEST, preferred_element_type=F32)
    out_ref[...] = jnp.zeros_like(out_ref)
    out_ref[:, 0:width] = gram[0:width, 0:width]
    out_ref[:, width : 2 * width] = gram[width : 2 * width, width : 2 * width]


def fisher(lengths, own, other):
    width = own.shape[0] // 2
    return pl.pallas_call(
        fisher_kernel,
        out_shape=jax.ShapeDtypeStruct((width, 128), F32),
        in_specs=[pl.BlockSpec(memory_space=pltpu.SMEM)] + [pl.BlockSpec(memory_space=pltpu.VMEM)] * 2,
        out_specs=pl.BlockSpec(memory_space=pltpu.VMEM),
        name="fisher",
    )(lengths, own, other)


def split3(value):
    high = value.astype(BF16)
    rest = value - high.astype(F32)
    middle = rest.astype(BF16)
    return high, middle, (rest - middle.astype(F32)).astype(BF16)


def examples_kernel(lengths_ref, own_ref, other_ref, out_ref):
    examples = out_ref.shape[0]
    width = own_ref.shape[0] // 2
    slots = own_ref.shape[1]
    both = own_ref[...] + other_ref[...]
    inputs, outputs = both[0:width], both[width : 2 * width]
    index = lax.broadcasted_iota(jnp.int32, (examples, 1), 0)
    starts = jnp.zeros((examples, 1), jnp.int32)
    counts = jnp.zeros((examples, 1), jnp.int32)
    begin = jnp.int32(0)
    for e in range(examples):
        length = lengths_ref[0, e]
        starts = jnp.where(index == e, begin, starts)
        counts = jnp.where(index == e, length, counts)
        begin = begin + length
    slot = lax.broadcasted_iota(jnp.int32, (examples, slots), 1)
    member = jnp.where((slot >= starts) & (slot < starts + counts), 1.0, 0.0).astype(BF16)
    divisor = counts.astype(F32)
    group = 8
    for first in range(0, width, group):
        outer = jnp.concatenate([outputs[i : i + 1] * inputs for i in range(first, first + group)], axis=0)
        total = None
        for piece in reversed(split3(outer)):
            part = lax.dot_general(member, piece, NT, preferred_element_type=F32)
            total = part if total is None else total + part
        out_ref[:, first * width : (first + group) * width] = total / divisor


def example_grads(lengths, own, other):
    width = own.shape[0] // 2
    return pl.pallas_call(
        examples_kernel,
        out_shape=jax.ShapeDtypeStruct((lengths.shape[1] - 1, width * width), F32),
        in_specs=[pl.BlockSpec(memory_space=pltpu.SMEM)] + [pl.BlockSpec(memory_space=pltpu.VMEM)] * 2,
        out_specs=pl.BlockSpec(memory_space=pltpu.VMEM),
        name="examples",
    )(lengths, own, other)


def arrange_examples_kernel(n_query, blocks_ref, out_ref, rows):
    blocks, examples, columns = blocks_ref.shape
    query = lax.axis_index("query")
    for b in range(blocks):
        place = (b // n_query) * n_query + (query ^ (b % n_query))
        rows[pl.ds(pl.multiple_of(place * examples, 8), examples), :] = blocks_ref[b]
    for c in range(0, columns, 128):
        out_ref[c : c + 128, :] = rows[:, c : c + 128].T


def arrange_examples(blocks, n_query):
    count, examples, columns = blocks.shape
    return pl.pallas_call(
        functools.partial(arrange_examples_kernel, n_query),
        out_shape=jax.ShapeDtypeStruct((columns, count * examples), F32),
        in_specs=[pl.BlockSpec(memory_space=pltpu.VMEM)],
        out_specs=pl.BlockSpec(memory_space=pltpu.VMEM),
        scratch_shapes=[pltpu.VMEM((count * examples, columns), F32)],
        name="arrange_examples",
    )(blocks)


def split_queries_kernel(low_dp, own_ref, *refs):
    same_refs, other_refs, (high_ref, low_ref) = refs[: low_dp - 1], refs[low_dp - 1 : -2], refs[-2:]
    rows = own_ref.shape[1]
    half = rows // 2
    place = lax.axis_index("dp") % low_dp
    core = lax.axis_index("proj")

    def put(start, value):
        at = pl.ds(pl.multiple_of(start, 16), value.shape[0])
        high = value.astype(BF16)
        high_ref[at, :] = high
        low_ref[at, :] = (value - high.astype(F32)).astype(BF16)

    put(place * rows, own_ref[0])
    for r in range(1, low_dp):
        put((place ^ r) * rows + core * half, same_refs[r - 1][...])
        put((place ^ r) * rows + (1 - core) * half, other_refs[r - 1][...])


def split_queries(low_dp, own, same, other):
    rows, columns = own.shape[1:]
    shape = jax.ShapeDtypeStruct((low_dp * rows, columns), BF16)
    return pl.pallas_call(
        functools.partial(split_queries_kernel, low_dp),
        out_shape=(shape, shape),
        in_specs=[pl.BlockSpec(memory_space=pltpu.VMEM)] * (1 + len(same) + len(other)),
        out_specs=(pl.BlockSpec(memory_space=pltpu.VMEM),) * 2,
        name="split_queries",
    )(own, *same, *other)


def inverse_tiled(fisher_sum):
    width = fisher_sum.shape[0]
    row = lax.broadcasted_iota(jnp.int32, (width, width), 0)
    column = lax.broadcasted_iota(jnp.int32, (width, width), 1)
    trace = jnp.sum(jnp.where(row == column, fisher_sum, 0.0), keepdims=True)
    damped = fisher_sum * (width / trace) + jnp.where(row == column, 1.0, 0.0)
    state = jnp.concatenate([damped] * (128 // width), axis=1)
    lane = lax.broadcasted_iota(jnp.int32, state.shape, 1) % width
    sublane = lax.broadcasted_iota(jnp.int32, state.shape, 0)
    for k in range(width):
        scale = 1.0 / state[k : k + 1, k : k + 1]
        pivot_row = jnp.where(lane[0:1] == k, 1.0, state[k : k + 1, :]) * scale
        pivot_column = jnp.where(sublane == k, 0.0, jnp.broadcast_to(state[:, k : k + 1], state.shape))
        cleared = jnp.where(lane == k, 0.0, state)
        state = jnp.where(sublane == k, pivot_row, cleared - pivot_column * pivot_row)
    return state


def block_diagonal(tiled):
    width, lanes = tiled.shape
    size = 256
    value = jnp.concatenate([jnp.concatenate([tiled] * (size // lanes), axis=1)] * (size // width), axis=0)
    row = lax.broadcasted_iota(jnp.int32, (size, size), 0) // width
    column = lax.broadcasted_iota(jnp.int32, (size, size), 1) // width
    return jnp.where(row == column, value, 0.0)


def score_kernel(own_ref, other_ref, examples_ref, high_ref, low_ref, mine_ref, theirs_ref, turn, back):
    width = own_ref.shape[0]
    total = own_ref[...] + other_ref[...]
    in_blocks = block_diagonal(inverse_tiled(total[:, 0:width]))
    out_blocks = block_diagonal(inverse_tiled(total[:, width : 2 * width]))
    size = in_blocks.shape[0]
    rows, count = examples_ref.shape
    for c in range(0, rows, size):
        turn[c : c + size, :] = jnp.dot(in_blocks, examples_ref[c : c + size, :], precision=HIGHEST, preferred_element_type=F32)
    for c in range(0, rows, size):
        block = jnp.concatenate(
            [turn[pl.ds(j, width, stride=width), :] for j in range(c // width, (c + size) // width)], axis=0
        )
        back[c : c + size, :] = jnp.dot(out_blocks, block, precision=HIGHEST, preferred_element_type=F32)
    conditioned = jnp.concatenate([back[pl.ds(i, width, stride=width), :] for i in range(width)], axis=0)
    high = conditioned.astype(BF16)
    low = (conditioned - high.astype(F32)).astype(BF16)
    scores = (
        jnp.dot(low_ref[...], high, preferred_element_type=F32)
        + jnp.dot(high_ref[...], low, preferred_element_type=F32)
        + jnp.dot(high_ref[...], high, preferred_element_type=F32)
    )
    scores = (scores * (1.0 / width)).T
    mine_ref[...] = scores[0 : count // 2]
    theirs_ref[...] = scores[count // 2 : count]


def score(own, other, examples, high, low):
    rows, count = examples.shape
    shape = jax.ShapeDtypeStruct((count // 2, high.shape[0]), F32)
    return pl.pallas_call(
        score_kernel,
        out_shape=(shape, shape),
        in_specs=[pl.BlockSpec(memory_space=pltpu.VMEM)] * 5,
        out_specs=(pl.BlockSpec(memory_space=pltpu.VMEM),) * 2,
        scratch_shapes=[pltpu.VMEM((rows, count), F32)] * 2,
        compiler_params=pltpu.CompilerParams(vmem_limit_bytes=40 * MIB),
        name="score",
    )(own, other, examples, high, low)


def body(mesh, activations, out_grads, proj_in, proj_out, lengths, queries):
    n_dp, n_query = mesh.shape["dp"], mesh.shape["query"]
    core_bit = 1
    query_bits = [2 * b for b in bits_of(n_query)]
    dp_bits = [2 * n_query * b for b in bits_of(n_dp)]
    low_bits, top_bit = dp_bits[:-1], dp_bits[-1]
    low_dp = n_dp // 2

    own = project(activations, out_grads, proj_in, proj_out)
    other = swap(own, mesh, core_bit)

    half = queries.shape[1] // 2
    mine = lax.dynamic_slice_in_dim(queries[0], lax.axis_index("proj") * half, half, 0)
    halves = [mine]
    for bit in low_bits:
        halves = halves + [swap(h, mesh, bit) for h in halves]
    same = halves[1:]
    other_half = [swap(h, mesh, core_bit) for h in same]

    factor = fisher(lengths, own, other)
    blocks = example_grads(lengths, own, other)[None]
    bits = query_bits + dp_bits
    for bit in bits[:-1]:
        factor = factor + swap(factor, mesh, bit | core_bit)
    factor_other = swap(factor, mesh, bits[-1] | core_bit)
    for bit in query_bits + [top_bit]:
        blocks = jnp.concatenate([blocks, swap(blocks, mesh, bit | core_bit)], axis=0)

    examples = arrange_examples(blocks, n_query)
    high, low = split_queries(low_dp, queries, same, other_half)
    kept, sent = score(factor, factor_other, examples, high, low)
    received = swap(sent, mesh, top_bit | core_bit)
    upper = lax.axis_index("dp") >= low_dp
    return jnp.concatenate([jnp.where(upper, received, kept), jnp.where(upper, kept, received)], axis=1)


def solution(mesh):
    in_specs = (
        P(("grp", "dp", "query"), "proj"),
        P(("grp", "dp", "query"), "proj"),
        P("proj", None),
        P("proj", None),
        P(("grp", "dp", "query"), None),
        P("query", "dp", None),
    )
    out_specs = P(("grp", "dp"), "query")
    return jax.shard_map(
        functools.partial(body, mesh), mesh=mesh, in_specs=in_specs, out_specs=out_specs, check_vma=False
    )
```

time: 151 us -> 55.2 us (0.37)
  waiting for transfers between devices: 57.6 us -> 11.8 us
  blocking collectives: 42.3 us -> 0 us
  Pallas kernels: 0 us -> 21.9 us
  matrix products: 18.6 us -> 0 us
  between operations: 14.9 us -> 0.05 us
  starting transfers between devices: 0.04 us -> 11.7 us
  other arithmetic: 15.3 us -> 3.78 us
  local copies, waits for them, and re-layouts: 1.94 us -> 5.47 us
    psum x1 -> x0, blocking collectives: 37.3 us -> none  [body(): lax.psum((local_in, local_out), ('dp', 'query'))]
    all_gather x1 -> x0, waiting for transfers between devices: 37.3 us -> none  [body(): lax.all_gather(conditioned[None], 'dp', axis=1, tiled=True)[0]]
    pallas_call x0 -> x6, Pallas kernels: none -> 21.9 us  [the longest x1 6.55 us: score(): pl.pallas_call(score_kernel, out_shape=(shape, shape), in_specs=[pl.Block...]
    psum x1 -> x0, waiting for transfers between devices: 20.3 us -> none  [body(): input_proj, output_proj = lax.psum((input_part, output_part), 'proj')]
    dot_general x8 -> x0, matrix products: 17.8 us -> none  [the longest x1 6.06 us: body(): jnp.dot(out_grads, proj_out, preferred_element_type=jnp.float32)]
    another operation x11 -> x0, other arithmetic: 13.6 us -> none  [the longest x6 7.19 us: inverse(): factor = jnp.linalg.cholesky(scaled)]
    ppermute x0 -> x9, waiting for transfers between devices: none -> 11.8 us  [swap(): return lax.ppermute(value, AXES, [(i, i ^ mask) for i in range(count)])]
    ppermute x0 -> x9, starting transfers between devices: none -> 11.7 us  [swap(): return lax.ppermute(value, AXES, [(i, i ^ mask) for i in range(count)])]
  transfers between devices with their start and end apart: 2 -> 9, of which waited for: 2 -> 5; matrix products, arithmetic and copies ran while one was open for 1% -> 6% of each run, Pallas kernels for 0% -> 28%
where the time goes in v1:
time: 55.2 us; the launch traced here: 54.7 us
  Pallas kernels  21.9 us (40%)
  waiting for transfers between devices  11.8 us (21%)
  starting transfers between devices  11.7 us (21%)
  local copies, waits for them, and re-layouts  5.47 us (10%)
  other arithmetic  3.78 us (7%)
    ppermute x9, waiting for transfers between devices, swap(): return lax.ppermute(value, AXES, [(i, i ^ mask) for i in range(count)])  11.8 us
    ppermute x9, starting transfers between devices, swap(): return lax.ppermute(value, AXES, [(i, i ^ mask) for i in range(count)])  11.7 us
    pallas_call x1, Pallas kernels, score(): pl.pallas_call(score_kernel, out_shape=(shape, shape), in_specs=[pl.Block...  6.55 us
    pallas_call x1, Pallas kernels, project(): pl.pallas_call(functools.partial(project_kernel, plan), out_shape=jax.Sha...  6.53 us
    unnamed x12, local copies, waits for them, and re-layouts  4.5 us
    pallas_call x1, Pallas kernels, example_grads(): pl.pallas_call(examples_kernel, out_shape=jax.ShapeDtypeStruct((lengths.s...  2.6 us
    concatenate x2, other arithmetic, body(): jnp.concatenate([blocks, swap(blocks, mesh, bit | core_bit)], axis=0)  2.41 us
    pallas_call x1, Pallas kernels, split_queries(): pl.pallas_call(functools.partial(split_queries_kernel, low_dp), out_shape...  2.34 us
  transfers between devices with their start and end apart: 9, of which 5 were waited for; matrix products, arithmetic and copies ran while one was open for 6% of the time, Pallas kernels for 28%

profile of v1, /device:TPU:0, one launch (start us, length us, event | category | flops | bytes accessed | tf_op | source)
XLA Modules:
  0.0 54.7 jit_solution(5354094336911201551)
XLA Ops:
  0.0 1.0 %dynamic-slice_bitcast_fusion = f32[64,1024]{1,0:T(8,128)S(1)} fusion(f32[1,128,1024]{2,1,0:T(8,128)} %own_ref.1, s32[]{:T(128)S(6)} %select_n.16), kind=kLoop, calls=%fused_computation.1 | loop fusion | bytes 524292 | tf_op jit(solution)/shard_map/dynamic_slice | solution.py:281
  1.0 3.1 %collective-permute-start.6 = (f32[64,1024]{1,0:T(8,128)S(1)}, f32[64,1024]{1,0:T(8,128)S(1)}, u32[]{:S(2)}, u32[]{:S(2)}) collective-permute-start(f32[64,1024]{1,0:T(8,128)S(1)} %dynamic-slice_bitcast_fusion), channel_id=1, source_target_pairs={{0,4},{1,5},{2,6},{3,7},{4,0},{5,1},{6,2},{7,3},{8,12},{9,13},{10,... | collective-permute-start | bytes 786440 | tf_op jit(solution)/shard_map/ppermute | solution.py:20
  4.1 6.5 %project.1.own_ref = f32[64,512]{1,0:T(8,128)} custom-call(bf16[512,2048]{1,0:T(8,128)(2,1)} %a_hbm.1, bf16[512,7168]{1,0:T(8,128)(2,1)} %g_hbm.1, bf16[32,2048]{1,0:T(8,128)(2,1)} %bitcast.9, bf16[32,7168]{1,0:T(8,128)(2,1)} %bitcast.8), custom_call_target="tpu_custom_call" | custom-call | tf_op jit(solution)/shard_map/project/pallas_call | solution.py:61
  10.7 1.5 %collective-permute-done.other_ref = f32[64,512]{1,0:T(8,128)S(1)} collective-permute-done((f32[64,512]{1,0:T(8,128)}, f32[64,512]{1,0:T(8,128)S(1)}, u32[]{:S(2)}, u32[]{:S(2)}) %collective-permute-start) | collective-permute-done | bytes 131104 | tf_op jit(solution)/shard_map/ppermute | solution.py:20
  12.9 2.6 %examples.1 = f32[16,1024]{1,0:T(8,128)} custom-call(s32[1,17]{1,0:T(1,128)} %lengths_ref.3, f32[64,512]{1,0:T(8,128)} %project.1.own_ref, f32[64,512]{1,0:T(8,128)} %copy-done.3), custom_call_target="tpu_custom_call" | custom-call | tf_op jit(solution)/shard_map/examples/pallas_call | solution.py:139
  15.5 1.2 %collective-permute-start.4 = (f32[1,16,1024]{2,1,0:T(8,128)}, f32[1,16,1024]{2,1,0:T(8,128)S(1)}, u32[]{:S(2)}, u32[]{:S(2)}) collective-permute-start(f32[1,16,1024]{2,1,0:T(8,128)} %bitcast.5), channel_id=1, source_target_pairs={{0,3},{1,2},{2,1},{3,0},{4,7},{5,6},{6,5},{7,4},{8,11},{9,10},{10,... | collective-permute-start | bytes 196616 | tf_op jit(solution)/shard_map/ppermute | solution.py:20
  17.1 2.7 %collective-permute-done.4 = f32[1,16,1024]{2,1,0:T(8,128)S(1)} collective-permute-done((f32[1,16,1024]{2,1,0:T(8,128)}, f32[1,16,1024]{2,1,0:T(8,128)S(1)}, u32[]{:S(2)}, u32[]{:S(2)}) %collective-permute-start.4) | collective-permute-done | bytes 65568 | tf_op jit(solution)/shard_map/ppermute | solution.py:20
  19.7 0.8 %pad_maximum_fusion.1 = f32[2,16,1024]{2,1,0:T(8,128)S(1)} fusion(f32[1,16,1024]{2,1,0:T(8,128)S(1)} %collective-permute-done.4, f32[1,16,1024]{2,1,0:T(8,128)} %bitcast.6), kind=kLoop, calls=%fused_computation.2 | loop fusion | flops 32768 | bytes 262144 | tf_op jit(solution)/shard_map/concatenate | solution.py:295
  20.6 2.4 %collective-permute-start.5 = (f32[2,16,1024]{2,1,0:T(8,128)S(1)}, f32[2,16,1024]{2,1,0:T(8,128)S(1)}, u32[]{:S(2)}, u32[]{:S(2)}) collective-permute-start(f32[2,16,1024]{2,1,0:T(8,128)S(1)} %pad_maximum_fusion.1), channel_id=1, source_target_pairs={{0,9},{1,8},{2,11},{3,10},{4,13},{5,12},{6,15},{7,14},{8,1},{9,0},... | collective-permute-start | bytes 393224 | tf_op jit(solution)/shard_map/ppermute | solution.py:20
  23.0 1.9 %fisher.1 = f32[32,128]{1,0:T(8,128)} custom-call(s32[1,17]{1,0:T(1,128)} %lengths_ref.3, f32[64,512]{1,0:T(8,128)} %project.1.own_ref, f32[64,512]{1,0:T(8,128)} %copy-done.3), custom_call_target="tpu_custom_call" | custom-call | tf_op jit(solution)/shard_map/fisher/pallas_call | solution.py:93
  24.9 1.5 %collective-permute-start.1 = (f32[32,128]{1,0:T(8,128)}, f32[32,128]{1,0:T(8,128)S(1)}, u32[]{:S(2)}, u32[]{:S(2)}) collective-permute-start(f32[32,128]{1,0:T(8,128)} %fisher.1), channel_id=1, source_target_pairs={{0,3},{1,2},{2,1},{3,0},{4,7},{5,6},{6,5},{7,4},{8,11},{9,10},{10,... | collective-permute-start | bytes 49160 | tf_op jit(solution)/shard_map/ppermute | solution.py:20
  26.4 1.9 %collective-permute-done.1 = f32[32,128]{1,0:T(8,128)S(1)} collective-permute-done((f32[32,128]{1,0:T(8,128)}, f32[32,128]{1,0:T(8,128)S(1)}, u32[]{:S(2)}, u32[]{:S(2)}) %collective-permute-start.1) | collective-permute-done | bytes 16416 | tf_op jit(solution)/shard_map/ppermute | solution.py:20
  28.3 0.7 %add.9 = f32[32,128]{1,0:T(8,128)S(1)} add(f32[32,128]{1,0:T(8,128)} %fisher.1, f32[32,128]{1,0:T(8,128)S(1)} %collective-permute-done.1) | non-fusion elementwise | flops 4096 | bytes 49152 | tf_op jit(solution)/shard_map/add | solution.py:292
  29.5 2.8 %collective-permute-done.2 = f32[32,128]{1,0:T(8,128)S(1)} collective-permute-done((f32[32,128]{1,0:T(8,128)S(1)}, f32[32,128]{1,0:T(8,128)S(1)}, u32[]{:S(2)}, u32[]{:S(2)}) %collective-permute-start.2) | collective-permute-done | bytes 16416 | tf_op jit(solution)/shard_map/ppermute | solution.py:20
  32.8 1.6 %pad_maximum_fusion.blocks_ref = f32[4,16,1024]{2,1,0:T(8,128)} fusion(f32[2,16,1024]{2,1,0:T(8,128)S(1)} %collective-permute-done.5, f32[1,16,1024]{2,1,0:T(8,128)S(1)} %collective-permute-done.4, f32[1,16,1024]{2,1,0:T(8,128)} %bitcast.7), kind=kLoop, calls=%fused_computation | loop fusion | flops 131072 | bytes 524288 | tf_op jit(solution)/shard_map/concatenate | solution.py:295
  34.4 2.0 %arrange_examples.1.examples_ref = f32[1024,64]{1,0:T(8,128)} custom-call(f32[4,16,1024]{2,1,0:T(8,128)} %pad_maximum_fusion.blocks_ref), custom_call_target="tpu_custom_call" | custom-call | tf_op jit(solution)/shard_map/arrange_examples/pallas_call | solution.py:160
  36.4 0.7 %copy-done.5 = f32[64,1024]{1,0:T(8,128)} copy-done((f32[64,1024]{1,0:T(8,128)}, f32[64,1024]{1,0:T(8,128)S(1)}, u32[]{:S(2)}) %copy-start.5) | copy-done | bytes 262168
  37.1 2.3 %split_queries.1 = (bf16[256,1024]{1,0:T(8,128)(2,1)}, bf16[256,1024]{1,0:T(8,128)(2,1)}) custom-call(f32[1,128,1024]{2,1,0:T(8,128)} %own_ref.1, f32[64,1024]{1,0:T(8,128)} %copy-done.4, f32[64,1024]{1,0:T(8,128)} %copy-done.5), custom_call_target="tpu_custom_call" | custom-call | tf_op jit(solution)/shard_map/split_queries/pallas_call | solution.py:192
  39.4 1.0 %copy-done = f32[1024,64]{1,0:T(8,128)S(1)} copy-done((f32[1024,64]{1,0:T(8,128)S(1)}, f32[1024,64]{1,0:T(8,128)}, u32[]{:S(2)}) %copy-start) | copy-done | bytes 262168
  40.5 1.0 %copy-done.1 = bf16[256,1024]{1,0:T(8,128)(2,1)S(1)} copy-done((bf16[256,1024]{1,0:T(8,128)(2,1)S(1)}, bf16[256,1024]{1,0:T(8,128)(2,1)}, u32[]{:S(2)}) %copy-start.1) | copy-done | bytes 524312
  41.5 1.0 %copy-done.2 = bf16[256,1024]{1,0:T(8,128)(2,1)S(1)} copy-done((bf16[256,1024]{1,0:T(8,128)(2,1)S(1)}, bf16[256,1024]{1,0:T(8,128)(2,1)}, u32[]{:S(2)}) %copy-start.2) | copy-done | bytes 524312
  42.6 6.5 %score.1 = (f32[32,256]{1,0:T(8,128)S(1)}, f32[32,256]{1,0:T(8,128)S(1)}) custom-call(f32[32,128]{1,0:T(8,128)S(1)} %add.10.own_ref, f32[32,128]{1,0:T(8,128)S(1)} %collective-permute-done.3.other_ref, f32[1024,64]{1,0:T(8,128)S(1)} %copy-done, bf16[256,1024]{1,0:T(8,128)(2,1)S(1)} %copy-done.1, bf16[256,1024]{1,0:T(8,128)(2,1)S(1)} %copy-done.2), custom_call_target="tpu_custom_call" | custom-call | tf_op jit(solution)/shard_map/score/pallas_call | solution.py:258
  49.1 2.1 %collective-permute-start.8 = (f32[32,256]{1,0:T(8,128)S(1)}, f32[32,256]{1,0:T(8,128)S(1)}, u32[]{:S(2)}, u32[]{:S(2)}) collective-permute-start(f32[32,256]{1,0:T(8,128)S(1)} %get-tuple-element.11), channel_id=1, source_target_pairs={{0,9},{1,8},{2,11},{3,10},{4,13},{5,12},{6,15},{7,14},{8,1},{9,0},... | collective-permute-start | bytes 98312 | tf_op jit(solution)/shard_map/ppermute | solution.py:20
  51.2 2.9 %collective-permute-done.8 = f32[32,256]{1,0:T(8,128)S(1)} collective-permute-done((f32[32,256]{1,0:T(8,128)S(1)}, f32[32,256]{1,0:T(8,128)S(1)}, u32[]{:S(2)}, u32[]{:S(2)}) %collective-permute-start.8) | collective-permute-done | bytes 32800 | tf_op jit(solution)/shard_map/ppermute | solution.py:20
  (19 shorter events, 2.7 us)
Async XLA Ops:
  1.0 15.7 %collective-permute-start.6 = (f32[64,1024]{1,0:T(8,128)S(1)}, f32[64,1024]{1,0:T(8,128)S(1)}, u32[]{:S(2)}, u32[]{:S(2)}) collective-permute-start(f32[64,1024]{1,0:T(8,128)S(1)} %dynamic-slice_bitcast_fusion), channel_id=1, source_target_pairs={{0,4},{1,5},{2,6},{3,7},{4,0},{5,1},{6,2},{7,3},{8,12},{9,13},{10,... | collective-permute-start | bytes 786440 | tf_op jit(solution)/shard_map/ppermute | solution.py:20
  10.6 1.6 %collective-permute-start = (f32[64,512]{1,0:T(8,128)}, f32[64,512]{1,0:T(8,128)S(1)}, u32[]{:S(2)}, u32[]{:S(2)}) collective-permute-start(f32[64,512]{1,0:T(8,128)} %project.1.own_ref), channel_id=1, source_target_pairs={{0,1},{1,0},{2,3},{3,2},{4,5},{5,4},{6,7},{7,6},{8,9},{9,8},{10,11... | collective-permute-start | bytes 393224 | tf_op jit(solution)/shard_map/ppermute | solution.py:20
  12.2 0.6 %copy-start.3 = (f32[64,512]{1,0:T(8,128)}, f32[64,512]{1,0:T(8,128)S(1)}, u32[]{:S(2)}) copy-start(f32[64,512]{1,0:T(8,128)S(1)} %collective-permute-done.other_ref) | copy-start | bytes 393220
  15.5 4.3 %collective-permute-start.4 = (f32[1,16,1024]{2,1,0:T(8,128)}, f32[1,16,1024]{2,1,0:T(8,128)S(1)}, u32[]{:S(2)}, u32[]{:S(2)}) collective-permute-start(f32[1,16,1024]{2,1,0:T(8,128)} %bitcast.5), channel_id=1, source_target_pairs={{0,3},{1,2},{2,1},{3,0},{4,7},{5,6},{6,5},{7,4},{8,11},{9,10},{10,... | collective-permute-start | bytes 196616 | tf_op jit(solution)/shard_map/ppermute | solution.py:20
  16.7 19.6 %copy-start.4 = (f32[64,1024]{1,0:T(8,128)}, f32[64,1024]{1,0:T(8,128)S(1)}, u32[]{:S(2)}) copy-start(f32[64,1024]{1,0:T(8,128)S(1)} %collective-permute-done.6.refs_0_) | copy-start | bytes 786436
  16.7 19.6 %collective-permute-start.7 = (f32[64,1024]{1,0:T(8,128)S(1)}, f32[64,1024]{1,0:T(8,128)S(1)}, u32[]{:S(2)}, u32[]{:S(2)}) collective-permute-start(f32[64,1024]{1,0:T(8,128)S(1)} %collective-permute-done.6.refs_0_), channel_id=1, source_target_pairs={{0,1},{1,0},{2,3},{3,2},{4,5},{5,4},{6,7},{7,6},{8,9},{9,8},{10,11... | collective-permute-start | bytes 786440 | tf_op jit(solution)/shard_map/ppermute | solution.py:20
  20.6 12.2 %collective-permute-start.5 = (f32[2,16,1024]{2,1,0:T(8,128)S(1)}, f32[2,16,1024]{2,1,0:T(8,128)S(1)}, u32[]{:S(2)}, u32[]{:S(2)}) collective-permute-start(f32[2,16,1024]{2,1,0:T(8,128)S(1)} %pad_maximum_fusion.1), channel_id=1, source_target_pairs={{0,9},{1,8},{2,11},{3,10},{4,13},{5,12},{6,15},{7,14},{8,1},{9,0},... | collective-permute-start | bytes 393224 | tf_op jit(solution)/shard_map/ppermute | solution.py:20
  24.9 3.4 %collective-permute-start.1 = (f32[32,128]{1,0:T(8,128)}, f32[32,128]{1,0:T(8,128)S(1)}, u32[]{:S(2)}, u32[]{:S(2)}) collective-permute-start(f32[32,128]{1,0:T(8,128)} %fisher.1), channel_id=1, source_target_pairs={{0,3},{1,2},{2,1},{3,0},{4,7},{5,6},{6,5},{7,4},{8,11},{9,10},{10,... | collective-permute-start | bytes 49160 | tf_op jit(solution)/shard_map/ppermute | solution.py:20
  29.1 3.2 %collective-permute-start.2 = (f32[32,128]{1,0:T(8,128)S(1)}, f32[32,128]{1,0:T(8,128)S(1)}, u32[]{:S(2)}, u32[]{:S(2)}) collective-permute-start(f32[32,128]{1,0:T(8,128)S(1)} %add.9), channel_id=1, source_target_pairs={{0,5},{1,4},{2,7},{3,6},{4,1},{5,0},{6,3},{7,2},{8,13},{9,12},{10,... | collective-permute-start | bytes 49160 | tf_op jit(solution)/shard_map/ppermute | solution.py:20
  32.2 7.2 %collective-permute-start.3 = (f32[32,128]{1,0:T(8,128)S(1)}, f32[32,128]{1,0:T(8,128)S(1)}, u32[]{:S(2)}, u32[]{:S(2)}) collective-permute-start(f32[32,128]{1,0:T(8,128)S(1)} %add.10.own_ref), channel_id=1, source_target_pairs={{0,9},{1,8},{2,11},{3,10},{4,13},{5,12},{6,15},{7,14},{8,1},{9,0},... | collective-permute-start | bytes 49160 | tf_op jit(solution)/shard_map/ppermute | solution.py:20
  36.4 0.7 %copy-start.5 = (f32[64,1024]{1,0:T(8,128)}, f32[64,1024]{1,0:T(8,128)S(1)}, u32[]{:S(2)}) copy-start(f32[64,1024]{1,0:T(8,128)S(1)} %collective-permute-done.7.refs_1_) | copy-start | bytes 786436
  39.4 1.0 %copy-start = (f32[1024,64]{1,0:T(8,128)S(1)}, f32[1024,64]{1,0:T(8,128)}, u32[]{:S(2)}) copy-start(f32[1024,64]{1,0:T(8,128)} %arrange_examples.1.examples_ref) | copy-start | bytes 786436
  40.5 1.0 %copy-start.1 = (bf16[256,1024]{1,0:T(8,128)(2,1)S(1)}, bf16[256,1024]{1,0:T(8,128)(2,1)}, u32[]{:S(2)}) copy-start(bf16[256,1024]{1,0:T(8,128)(2,1)} %get-tuple-element.9.high_ref) | copy-start | bytes 1572868
  41.5 1.0 %copy-start.2 = (bf16[256,1024]{1,0:T(8,128)(2,1)S(1)}, bf16[256,1024]{1,0:T(8,128)(2,1)}, u32[]{:S(2)}) copy-start(bf16[256,1024]{1,0:T(8,128)(2,1)} %get-tuple-element.10.low_ref) | copy-start | bytes 1572868
  49.1 5.0 %collective-permute-start.8 = (f32[32,256]{1,0:T(8,128)S(1)}, f32[32,256]{1,0:T(8,128)S(1)}, u32[]{:S(2)}, u32[]{:S(2)}) collective-permute-start(f32[32,256]{1,0:T(8,128)S(1)} %get-tuple-element.11), channel_id=1, source_target_pairs={{0,9},{1,8},{2,11},{3,10},{4,13},{5,12},{6,15},{7,14},{8,1},{9,0},... | collective-permute-start | bytes 98312 | tf_op jit(solution)/shard_map/ppermute | solution.py:20

commit v2 on v1

v2 whole, which is shorter than its diff:
```python
import functools
import math

import jax
import jax.numpy as jnp
from jax import lax
from jax.experimental import pallas as pl
from jax.experimental.pallas import tpu as pltpu
from jax.sharding import PartitionSpec as P

F32 = jnp.float32
BF16 = jnp.bfloat16
HIGHEST = lax.Precision.HIGHEST
NT = (((1,), (1,)), ((), ()))
AXES = ("dp", "query", "proj")
MIB = 2**20
CHUNK = 256
QUERY_STEP = 1


def swap(value, mesh, mask):
    count = math.prod(mesh.shape[axis] for axis in AXES)
    return lax.ppermute(value, AXES, [(i, i ^ mask) for i in range(count)])


def bits_of(size):
    return [1 << b for b in range(size.bit_length() - 1)]


def pick_kernel(queries_hbm, half_ref, sem):
    half = half_ref.shape[0]
    start = pl.multiple_of(lax.axis_index("proj") * half, 8)
    copy = pltpu.make_async_copy(queries_hbm.at[0, pl.ds(start, half)], half_ref, sem)
    copy.start()
    copy.wait()


def pick_queries(queries):
    rows, columns = queries.shape[1:]
    return pl.pallas_call(
        pick_kernel,
        out_shape=jax.ShapeDtypeStruct((rows // 2, columns), F32),
        in_specs=[pl.BlockSpec(memory_space=pl.ANY)],
        out_specs=pl.BlockSpec(memory_space=pltpu.VMEM),
        scratch_shapes=[pltpu.SemaphoreType.DMA],
        compiler_params=pltpu.CompilerParams(vmem_limit_bytes=4 * MIB),
        cost_estimate=pl.CostEstimate(flops=4 * 10**9, bytes_accessed=10**6, transcendentals=0),
        name="pick_queries",
    )(pltpu.with_memory_space_constraint(queries, pltpu.HBM))


def project_kernel(a_ref, g_ref, p_in_ref, p_out_ref, after_ref, out_ref):
    width = p_in_ref.shape[0]
    out_ref[0:width, :] = lax.dot_general(p_in_ref[...], a_ref[...], NT, preferred_element_type=F32)
    out_ref[width : 2 * width, :] = lax.dot_general(p_out_ref[...], g_ref[...], NT, preferred_element_type=F32)


def project(activations, out_grads, proj_in, proj_out, after):
    return pl.pallas_call(
        project_kernel,
        out_shape=jax.ShapeDtypeStruct((2 * proj_in.shape[1], activations.shape[0]), F32),
        in_specs=[pl.BlockSpec(memory_space=pltpu.VMEM)] * 4 + [pl.BlockSpec(memory_space=pl.ANY)],
        out_specs=pl.BlockSpec(memory_space=pltpu.VMEM),
        compiler_params=pltpu.CompilerParams(vmem_limit_bytes=16 * MIB),
        name="project",
    )(activations, out_grads, proj_in.T, proj_out.T, after)


def fisher_kernel(lengths_ref, own_ref, other_ref, out_ref):
    width = out_ref.shape[0]
    both = own_ref[...] + other_ref[...]
    live_slots = lax.fori_loop(0, lengths_ref.shape[1] - 1, lambda e, n: n + lengths_ref[0, e], jnp.int32(0))
    slot = lax.broadcasted_iota(jnp.int32, both.shape, 1)
    live = jnp.where(slot < live_slots, both, 0.0)
    gram = lax.dot_general(live, both, NT, precision=HIGHEST, preferred_element_type=F32)
    out_ref[...] = jnp.zeros_like(out_ref)
    out_ref[:, 0:width] = gram[0:width, 0:width]
    out_ref[:, width : 2 * width] = gram[width : 2 * width, width : 2 * width]


def fisher(lengths, own, other):
    width = own.shape[0] // 2
    return pl.pallas_call(
        fisher_kernel,
        out_shape=jax.ShapeDtypeStruct((width, 128), F32),
        in_specs=[pl.BlockSpec(memory_space=pltpu.SMEM)] + [pl.BlockSpec(memory_space=pltpu.VMEM)] * 2,
        out_specs=pl.BlockSpec(memory_space=pltpu.VMEM),
        compiler_params=pltpu.CompilerParams(vmem_limit_bytes=8 * MIB),
        name="fisher",
    )(lengths, own, other)


def split3(value):
    high = value.astype(BF16)
    rest = value - high.astype(F32)
    middle = rest.astype(BF16)
    return high, middle, (rest - middle.astype(F32)).astype(BF16)


def examples_kernel(lengths_ref, own_ref, other_ref, out_ref):
    examples = out_ref.shape[0]
    width = own_ref.shape[0] // 2
    slots = own_ref.shape[1]
    both = own_ref[...] + other_ref[...]
    inputs, outputs = both[0:width], both[width : 2 * width]
    index = lax.broadcasted_iota(jnp.int32, (examples, 1), 0)
    starts = jnp.zeros((examples, 1), jnp.int32)
    counts = jnp.zeros((examples, 1), jnp.int32)
    begin = jnp.int32(0)
    for e in range(examples):
        length = lengths_ref[0, e]
        starts = jnp.where(index == e, begin, starts)
        counts = jnp.where(index == e, length, counts)
        begin = begin + length
    slot = lax.broadcasted_iota(jnp.int32, (examples, slots), 1)
    member = jnp.where((slot >= starts) & (slot < starts + counts), 1.0, 0.0).astype(BF16)
    divisor = counts.astype(F32)
    group = 8
    for first in range(0, width, group):
        outer = jnp.concatenate([outputs[i : i + 1] * inputs for i in range(first, first + group)], axis=0)
        total = None
        for piece in reversed(split3(outer)):
            part = lax.dot_general(member, piece, NT, preferred_element_type=F32)
            total = part if total is None else total + part
        out_ref[:, first * width : (first + group) * width] = total / divisor


def example_grads(lengths, own, other):
    width = own.shape[0] // 2
    return pl.pallas_call(
        examples_kernel,
        out_shape=jax.ShapeDtypeStruct((lengths.shape[1] - 1, width * width), F32),
        in_specs=[pl.BlockSpec(memory_space=pltpu.SMEM)] + [pl.BlockSpec(memory_space=pltpu.VMEM)] * 2,
        out_specs=pl.BlockSpec(memory_space=pltpu.VMEM),
        compiler_params=pltpu.CompilerParams(vmem_limit_bytes=8 * MIB),
        cost_estimate=pl.CostEstimate(flops=2 * 10**9, bytes_accessed=10**6, transcendentals=0),
        name="examples",
    )(lengths, own, other)


def split2(value):
    high = value.astype(BF16)
    return high, (value - high.astype(F32)).astype(BF16)


def turn_pairs(load, scratch, width):
    columns, count = scratch.shape
    for c in range(columns // CHUNK):
        scratch[c * CHUNK : (c + 1) * CHUNK, :] = load(c).T
    chunks = []
    for c in range(columns // CHUNK):
        lines = range(c * CHUNK // width, (c + 1) * CHUNK // width)
        chunks.append(jnp.concatenate([scratch[pl.ds(j, width, stride=width), :] for j in lines], axis=0).T)
    return jnp.concatenate(chunks, axis=0)


def arrange_examples_kernel(n_query, blocks_ref, *refs):
    out_refs, (rows, scratch) = refs[:-2], refs[-2:]
    blocks, examples, columns = blocks_ref.shape
    query = lax.axis_index("query")
    for b in range(blocks):
        place = (b // n_query) * n_query + (query ^ (b % n_query))
        rows[pl.ds(pl.multiple_of(place * examples, 8), examples), :] = blocks_ref[b]
    width = math.isqrt(columns)
    turned = turn_pairs(lambda c: rows[:, c * CHUNK : (c + 1) * CHUNK], scratch, width)
    for out_ref, piece in zip(out_refs, split3(turned)):
        out_ref[...] = piece


def arrange_examples(blocks, n_query):
    number, examples, columns = blocks.shape
    count = number * examples
    shape = jax.ShapeDtypeStruct((count * columns // CHUNK, CHUNK), BF16)
    return pl.pallas_call(
        functools.partial(arrange_examples_kernel, n_query),
        out_shape=(shape,) * 3,
        in_specs=[pl.BlockSpec(memory_space=pltpu.VMEM)],
        out_specs=(pl.BlockSpec(memory_space=pltpu.VMEM),) * 3,
        scratch_shapes=[pltpu.VMEM((count, columns), F32), pltpu.VMEM((columns, count), F32)],
        compiler_params=pltpu.CompilerParams(vmem_limit_bytes=12 * MIB),
        name="arrange_examples",
    )(blocks)


def split_queries_kernel(bits, own_ref, *refs):
    parts = 1 << len(bits)
    same_refs, other_refs, (high_ref, low_ref) = refs[: parts - 1], refs[parts - 1 : -2], refs[-2:]
    rows = own_ref.shape[1]
    half = rows // 2
    dp, core = lax.axis_index("dp"), lax.axis_index("proj")
    place = sum(((dp // bit) % 2) << b for b, bit in enumerate(bits))

    def put(start, value):
        at = pl.ds(pl.multiple_of(start, 16), value.shape[0])
        high_ref[at, :], low_ref[at, :] = split2(value)

    put(place * rows, own_ref[0])
    for r in range(1, parts):
        put((place ^ r) * rows + core * half, same_refs[r - 1][...])
        put((place ^ r) * rows + (1 - core) * half, other_refs[r - 1][...])


def split_queries(bits, own, same, other):
    parts = 1 + len(same)
    rows, columns = own.shape[1:]
    shape = jax.ShapeDtypeStruct((parts * rows, columns), BF16)
    return pl.pallas_call(
        functools.partial(split_queries_kernel, bits),
        out_shape=(shape, shape),
        in_specs=[pl.BlockSpec(memory_space=pltpu.VMEM)] * (1 + len(same) + len(other)),
        out_specs=(pl.BlockSpec(memory_space=pltpu.VMEM),) * 2,
        compiler_params=pltpu.CompilerParams(vmem_limit_bytes=(4 + 2 * parts) * MIB),
        name="split_queries",
    )(own, *same, *other)


def inverse_tiled(fisher_sum):
    width = fisher_sum.shape[0]
    row = lax.broadcasted_iota(jnp.int32, (width, width), 0)
    column = lax.broadcasted_iota(jnp.int32, (width, width), 1)
    trace = jnp.sum(jnp.where(row == column, fisher_sum, 0.0), keepdims=True)
    damped = fisher_sum * (width / trace) + jnp.where(row == column, 1.0, 0.0)
    state = jnp.concatenate([damped] * (128 // width), axis=1)
    lane = lax.broadcasted_iota(jnp.int32, state.shape, 1) % width
    sublane = lax.broadcasted_iota(jnp.int32, state.shape, 0)
    top = lane[0:1]

    def apply(m, x, y):
        return m[0][0] * x + m[0][1] * y, m[1][0] * x + m[1][1] * y

    def invert(m):
        scale = 1.0 / (m[0][0] * m[1][1] - m[0][1] * m[1][0])
        return (m[1][1] * scale, -m[0][1] * scale), (-m[1][0] * scale, m[0][0] * scale)

    for k in range(0, width, 4):
        columns = [jnp.broadcast_to(state[:, k + c : k + c + 1], state.shape) for c in range(4)]
        pivot = [[columns[c][k + r : k + r + 1, :] for c in range(4)] for r in range(4)]
        inside = (top >= k) & (top < k + 4)
        rows = [
            jnp.where(top == k + r, 1.0, jnp.where(inside, 0.0, state[k + r : k + r + 1, :])) for r in range(4)
        ]
        corner = invert((pivot[0][0:2], pivot[1][0:2]))
        upper = apply(corner, rows[0], rows[1])
        right = [apply(corner, pivot[0][c], pivot[1][c]) for c in (2, 3)]
        schur = [
            [pivot[r][c] - pivot[r][0] * right[c - 2][0] - pivot[r][1] * right[c - 2][1] for c in (2, 3)] for r in (2, 3)
        ]
        lower = apply(
            invert(schur), *(rows[r] - pivot[r][0] * upper[0] - pivot[r][1] * upper[1] for r in (2, 3))
        )
        solved = [upper[r] - right[0][r] * lower[0] - right[1][r] * lower[1] for r in range(2)] + list(lower)
        change = columns[0] * solved[0] + columns[1] * solved[1] + columns[2] * solved[2] + columns[3] * solved[3]
        state = jnp.where((lane >= k) & (lane < k + 4), 0.0, state) - change
        for r in range(4):
            state = jnp.where(sublane == k + r, solved[r], state)
    return state


def block_diagonal(tiled):
    width, lanes = tiled.shape
    value = jnp.concatenate([jnp.concatenate([tiled] * (CHUNK // lanes), axis=1)] * (CHUNK // width), axis=0)
    row = lax.broadcasted_iota(jnp.int32, (CHUNK, CHUNK), 0) // width
    column = lax.broadcasted_iota(jnp.int32, (CHUNK, CHUNK), 1) // width
    return jnp.where(row == column, value, 0.0)


def inverses_kernel(own_ref, other_ref, in_ref, out_ref):
    width = own_ref.shape[0]
    total = own_ref[...] + other_ref[...]
    for ref, fisher_sum in ((in_ref, total[:, 0:width]), (out_ref, total[:, width : 2 * width])):
        for piece, value in enumerate(split3(block_diagonal(inverse_tiled(fisher_sum)))):
            ref[piece] = value


def inverses(own, other):
    shape = jax.ShapeDtypeStruct((3, CHUNK, CHUNK), BF16)
    return pl.pallas_call(
        inverses_kernel,
        out_shape=(shape, shape),
        in_specs=[pl.BlockSpec(memory_space=pltpu.VMEM)] * 2,
        out_specs=(pl.BlockSpec(memory_space=pltpu.VMEM),) * 2,
        compiler_params=pltpu.CompilerParams(vmem_limit_bytes=8 * MIB),
        name="inverses",
    )(own, other)


def times_blocks(high, middle, low, blocks_ref):
    rows = high.shape[0]
    by_high = jnp.dot(jnp.concatenate([high, middle, low], axis=0), blocks_ref[0], preferred_element_type=F32)
    by_middle = jnp.dot(jnp.concatenate([high, middle], axis=0), blocks_ref[1], preferred_element_type=F32)
    by_low = jnp.dot(high, blocks_ref[2], preferred_element_type=F32)
    small = by_high[2 * rows :] + by_middle[rows:] + by_low
    return by_high[0:rows] + (by_high[rows : 2 * rows] + by_middle[0:rows] + small)


def score_kernel(high_ref, middle_ref, low_ref, in_ref, out_ref, q_high_ref, q_low_ref, mine_ref, theirs_ref, scratch):
    columns, count = scratch.shape
    width = math.isqrt(columns)
    left = times_blocks(high_ref[...], middle_ref[...], low_ref[...], out_ref)
    turned = turn_pairs(lambda c: left[c * count : (c + 1) * count], scratch, width)
    high, low = split2(times_blocks(*split3(turned), in_ref))
    total = None
    for c in range(columns // CHUNK):
        at, cols = slice(c * count, (c + 1) * count), slice(c * CHUNK, (c + 1) * CHUNK)
        both = jnp.concatenate([high[at], low[at]], axis=0)
        by_high = lax.dot_general(both, q_high_ref[:, cols], NT, preferred_element_type=F32)
        by_low = lax.dot_general(high[at], q_low_ref[:, cols], NT, preferred_element_type=F32)
        part = by_high[0:count] + (by_high[count:] + by_low)
        total = part if total is None else total + part
    total = total * (1.0 / width)
    mine_ref[...] = total[0 : count // 2]
    theirs_ref[...] = total[count // 2 :]


def score(pieces, in_blocks, out_blocks, high, low):
    columns = high.shape[1]
    count = pieces[0].shape[0] * CHUNK // columns
    shape = jax.ShapeDtypeStruct((count // 2, high.shape[0]), F32)
    return pl.pallas_call(
        score_kernel,
        out_shape=(shape, shape),
        in_specs=[pl.BlockSpec(memory_space=pltpu.VMEM)] * 7,
        out_specs=(pl.BlockSpec(memory_space=pltpu.VMEM),) * 2,
        scratch_shapes=[pltpu.VMEM((columns, count), F32)],
        compiler_params=pltpu.CompilerParams(vmem_limit_bytes=(8 + high.shape[0] // 128) * MIB),
        name="score",
    )(*pieces, in_blocks, out_blocks, high, low)


def place_kernel(bit, size, kept_ref, received_ref, out_ref):
    mine = (lax.axis_index("dp") // bit) % 2
    for k in range(kept_ref.shape[1] // size):
        first = (k // bit) * 2 * bit + k % bit
        for ref, value in ((kept_ref, mine), (received_ref, 1 - mine)):
            start = pl.multiple_of((first + value * bit) * size, size)
            out_ref[:, pl.ds(start, size)] = ref[:, k * size : (k + 1) * size]


def place(bit, size, kept, received):
    rows, columns = kept.shape
    return pl.pallas_call(
        functools.partial(place_kernel, bit, size),
        out_shape=jax.ShapeDtypeStruct((rows, 2 * columns), F32),
        in_specs=[pl.BlockSpec(memory_space=pltpu.VMEM)] * 2,
        out_specs=pl.BlockSpec(memory_space=pltpu.VMEM),
        compiler_params=pltpu.CompilerParams(vmem_limit_bytes=8 * MIB),
        name="place",
    )(kept, received)


FINAL_LOW = False
ORDER = "21x"
E_STAGES = (1, 2)
Q_STAGE = 1


def body(mesh, activations, out_grads, proj_in, proj_out, lengths, queries):
    n_dp, n_query = mesh.shape["dp"], mesh.shape["query"]
    core_bit = 1
    query_bits = [2 * b for b in bits_of(n_query)]
    unit = 2 * n_query
    final = 1 if FINAL_LOW else n_dp // 2
    far = tuple(b for b in bits_of(n_dp) if b != final)

    half = pick_queries(queries)
    same = [half]
    for bit in far:
        same = same + [swap(h, mesh, bit * unit) for h in same]
    same = same[1:]

    own = project(activations, out_grads, proj_in, proj_out, half)
    other = swap(own, mesh, core_bit)

    own, other, same = lax.optimization_barrier((own, other, same))

    factor = fisher(lengths, own, other)
    factor, own, other = lax.optimization_barrier((factor, own, other))
    blocks = example_grads(lengths, own, other)[None]
    dp_bits = [b * unit for b in bits_of(n_dp)]
    groups = {"x": query_bits, "1": dp_bits[:1], "2": dp_bits[1:]}
    steps = [bit | core_bit for name in ORDER for bit in groups[name]]
    exchange = [bit | core_bit for bit in query_bits + [final * unit]]
    stages = {E_STAGES[0] + i: [m] for i, m in enumerate(exchange[:-1])}
    stages.setdefault(max(E_STAGES[1], E_STAGES[0] + len(exchange) - 1), []).append(exchange[-1])

    def beside(stage, factor, blocks, same):
        for mask in stages.get(stage, ()):
            blocks, factor = lax.optimization_barrier((blocks, factor))
            blocks = jnp.concatenate([blocks, swap(blocks, mesh, mask)], axis=0)
        if stage == Q_STAGE:
            same, factor = lax.optimization_barrier((same, factor))
        return factor, blocks, same

    for step, mask in enumerate(steps):
        factor, blocks, same = beside(step, factor, blocks, same)
        received = swap(factor, mesh, mask)
        if step < len(steps) - 1:
            factor = factor + received
    received, blocks, same = beside(len(steps), received, blocks, same)
    others = [swap(h, mesh, core_bit) for h in same]
    in_blocks, out_blocks = inverses(factor, received)

    arranged = arrange_examples(blocks, n_query)
    high, low = split_queries(far, queries, same, others)
    kept, sent = score(arranged, in_blocks, out_blocks, high, low)
    return place(final, queries.shape[1], kept, swap(sent, mesh, final * unit | core_bit))


def solution(mesh):
    in_specs = (
        P(("grp", "dp", "query"), "proj"),
        P(("grp", "dp", "query"), "proj"),
        P("proj", None),
        P("proj", None),
        P(("grp", "dp", "query"), None),
        P("query", "dp", None),
    )
    out_specs = P(("grp", "dp"), "query")
    return jax.shard_map(
        functools.partial(body, mesh), mesh=mesh, in_specs=in_specs, out_specs=out_specs, check_vma=False
    )
```

time: 55.2 us -> 37.2 us (0.67)
  Pallas kernels: 21.9 us -> 11.2 us
  local copies, waits for them, and re-layouts: 5.47 us -> 0.03 us
  other arithmetic: 3.78 us -> 0.04 us
  waiting for transfers between devices: 11.8 us -> 14.5 us
    pallas_call x1, Pallas kernels: 6.55 us -> 1.82 us  [score(): pl.pallas_call(score_kernel, out_shape=(shape, shape), in_specs=[pl.Block...]
    unnamed x12, local copies, waits for them, and re-layouts: 4.5 us -> 0.03 us
    concatenate x3 -> x2, other arithmetic: 3.04 us -> 0.03 us  [beside(): blocks = jnp.concatenate([blocks, swap(blocks, mesh, mask)], axis=0)]
    ppermute x9, waiting for transfers between devices: 11.8 us -> 14.5 us  [swap(): return lax.ppermute(value, AXES, [(i, i ^ mask) for i in range(count)])]
    pallas_call x2 -> x5, Pallas kernels: 8.87 us -> 6.44 us  [the longest x1 2.88 us: project(): pl.pallas_call(project_kernel, out_shape=jax.ShapeDtypeStruct((2 * proj_i...]
    pallas_call x1, Pallas kernels: 1.97 us -> 0.58 us  [arrange_examples(): pl.pallas_call(functools.partial(arrange_examples_kernel, n_query), out_s...]
    pallas_call x1, Pallas kernels: 2.6 us -> 1.51 us  [example_grads(): pl.pallas_call(examples_kernel, out_shape=jax.ShapeDtypeStruct((lengths.s...]
    pallas_call x1, Pallas kernels: 1.95 us -> 0.89 us  [fisher(): pl.pallas_call(fisher_kernel, out_shape=jax.ShapeDtypeStruct((width, 128)...]
  transfers between devices with their start and end apart: 9 -> 9, of which waited for: 5 -> 7; matrix products, arithmetic and copies ran while one was open for 6% -> 0% of each run, Pallas kernels for 28% -> 18%
where the time goes in v2:
time: 37.2 us; the launch traced here: 37.1 us
  waiting for transfers between devices  14.5 us (39%)
  Pallas kernels  11.2 us (30%)
  starting transfers between devices  11.2 us (30%)
    ppermute x9, waiting for transfers between devices, swap(): return lax.ppermute(value, AXES, [(i, i ^ mask) for i in range(count)])  14.5 us
    ppermute x9, starting transfers between devices, swap(): return lax.ppermute(value, AXES, [(i, i ^ mask) for i in range(count)])  11.2 us
    pallas_call x1, Pallas kernels, project(): pl.pallas_call(project_kernel, out_shape=jax.ShapeDtypeStruct((2 * proj_i...  2.88 us
    pallas_call x1, Pallas kernels, score(): pl.pallas_call(score_kernel, out_shape=(shape, shape), in_specs=[pl.Block...  1.82 us
    pallas_call x1, Pallas kernels, inverses(): pl.pallas_call(inverses_kernel, out_shape=(shape, shape), in_specs=[pl.Bl...  1.63 us
    pallas_call x1, Pallas kernels, example_grads(): pl.pallas_call(examples_kernel, out_shape=jax.ShapeDtypeStruct((lengths.s...  1.51 us
    pallas_call x1, Pallas kernels, pick_queries(): pl.pallas_call(pick_kernel, out_shape=jax.ShapeDtypeStruct((rows // 2, co...  1.11 us
    pallas_call x1, Pallas kernels, fisher(): pl.pallas_call(fisher_kernel, out_shape=jax.ShapeDtypeStruct((width, 128)...  0.89 us
  transfers between devices with their start and end apart: 9, of which 7 were waited for; matrix products, arithmetic and copies ran while one was open for 0% of the time, Pallas kernels for 18%

profile of v2, /device:TPU:0, one launch (start us, length us, event | category | flops | bytes accessed | tf_op | source)
XLA Modules:
  0.0 37.1 jit_solution(18345439814066727395)
XLA Ops:
  0.0 1.1 %pick_queries.1.after_ref = f32[64,1024]{1,0:T(8,128)S(1)} custom-call(f32[1,128,1024]{2,1,0:T(8,128)} %own_ref.1), custom_call_target="tpu_custom_call" | custom-call | flops 4000000000 | bytes 1000000 | tf_op jit(solution)/shard_map/pick_queries/pallas_call | solution.py:40
  1.1 3.1 %collective-permute-start.1 = (f32[64,1024]{1,0:T(8,128)S(1)}, f32[64,1024]{1,0:T(8,128)S(1)}, u32[]{:S(2)}, u32[]{:S(2)}) collective-permute-start(f32[64,1024]{1,0:T(8,128)S(1)} %pick_queries.1.after_ref), channel_id=1, source_target_pairs={{0,4},{1,5},{2,6},{3,7},{4,0},{5,1},{6,2},{7,3},{8,12},{9,13},{10,... | collective-permute-start | bytes 786440 | tf_op jit(solution)/shard_map/ppermute | solution.py:23
  4.3 2.9 %project.1.own_ref = f32[64,512]{1,0:T(8,128)S(1)} custom-call(bf16[512,2048]{1,0:T(8,128)(2,1)S(1)} %copy-done.1, bf16[512,7168]{1,0:T(8,128)(2,1)S(1)} %copy-done, bf16[32,2048]{1,0:T(8,128)(2,1)S(1)} %bitcast.4, bf16[32,7168]{1,0:T(8,128)(2,1)S(1)} %bitcast.3, f32[64,1024]{1,0:T(8,128)S(1)} %pick_queries.1.after_ref), custom_call_target="tpu_custom_call" | custom-call | tf_op jit(solution)/shard_map/project/pallas_call | solution.py:59
  7.1 0.2 collective-permute-start
  7.3 1.2 %collective-permute-done.other_ref = f32[64,512]{1,0:T(8,128)S(1)} collective-permute-done((f32[64,512]{1,0:T(8,128)S(1)}, f32[64,512]{1,0:T(8,128)S(1)}, u32[]{:S(2)}, u32[]{:S(2)}) %collective-permute-start) | collective-permute-done | bytes 131104 | tf_op jit(solution)/shard_map/ppermute | solution.py:23
  8.5 2.0 %collective-permute-done.1.refs_0_ = f32[64,1024]{1,0:T(8,128)S(1)} collective-permute-done((f32[64,1024]{1,0:T(8,128)S(1)}, f32[64,1024]{1,0:T(8,128)S(1)}, u32[]{:S(2)}, u32[]{:S(2)}) %collective-permute-start.1) | collective-permute-done | bytes 262176 | tf_op jit(solution)/shard_map/ppermute | solution.py:23
  10.6 0.9 %fisher.1 = f32[32,128]{1,0:T(8,128)S(1)} custom-call(s32[1,17]{1,0:T(1,128)S(1)} %copy-done.5, f32[64,512]{1,0:T(8,128)S(1)} %project.1.own_ref, f32[64,512]{1,0:T(8,128)S(1)} %collective-permute-done.other_ref), custom_call_target="tpu_custom_call" | custom-call | tf_op jit(solution)/shard_map/fisher/pallas_call | solution.py:83
  11.5 1.5 %collective-permute-start.2 = (f32[32,128]{1,0:T(8,128)S(1)}, f32[32,128]{1,0:T(8,128)S(1)}, u32[]{:S(2)}, u32[]{:S(2)}) collective-permute-start(f32[32,128]{1,0:T(8,128)S(1)} %fisher.1), channel_id=1, source_target_pairs={{0,9},{1,8},{2,11},{3,10},{4,13},{5,12},{6,15},{7,14},{8,1},{9,0},... | collective-permute-start | bytes 49160 | tf_op jit(solution)/shard_map/ppermute | solution.py:23
  13.0 1.5 %examples.1 = f32[16,1024]{1,0:T(8,128)S(1)} custom-call(s32[1,17]{1,0:T(1,128)S(1)} %copy-done.5, f32[64,512]{1,0:T(8,128)S(1)} %project.1.own_ref, f32[64,512]{1,0:T(8,128)S(1)} %collective-permute-done.other_ref), custom_call_target="tpu_custom_call" | custom-call | flops 2000000000 | bytes 1000000 | tf_op jit(solution)/shard_map/examples/pallas_call | solution.py:130
  14.5 1.1 %collective-permute-done.2 = f32[32,128]{1,0:T(8,128)S(1)} collective-permute-done((f32[32,128]{1,0:T(8,128)S(1)}, f32[32,128]{1,0:T(8,128)S(1)}, u32[]{:S(2)}, u32[]{:S(2)}) %collective-permute-start.2) | collective-permute-done | bytes 16416 | tf_op jit(solution)/shard_map/ppermute | solution.py:23
  15.6 1.5 %collective-permute-start.3 = (f32[1,16,1024]{2,1,0:T(8,128)S(1)}, f32[1,16,1024]{2,1,0:T(8,128)S(1)}, u32[]{:S(2)}, u32[]{:S(2)}) collective-permute-start(f32[1,16,1024]{2,1,0:T(8,128)S(1)} %bitcast.5), channel_id=1, source_target_pairs={{0,3},{1,2},{2,1},{3,0},{4,7},{5,6},{6,5},{7,4},{8,11},{9,10},{10,... | collective-permute-start | bytes 196616 | tf_op jit(solution)/shard_map/ppermute | solution.py:23
  17.1 1.4 %collective-permute-start.4 = (f32[32,128]{1,0:T(8,128)S(1)}, f32[32,128]{1,0:T(8,128)S(1)}, u32[]{:S(2)}, u32[]{:S(2)}) collective-permute-start(f32[32,128]{1,0:T(8,128)S(1)} %add.6), channel_id=1, source_target_pairs={{0,5},{1,4},{2,7},{3,6},{4,1},{5,0},{6,3},{7,2},{8,13},{9,12},{10,... | collective-permute-start | bytes 49160 | tf_op jit(solution)/shard_map/ppermute | solution.py:23
  18.5 0.2 collective-permute-start.7
  18.8 1.5 %collective-permute-done.4 = f32[32,128]{1,0:T(8,128)S(1)} collective-permute-done((f32[32,128]{1,0:T(8,128)S(1)}, f32[32,128]{1,0:T(8,128)S(1)}, u32[]{:S(2)}, u32[]{:S(2)}) %collective-permute-start.4) | collective-permute-done | bytes 16416 | tf_op jit(solution)/shard_map/ppermute | solution.py:23
  20.3 2.5 %collective-permute-start.5 = (f32[2,16,1024]{2,1,0:T(8,128)S(1)}, f32[2,16,1024]{2,1,0:T(8,128)S(1)}, u32[]{:S(2)}, u32[]{:S(2)}) collective-permute-start(f32[2,16,1024]{2,1,0:T(8,128)S(1)} %pad_maximum_fusion.1), channel_id=1, source_target_pairs={{0,9},{1,8},{2,11},{3,10},{4,13},{5,12},{6,15},{7,14},{8,1},{9,0},... | collective-permute-start | bytes 393224 | tf_op jit(solution)/shard_map/ppermute | solution.py:23
  22.8 0.5 %collective-permute-start.6 = (f32[32,128]{1,0:T(8,128)S(1)}, f32[32,128]{1,0:T(8,128)S(1)}, u32[]{:S(2)}, u32[]{:S(2)}) collective-permute-start(f32[32,128]{1,0:T(8,128)S(1)} %add.7.own_ref), channel_id=1, source_target_pairs={{0,3},{1,2},{2,1},{3,0},{4,7},{5,6},{6,5},{7,4},{8,11},{9,10},{10,... | collective-permute-start | bytes 49160 | tf_op jit(solution)/shard_map/ppermute | solution.py:23
  23.3 2.6 %collective-permute-done.6.other_ref = f32[32,128]{1,0:T(8,128)S(1)} collective-permute-done((f32[32,128]{1,0:T(8,128)S(1)}, f32[32,128]{1,0:T(8,128)S(1)}, u32[]{:S(2)}, u32[]{:S(2)}) %collective-permute-start.6) | collective-permute-done | bytes 16416 | tf_op jit(solution)/shard_map/ppermute | solution.py:23
  26.0 1.6 %inverses.1 = (bf16[3,256,256]{2,1,0:T(8,128)(2,1)S(1)}, bf16[3,256,256]{2,1,0:T(8,128)(2,1)S(1)}) custom-call(f32[32,128]{1,0:T(8,128)S(1)} %add.7.own_ref, f32[32,128]{1,0:T(8,128)S(1)} %collective-permute-done.6.other_ref), custom_call_target="tpu_custom_call" | custom-call | tf_op jit(solution)/shard_map/inverses/pallas_call | solution.py:277
  27.6 1.9 %collective-permute-done.5 = f32[2,16,1024]{2,1,0:T(8,128)S(1)} collective-permute-done((f32[2,16,1024]{2,1,0:T(8,128)S(1)}, f32[2,16,1024]{2,1,0:T(8,128)S(1)}, u32[]{:S(2)}, u32[]{:S(2)}) %collective-permute-start.5) | collective-permute-done | bytes 131104 | tf_op jit(solution)/shard_map/ppermute | solution.py:23
  29.5 0.6 %arrange_examples.1 = (bf16[256,256]{1,0:T(8,128)(2,1)S(1)}, bf16[256,256]{1,0:T(8,128)(2,1)S(1)}, bf16[256,256]{1,0:T(8,128)(2,1)S(1)}) custom-call(f32[4,16,1024]{2,1,0:T(8,128)S(1)} %pad_maximum_fusion.blocks_ref), custom_call_target="tpu_custom_call" | custom-call | tf_op jit(solution)/shard_map/arrange_examples/pallas_call | solution.py:174
  30.1 0.2 split_queries.1
  30.3 1.8 %score.1 = (f32[32,256]{1,0:T(8,128)S(1)}, f32[32,256]{1,0:T(8,128)S(1)}) custom-call(bf16[256,256]{1,0:T(8,128)(2,1)S(1)} %get-tuple-element.36.high_ref, bf16[256,256]{1,0:T(8,128)(2,1)S(1)} %get-tuple-element.37.middle_ref, bf16[256,256]{1,0:T(8,128)(2,1)S(1)} %get-tuple-element.38.low_ref, bf16[3,256,256]{2,1,0:T(8,128)(2,1)S(1)} %get-tuple-element.40.in_ref, ...), custom_call_target="tpu_custom_call" | custom-call | tf_op jit(solution)/shard_map/score/pallas_call | solution.py:319
  32.2 4.2 %collective-permute-done.8.received_ref = f32[32,256]{1,0:T(8,128)S(1)} collective-permute-done((f32[32,256]{1,0:T(8,128)S(1)}, f32[32,256]{1,0:T(8,128)S(1)}, u32[]{:S(2)}, u32[]{:S(2)}) %collective-permute-start.8) | collective-permute-done | bytes 32800 | tf_op jit(solution)/shard_map/ppermute | solution.py:23
  36.4 0.6 %place.1 = f32[32,512]{1,0:T(8,128)} custom-call(f32[32,256]{1,0:T(8,128)S(1)} %get-tuple-element.45.kept_ref, f32[32,256]{1,0:T(8,128)S(1)} %collective-permute-done.8.received_ref), custom_call_target="tpu_custom_call" | custom-call | tf_op jit(solution)/shard_map/place/pallas_call | solution.py:341
  (19 shorter events, 0.1 us)
Async XLA Ops:
  0.0 4.2 %copy-start.3 = (bf16[7168,32]{0,1:T(8,128)(2,1)S(1)}, bf16[7168,32]{0,1:T(8,128)(2,1)}, u32[]{:S(2)}) copy-start(bf16[7168,32]{0,1:T(8,128)(2,1)} %param.9) | copy-start | bytes 1376260
  0.0 4.2 %copy-start.4 = (bf16[2048,32]{0,1:T(8,128)(2,1)S(1)}, bf16[2048,32]{0,1:T(8,128)(2,1)}, u32[]{:S(2)}) copy-start(bf16[2048,32]{0,1:T(8,128)(2,1)} %param.8) | copy-start | bytes 393220
  0.0 4.2 %copy-start = (bf16[512,7168]{1,0:T(8,128)(2,1)S(1)}, bf16[512,7168]{1,0:T(8,128)(2,1)}, u32[]{:S(2)}) copy-start(bf16[512,7168]{1,0:T(8,128)(2,1)} %g_ref.1) | copy-start | bytes 22020100
  0.0 4.2 %copy-start.1 = (bf16[512,2048]{1,0:T(8,128)(2,1)S(1)}, bf16[512,2048]{1,0:T(8,128)(2,1)}, u32[]{:S(2)}) copy-start(bf16[512,2048]{1,0:T(8,128)(2,1)} %a_ref.1) | copy-start | bytes 6291460
  1.1 9.4 %copy-start.5 = (s32[1,17]{1,0:T(1,128)S(1)}, s32[1,17]{1,0:T(1,128)}, u32[]{:S(2)}) copy-start(s32[1,17]{1,0:T(1,128)} %lengths_ref.3) | copy-start | bytes 208
  1.1 9.4 %collective-permute-start.1 = (f32[64,1024]{1,0:T(8,128)S(1)}, f32[64,1024]{1,0:T(8,128)S(1)}, u32[]{:S(2)}, u32[]{:S(2)}) collective-permute-start(f32[64,1024]{1,0:T(8,128)S(1)} %pick_queries.1.after_ref), channel_id=1, source_target_pairs={{0,4},{1,5},{2,6},{3,7},{4,0},{5,1},{6,2},{7,3},{8,12},{9,13},{10,... | collective-permute-start | bytes 786440 | tf_op jit(solution)/shard_map/ppermute | solution.py:23
  4.3 25.8 %copy-start.2 = (f32[1,128,1024]{2,1,0:T(8,128)S(1)}, f32[1,128,1024]{2,1,0:T(8,128)}, u32[]{:S(2)}) copy-start(f32[1,128,1024]{2,1,0:T(8,128)} %own_ref.1) | copy-start | bytes 1572868
  7.1 1.4 %collective-permute-start = (f32[64,512]{1,0:T(8,128)S(1)}, f32[64,512]{1,0:T(8,128)S(1)}, u32[]{:S(2)}, u32[]{:S(2)}) collective-permute-start(f32[64,512]{1,0:T(8,128)S(1)} %project.1.own_ref), channel_id=1, source_target_pairs={{0,1},{1,0},{2,3},{3,2},{4,5},{5,4},{6,7},{7,6},{8,9},{9,8},{10,11... | collective-permute-start | bytes 393224 | tf_op jit(solution)/shard_map/ppermute | solution.py:23
  11.5 4.1 %collective-permute-start.2 = (f32[32,128]{1,0:T(8,128)S(1)}, f32[32,128]{1,0:T(8,128)S(1)}, u32[]{:S(2)}, u32[]{:S(2)}) collective-permute-start(f32[32,128]{1,0:T(8,128)S(1)} %fisher.1), channel_id=1, source_target_pairs={{0,9},{1,8},{2,11},{3,10},{4,13},{5,12},{6,15},{7,14},{8,1},{9,0},... | collective-permute-start | bytes 49160 | tf_op jit(solution)/shard_map/ppermute | solution.py:23
  15.6 4.7 %collective-permute-start.3 = (f32[1,16,1024]{2,1,0:T(8,128)S(1)}, f32[1,16,1024]{2,1,0:T(8,128)S(1)}, u32[]{:S(2)}, u32[]{:S(2)}) collective-permute-start(f32[1,16,1024]{2,1,0:T(8,128)S(1)} %bitcast.5), channel_id=1, source_target_pairs={{0,3},{1,2},{2,1},{3,0},{4,7},{5,6},{6,5},{7,4},{8,11},{9,10},{10,... | collective-permute-start | bytes 196616 | tf_op jit(solution)/shard_map/ppermute | solution.py:23
  17.1 3.2 %collective-permute-start.4 = (f32[32,128]{1,0:T(8,128)S(1)}, f32[32,128]{1,0:T(8,128)S(1)}, u32[]{:S(2)}, u32[]{:S(2)}) collective-permute-start(f32[32,128]{1,0:T(8,128)S(1)} %add.6), channel_id=1, source_target_pairs={{0,5},{1,4},{2,7},{3,6},{4,1},{5,0},{6,3},{7,2},{8,13},{9,12},{10,... | collective-permute-start | bytes 49160 | tf_op jit(solution)/shard_map/ppermute | solution.py:23
  18.5 11.6 %collective-permute-start.7 = (f32[64,1024]{1,0:T(8,128)S(1)}, f32[64,1024]{1,0:T(8,128)S(1)}, u32[]{:S(2)}, u32[]{:S(2)}) collective-permute-start(f32[64,1024]{1,0:T(8,128)S(1)} %collective-permute-done.1.refs_0_), channel_id=1, source_target_pairs={{0,1},{1,0},{2,3},{3,2},{4,5},{5,4},{6,7},{7,6},{8,9},{9,8},{10,11... | collective-permute-start | bytes 786440 | tf_op jit(solution)/shard_map/ppermute | solution.py:23
  20.3 9.2 %collective-permute-start.5 = (f32[2,16,1024]{2,1,0:T(8,128)S(1)}, f32[2,16,1024]{2,1,0:T(8,128)S(1)}, u32[]{:S(2)}, u32[]{:S(2)}) collective-permute-start(f32[2,16,1024]{2,1,0:T(8,128)S(1)} %pad_maximum_fusion.1), channel_id=1, source_target_pairs={{0,9},{1,8},{2,11},{3,10},{4,13},{5,12},{6,15},{7,14},{8,1},{9,0},... | collective-permute-start | bytes 393224 | tf_op jit(solution)/shard_map/ppermute | solution.py:23
  22.8 3.2 %collective-permute-start.6 = (f32[32,128]{1,0:T(8,128)S(1)}, f32[32,128]{1,0:T(8,128)S(1)}, u32[]{:S(2)}, u32[]{:S(2)}) collective-permute-start(f32[32,128]{1,0:T(8,128)S(1)} %add.7.own_ref), channel_id=1, source_target_pairs={{0,3},{1,2},{2,1},{3,0},{4,7},{5,6},{6,5},{7,4},{8,11},{9,10},{10,... | collective-permute-start | bytes 49160 | tf_op jit(solution)/shard_map/ppermute | solution.py:23
  32.1 4.3 %collective-permute-start.8 = (f32[32,256]{1,0:T(8,128)S(1)}, f32[32,256]{1,0:T(8,128)S(1)}, u32[]{:S(2)}, u32[]{:S(2)}) collective-permute-start(f32[32,256]{1,0:T(8,128)S(1)} %get-tuple-element.46), channel_id=1, source_target_pairs={{0,9},{1,8},{2,11},{3,10},{4,13},{5,12},{6,15},{7,14},{8,1},{9,0},... | collective-permute-start | bytes 98312 | tf_op jit(solution)/shard_map/ppermute | solution.py:23

commit v3 on v2

--- a/solution.py
+++ b/solution.py
@@ -12,7 +12,7 @@
 BF16 = jnp.bfloat16
 HIGHEST = lax.Precision.HIGHEST
 NT = (((1,), (1,)), ((), ()))
-AXES = ("dp", "query", "proj")
+AXES = ("grp", "dp", "query", "proj")
 MIB = 2**20
 CHUNK = 256
 QUERY_STEP = 1
@@ -27,22 +27,28 @@
     return [1 << b for b in range(size.bit_length() - 1)]
 
 
-def pick_kernel(queries_hbm, half_ref, sem):
-    half = half_ref.shape[0]
-    start = pl.multiple_of(lax.axis_index("proj") * half, 8)
-    copy = pltpu.make_async_copy(queries_hbm.at[0, pl.ds(start, half)], half_ref, sem)
-    copy.start()
-    copy.wait()
-
-
-def pick_queries(queries):
+def pick_kernel(groups, queries_hbm, half_ref, piece_ref, sems):
+    half, piece = half_ref.shape[0], piece_ref.shape[0]
+    core = lax.axis_index("proj")
+    index = core * groups + lax.axis_index("grp")
+    copies = [
+        pltpu.make_async_copy(queries_hbm.at[0, pl.ds(pl.multiple_of(core * half, 8), half)], half_ref, sems.at[0]),
+        pltpu.make_async_copy(queries_hbm.at[0, pl.ds(pl.multiple_of(index * piece, 8), piece)], piece_ref, sems.at[1]),
+    ]
+    for copy in copies:
+        copy.start()
+    for copy in copies:
+        copy.wait()
+
+
+def pick_queries(queries, groups):
     rows, columns = queries.shape[1:]
     return pl.pallas_call(
-        pick_kernel,
-        out_shape=jax.ShapeDtypeStruct((rows // 2, columns), F32),
+        functools.partial(pick_kernel, groups),
+        out_shape=tuple(jax.ShapeDtypeStruct((rows // n, columns), F32) for n in (2, 2 * groups)),
         in_specs=[pl.BlockSpec(memory_space=pl.ANY)],
-        out_specs=pl.BlockSpec(memory_space=pltpu.VMEM),
-        scratch_shapes=[pltpu.SemaphoreType.DMA],
+        out_specs=(pl.BlockSpec(memory_space=pltpu.VMEM),) * 2,
+        scratch_shapes=[pltpu.SemaphoreType.DMA((2,))],
         compiler_params=pltpu.CompilerParams(vmem_limit_bytes=4 * MIB),
         cost_estimate=pl.CostEstimate(flops=4 * 10**9, bytes_accessed=10**6, transcendentals=0),
         name="pick_queries",
@@ -66,43 +72,8 @@
     )(activations, out_grads, proj_in.T, proj_out.T, after)
 
 
-def fisher_kernel(lengths_ref, own_ref, other_ref, out_ref):
-    width = out_ref.shape[0]
-    both = own_ref[...] + other_ref[...]
-    live_slots = lax.fori_loop(0, lengths_ref.shape[1] - 1, lambda e, n: n + lengths_ref[0, e], jnp.int32(0))
-    slot = lax.broadcasted_iota(jnp.int32, both.shape, 1)
-    live = jnp.where(slot < live_slots, both, 0.0)
-    gram = lax.dot_general(live, both, NT, precision=HIGHEST, preferred_element_type=F32)
-    out_ref[...] = jnp.zeros_like(out_ref)
-    out_ref[:, 0:width] = gram[0:width, 0:width]
-    out_ref[:, width : 2 * width] = gram[width : 2 * width, width : 2 * width]
-
-
-def fisher(lengths, own, other):
-    width = own.shape[0] // 2
-    return pl.pallas_call(
-        fisher_kernel,
-        out_shape=jax.ShapeDtypeStruct((width, 128), F32),
-        in_specs=[pl.BlockSpec(memory_space=pltpu.SMEM)] + [pl.BlockSpec(memory_space=pltpu.VMEM)] * 2,
-        out_specs=pl.BlockSpec(memory_space=pltpu.VMEM),
-        compiler_params=pltpu.CompilerParams(vmem_limit_bytes=8 * MIB),
-        name="fisher",
-    )(lengths, own, other)
-
-
-def split3(value):
-    high = value.astype(BF16)
-    rest = value - high.astype(F32)
-    middle = rest.astype(BF16)
-    return high, middle, (rest - middle.astype(F32)).astype(BF16)
-
-
-def examples_kernel(lengths_ref, own_ref, other_ref, out_ref):
-    examples = out_ref.shape[0]
-    width = own_ref.shape[0] // 2
-    slots = own_ref.shape[1]
-    both = own_ref[...] + other_ref[...]
-    inputs, outputs = both[0:width], both[width : 2 * width]
+def masks_kernel(lengths_ref, after_ref, member_ref, live_ref, count_ref):
+    examples, slots = member_ref.shape
     index = lax.broadcasted_iota(jnp.int32, (examples, 1), 0)
     starts = jnp.zeros((examples, 1), jnp.int32)
     counts = jnp.zeros((examples, 1), jnp.int32)
@@ -113,8 +84,61 @@
         counts = jnp.where(index == e, length, counts)
         begin = begin + length
     slot = lax.broadcasted_iota(jnp.int32, (examples, slots), 1)
-    member = jnp.where((slot >= starts) & (slot < starts + counts), 1.0, 0.0).astype(BF16)
-    divisor = counts.astype(F32)
+    member_ref[...] = jnp.where((slot >= starts) & (slot < starts + counts), 1.0, 0.0).astype(BF16)
+    live_ref[...] = jnp.where(slot[0:8] < begin, 1.0, 0.0)
+    count_ref[...] = jnp.broadcast_to(counts.astype(F32), count_ref.shape)
+
+
+def masks(lengths, after):
+    examples, slots = lengths.shape[1] - 1, after.shape[1]
+    return pl.pallas_call(
+        masks_kernel,
+        out_shape=(
+            jax.ShapeDtypeStruct((examples, slots), BF16),
+            jax.ShapeDtypeStruct((8, slots), F32),
+            jax.ShapeDtypeStruct((examples, 128), F32),
+        ),
+        in_specs=[pl.BlockSpec(memory_space=pltpu.SMEM), pl.BlockSpec(memory_space=pl.ANY)],
+        out_specs=(pl.BlockSpec(memory_space=pltpu.VMEM),) * 3,
+        compiler_params=pltpu.CompilerParams(vmem_limit_bytes=4 * MIB),
+        cost_estimate=pl.CostEstimate(flops=2 * 10**9, bytes_accessed=10**6, transcendentals=0),
+        name="masks",
+    )(lengths, after)
+
+
+def fisher_kernel(live_ref, own_ref, other_ref, out_ref):
+    width = out_ref.shape[0]
+    both = own_ref[...] + other_ref[...]
+    gram = lax.dot_general(both * live_ref[0:1, :], both, NT, precision=HIGHEST, preferred_element_type=F32)
+    out_ref[...] = jnp.zeros_like(out_ref)
+    out_ref[:, 0:width] = gram[0:width, 0:width]
+    out_ref[:, width : 2 * width] = gram[width : 2 * width, width : 2 * width]
+
+
+def fisher(live, own, other):
+    width = own.shape[0] // 2
+    return pl.pallas_call(
+        fisher_kernel,
+        out_shape=jax.ShapeDtypeStruct((width, 128), F32),
+        in_specs=[pl.BlockSpec(memory_space=pltpu.VMEM)] * 3,
+        out_specs=pl.BlockSpec(memory_space=pltpu.VMEM),
+        compiler_params=pltpu.CompilerParams(vmem_limit_bytes=8 * MIB),
+        name="fisher",
+    )(live, own, other)
+
+
+def split3(value):
+    high = value.astype(BF16)
+    rest = value - high.astype(F32)
+    middle = rest.astype(BF16)
+    return high, middle, (rest - middle.astype(F32)).astype(BF16)
+
+
+def examples_kernel(member_ref, count_ref, own_ref, other_ref, out_ref):
+    width = own_ref.shape[0] // 2
+    both = own_ref[...] + other_ref[...]
+    inputs, outputs = both[0:width], both[width : 2 * width]
+    member, divisor = member_ref[...], count_ref[:, 0:1]
     group = 8
     for first in range(0, width, group):
         outer = jnp.concatenate([outputs[i : i + 1] * inputs for i in range(first, first + group)], axis=0)
@@ -125,17 +149,17 @@
         out_ref[:, first * width : (first + group) * width] = total / divisor
 
 
-def example_grads(lengths, own, other):
+def example_grads(member, count, own, other):
     width = own.shape[0] // 2
     return pl.pallas_call(
         examples_kernel,
-        out_shape=jax.ShapeDtypeStruct((lengths.shape[1] - 1, width * width), F32),
-        in_specs=[pl.BlockSpec(memory_space=pltpu.SMEM)] + [pl.BlockSpec(memory_space=pltpu.VMEM)] * 2,
+        out_shape=jax.ShapeDtypeStruct((member.shape[0], width * width), F32),
+        in_specs=[pl.BlockSpec(memory_space=pltpu.VMEM)] * 4,
         out_specs=pl.BlockSpec(memory_space=pltpu.VMEM),
         compiler_params=pltpu.CompilerParams(vmem_limit_bytes=8 * MIB),
         cost_estimate=pl.CostEstimate(flops=2 * 10**9, bytes_accessed=10**6, transcendentals=0),
         name="examples",
-    )(lengths, own, other)
+    )(member, count, own, other)
 
 
 def split2(value):
@@ -182,36 +206,37 @@
     )(blocks)
 
 
-def split_queries_kernel(bits, own_ref, *refs):
-    parts = 1 << len(bits)
-    same_refs, other_refs, (high_ref, low_ref) = refs[: parts - 1], refs[parts - 1 : -2], refs[-2:]
-    rows = own_ref.shape[1]
-    half = rows // 2
-    dp, core = lax.axis_index("dp"), lax.axis_index("proj")
-    place = sum(((dp // bit) % 2) << b for b, bit in enumerate(bits))
+def split_queries_kernel(groups, own_ref, *refs):
+    fetched_refs, (high_ref, low_ref) = refs[:-2], refs[-2:]
+    half = own_ref.shape[1] // 2
+    piece = half // groups
+    place, group, core = lax.axis_index("dp"), lax.axis_index("grp"), lax.axis_index("proj")
 
     def put(start, value):
         at = pl.ds(pl.multiple_of(start, 16), value.shape[0])
         high_ref[at, :], low_ref[at, :] = split2(value)
 
-    put(place * rows, own_ref[0])
-    for r in range(1, parts):
-        put((place ^ r) * rows + core * half, same_refs[r - 1][...])
-        put((place ^ r) * rows + (1 - core) * half, other_refs[r - 1][...])
-
-
-def split_queries(bits, own, same, other):
-    parts = 1 + len(same)
+    put(place * half, own_ref[0, pl.ds(pl.multiple_of(core * half, 8), half), :])
+    for r, ref in enumerate(fetched_refs, 1):
+        if r == 1:
+            put((place ^ r) * half, ref[...])
+            continue
+        for g in range(groups):
+            put((place ^ r) * half + (group ^ g) * piece, ref[g * piece : (g + 1) * piece, :])
+
+
+def split_queries(groups, own, fetched):
+    parts = 1 + len(fetched)
     rows, columns = own.shape[1:]
-    shape = jax.ShapeDtypeStruct((parts * rows, columns), BF16)
-    return pl.pallas_call(
-        functools.partial(split_queries_kernel, bits),
+    shape = jax.ShapeDtypeStruct((parts * rows // 2, columns), BF16)
+    return pl.pallas_call(
+        functools.partial(split_queries_kernel, groups),
         out_shape=(shape, shape),
-        in_specs=[pl.BlockSpec(memory_space=pltpu.VMEM)] * (1 + len(same) + len(other)),
+        in_specs=[pl.BlockSpec(memory_space=pltpu.VMEM)] * parts,
         out_specs=(pl.BlockSpec(memory_space=pltpu.VMEM),) * 2,
-        compiler_params=pltpu.CompilerParams(vmem_limit_bytes=(4 + 2 * parts) * MIB),
+        compiler_params=pltpu.CompilerParams(vmem_limit_bytes=(4 + parts) * MIB),
         name="split_queries",
-    )(own, *same, *other)
+    )(own, *fetched)
 
 
 def inverse_tiled(fisher_sum):
@@ -293,7 +318,7 @@
     return by_high[0:rows] + (by_high[rows : 2 * rows] + by_middle[0:rows] + small)
 
 
-def score_kernel(high_ref, middle_ref, low_ref, in_ref, out_ref, q_high_ref, q_low_ref, mine_ref, theirs_ref, scratch):
+def score_kernel(high_ref, middle_ref, low_ref, in_ref, out_ref, q_high_ref, q_low_ref, scores_ref, scratch):
     columns, count = scratch.shape
     width = math.isqrt(columns)
     left = times_blocks(high_ref[...], middle_ref[...], low_ref[...], out_ref)
@@ -307,39 +332,37 @@
         by_low = lax.dot_general(high[at], q_low_ref[:, cols], NT, preferred_element_type=F32)
         part = by_high[0:count] + (by_high[count:] + by_low)
         total = part if total is None else total + part
-    total = total * (1.0 / width)
-    mine_ref[...] = total[0 : count // 2]
-    theirs_ref[...] = total[count // 2 :]
+    scores_ref[...] = total * (1.0 / width)
 
 
 def score(pieces, in_blocks, out_blocks, high, low):
-    columns = high.shape[1]
+    rows, columns = high.shape
     count = pieces[0].shape[0] * CHUNK // columns
-    shape = jax.ShapeDtypeStruct((count // 2, high.shape[0]), F32)
     return pl.pallas_call(
         score_kernel,
-        out_shape=(shape, shape),
+        out_shape=jax.ShapeDtypeStruct((count, rows), F32),
         in_specs=[pl.BlockSpec(memory_space=pltpu.VMEM)] * 7,
-        out_specs=(pl.BlockSpec(memory_space=pltpu.VMEM),) * 2,
+        out_specs=pl.BlockSpec(memory_space=pltpu.VMEM),
         scratch_shapes=[pltpu.VMEM((columns, count), F32)],
-        compiler_params=pltpu.CompilerParams(vmem_limit_bytes=(8 + high.shape[0] // 128) * MIB),
+        compiler_params=pltpu.CompilerParams(vmem_limit_bytes=(6 + rows // 128) * MIB),
         name="score",
     )(*pieces, in_blocks, out_blocks, high, low)
 
 
-def place_kernel(bit, size, kept_ref, received_ref, out_ref):
-    mine = (lax.axis_index("dp") // bit) % 2
-    for k in range(kept_ref.shape[1] // size):
-        first = (k // bit) * 2 * bit + k % bit
-        for ref, value in ((kept_ref, mine), (received_ref, 1 - mine)):
-            start = pl.multiple_of((first + value * bit) * size, size)
-            out_ref[:, pl.ds(start, size)] = ref[:, k * size : (k + 1) * size]
-
-
-def place(bit, size, kept, received):
+def place_kernel(half, kept_ref, received_ref, out_ref):
+    core = lax.axis_index("proj")
+    kept, received = kept_ref[...], received_ref[...]
+    first = jnp.where(core == 0, kept, received)
+    second = jnp.where(core == 0, received, kept)
+    for k in range(kept.shape[1] // half):
+        at = slice(k * half, (k + 1) * half)
+        out_ref[:, 2 * k * half : 2 * (k + 1) * half] = jnp.concatenate([first[:, at], second[:, at]], axis=1)
+
+
+def place(half, kept, received):
     rows, columns = kept.shape
     return pl.pallas_call(
-        functools.partial(place_kernel, bit, size),
+        functools.partial(place_kernel, half),
         out_shape=jax.ShapeDtypeStruct((rows, 2 * columns), F32),
         in_specs=[pl.BlockSpec(memory_space=pltpu.VMEM)] * 2,
         out_specs=pl.BlockSpec(memory_space=pltpu.VMEM),
@@ -348,62 +371,55 @@
     )(kept, received)
 
 
-FINAL_LOW = False
-ORDER = "21x"
-E_STAGES = (1, 2)
-Q_STAGE = 1
+ORDER = "x12"
+E_STAGE = 1
+Y_STAGE = 2
 
 
 def body(mesh, activations, out_grads, proj_in, proj_out, lengths, queries):
-    n_dp, n_query = mesh.shape["dp"], mesh.shape["query"]
+    groups, n_dp, n_query = mesh.shape["grp"], mesh.shape["dp"], mesh.shape["query"]
     core_bit = 1
+    unit = 2 * n_query
     query_bits = [2 * b for b in bits_of(n_query)]
-    unit = 2 * n_query
-    final = 1 if FINAL_LOW else n_dp // 2
-    far = tuple(b for b in bits_of(n_dp) if b != final)
-
-    half = pick_queries(queries)
-    same = [half]
-    for bit in far:
-        same = same + [swap(h, mesh, bit * unit) for h in same]
-    same = same[1:]
+    dp_bits = [b * unit for b in bits_of(n_dp)]
+    group_bits = [b * unit * n_dp for b in bits_of(groups)]
+
+    half, piece = pick_queries(queries, groups)
+    fetched = [swap(half if r == 1 else piece, mesh, r * unit) for r in range(1, n_dp)]
 
     own = project(activations, out_grads, proj_in, proj_out, half)
+    member, live, count = masks(lengths, own)
     other = swap(own, mesh, core_bit)
-
-    own, other, same = lax.optimization_barrier((own, other, same))
-
-    factor = fisher(lengths, own, other)
+    own, other, live = lax.optimization_barrier((own, other, live))
+
+    factor = fisher(live, own, other)
     factor, own, other = lax.optimization_barrier((factor, own, other))
-    blocks = example_grads(lengths, own, other)[None]
-    dp_bits = [b * unit for b in bits_of(n_dp)]
-    groups = {"x": query_bits, "1": dp_bits[:1], "2": dp_bits[1:]}
-    steps = [bit | core_bit for name in ORDER for bit in groups[name]]
-    exchange = [bit | core_bit for bit in query_bits + [final * unit]]
-    stages = {E_STAGES[0] + i: [m] for i, m in enumerate(exchange[:-1])}
-    stages.setdefault(max(E_STAGES[1], E_STAGES[0] + len(exchange) - 1), []).append(exchange[-1])
-
-    def beside(stage, factor, blocks, same):
-        for mask in stages.get(stage, ()):
+    blocks = example_grads(member, count, own, other)[None]
+    groups_of = {"x": query_bits, "1": dp_bits[:1], "2": dp_bits[1:]}
+    steps = [bit | core_bit for name in ORDER for bit in groups_of[name]]
+
+    def beside(stage, factor, blocks, fetched):
+        i = stage - E_STAGE
+        if 0 <= i < len(query_bits):
             blocks, factor = lax.optimization_barrier((blocks, factor))
-            blocks = jnp.concatenate([blocks, swap(blocks, mesh, mask)], axis=0)
-        if stage == Q_STAGE:
-            same, factor = lax.optimization_barrier((same, factor))
-        return factor, blocks, same
+            blocks = jnp.concatenate([blocks, swap(blocks, mesh, query_bits[i] | core_bit)], axis=0)
+        if stage == Y_STAGE:
+            fetched, factor = lax.optimization_barrier((fetched, factor))
+            for bit in group_bits:
+                fetched = fetched[:1] + [jnp.concatenate([p, swap(p, mesh, bit)], axis=0) for p in fetched[1:]]
+        return factor, blocks, fetched
 
     for step, mask in enumerate(steps):
-        factor, blocks, same = beside(step, factor, blocks, same)
+        factor, blocks, fetched = beside(step, factor, blocks, fetched)
         received = swap(factor, mesh, mask)
         if step < len(steps) - 1:
             factor = factor + received
-    received, blocks, same = beside(len(steps), received, blocks, same)
-    others = [swap(h, mesh, core_bit) for h in same]
     in_blocks, out_blocks = inverses(factor, received)
 
     arranged = arrange_examples(blocks, n_query)
-    high, low = split_queries(far, queries, same, others)
-    kept, sent = score(arranged, in_blocks, out_blocks, high, low)
-    return place(final, queries.shape[1], kept, swap(sent, mesh, final * unit | core_bit))
+    high, low = split_queries(groups, queries, fetched)
+    scores = score(arranged, in_blocks, out_blocks, high, low)
+    return place(queries.shape[1] // 2, scores, swap(scores, mesh, core_bit))
 
 
 def solution(mesh):

time: 37.2 us -> 32.9 us (0.88)
  waiting for transfers between devices: 14.5 us -> 8.1 us
  starting transfers between devices: 11.2 us -> 13.9 us
  Pallas kernels: 11.2 us -> 10.5 us
    ppermute x9 -> x11, waiting for transfers between devices: 14.5 us -> 8.1 us  [swap(): return lax.ppermute(value, AXES, [(i, i ^ mask) for i in range(count)])]
    ppermute x9 -> x11, starting transfers between devices: 11.2 us -> 13.9 us  [swap(): return lax.ppermute(value, AXES, [(i, i ^ mask) for i in range(count)])]
    pallas_call x1, Pallas kernels: 0.89 us -> 0.27 us  [fisher(): pl.pallas_call(fisher_kernel, out_shape=jax.ShapeDtypeStruct((width, 128)...]
    pallas_call x5 -> x6, Pallas kernels: 5.26 us -> 5.2 us  [the longest x1 1.64 us: score(): pl.pallas_call(score_kernel, out_shape=jax.ShapeDtypeStruct((count, rows)...]
  transfers between devices with their start and end apart: 9 -> 11, of which waited for: 7 -> 6; matrix products, arithmetic and copies ran while one was open for 0% -> 0% of each run, Pallas kernels for 18% -> 21%
where the time goes in v3:
time: 32.9 us; the launch traced here: 32.8 us
  starting transfers between devices  13.9 us (42%)
  Pallas kernels  10.5 us (32%)
  waiting for transfers between devices  8.1 us (25%)
    ppermute x11, starting transfers between devices, swap(): return lax.ppermute(value, AXES, [(i, i ^ mask) for i in range(count)])  13.9 us
    ppermute x11, waiting for transfers between devices, swap(): return lax.ppermute(value, AXES, [(i, i ^ mask) for i in range(count)])  8.1 us
    pallas_call x1, Pallas kernels, project(): pl.pallas_call(project_kernel, out_shape=jax.ShapeDtypeStruct((2 * proj_i...  2.88 us
    pallas_call x1, Pallas kernels, score(): pl.pallas_call(score_kernel, out_shape=jax.ShapeDtypeStruct((count, rows)...  1.64 us
    pallas_call x1, Pallas kernels, inverses(): pl.pallas_call(inverses_kernel, out_shape=(shape, shape), in_specs=[pl.Bl...  1.63 us
    pallas_call x1, Pallas kernels, pick_queries(): pl.pallas_call(functools.partial(pick_kernel, groups), out_shape=tuple((j...  1.15 us
    pallas_call x1, Pallas kernels, example_grads(): pl.pallas_call(examples_kernel, out_shape=jax.ShapeDtypeStruct((member.sh...  0.96 us
    pallas_call x1, Pallas kernels, place(): pl.pallas_call(functools.partial(place_kernel, half), out_shape=jax.Shape...  0.72 us
  transfers between devices with their start and end apart: 11, of which 6 were waited for; matrix products, arithmetic and copies ran while one was open for 0% of the time, Pallas kernels for 21%

profile of v3, /device:TPU:0, one launch (start us, length us, event | category | flops | bytes accessed | tf_op | source)
XLA Modules:
  0.0 32.8 jit_solution(1744646224076000726)
XLA Ops:
  0.0 1.2 %pick_queries.1 = (f32[64,1024]{1,0:T(8,128)S(1)}, f32[32,1024]{1,0:T(8,128)S(1)}) custom-call(f32[1,128,1024]{2,1,0:T(8,128)} %own_ref.1), custom_call_target="tpu_custom_call" | custom-call | flops 4000000000 | bytes 1000000 | tf_op jit(solution)/shard_map/pick_queries/pallas_call | solution.py:46
  1.2 5.1 %collective-permute-start.5 = (f32[32,1024]{1,0:T(8,128)S(1)}, f32[32,1024]{1,0:T(8,128)S(1)}, u32[]{:S(2)}, u32[]{:S(2)}) collective-permute-start(f32[32,1024]{1,0:T(8,128)S(1)} %get-tuple-element.43), channel_id=1, source_target_pairs={{0,12},{1,13},{2,14},{3,15},{4,8},{5,9},{6,10},{7,11},{8,4},{9,5},... | collective-permute-start | bytes 393224 | tf_op jit(solution)/shard_map/ppermute | solution.py:23
  6.3 0.6 %collective-permute-start.3 = (f32[64,1024]{1,0:T(8,128)S(1)}, f32[64,1024]{1,0:T(8,128)S(1)}, u32[]{:S(2)}, u32[]{:S(2)}) collective-permute-start(f32[64,1024]{1,0:T(8,128)S(1)} %get-tuple-element.29.after_ref), channel_id=1, source_target_pairs={{0,4},{1,5},{2,6},{3,7},{4,0},{5,1},{6,2},{7,3},{8,12},{9,13},{10,... | collective-permute-start | bytes 786440 | tf_op jit(solution)/shard_map/ppermute | solution.py:23
  7.0 2.9 %project.1.after_ref.own_ref = f32[64,512]{1,0:T(8,128)S(1)} custom-call(bf16[512,2048]{1,0:T(8,128)(2,1)S(1)} %copy-done.1, bf16[512,7168]{1,0:T(8,128)(2,1)S(1)} %copy-done, bf16[32,2048]{1,0:T(8,128)(2,1)S(1)} %bitcast.4, bf16[32,7168]{1,0:T(8,128)(2,1)S(1)} %bitcast.3, f32[64,1024]{1,0:T(8,128)S(1)} %get-tuple-element.29.after_ref), custom_call_target="tpu_custom_call" | custom-call | tf_op jit(solution)/shard_map/project/pallas_call | solution.py:65
  9.9 0.6 %masks.1 = (bf16[16,512]{1,0:T(8,128)(2,1)S(1)}, f32[8,512]{1,0:T(8,128)S(1)}, f32[16,128]{1,0:T(8,128)S(1)}) custom-call(s32[1,17]{1,0:T(1,128)S(1)} %copy-done.5, f32[64,512]{1,0:T(8,128)S(1)} %project.1.after_ref.own_ref), custom_call_target="tpu_custom_call" | custom-call | flops 2000000000 | bytes 1000000 | tf_op jit(solution)/shard_map/masks/pallas_call | solution.py:94
  10.5 0.8 %collective-permute-done.other_ref = f32[64,512]{1,0:T(8,128)S(1)} collective-permute-done((f32[64,512]{1,0:T(8,128)S(1)}, f32[64,512]{1,0:T(8,128)S(1)}, u32[]{:S(2)}, u32[]{:S(2)}) %collective-permute-start) | collective-permute-done | bytes 131104 | tf_op jit(solution)/shard_map/ppermute | solution.py:23
  11.3 0.3 fisher.1
  11.5 1.5 %collective-permute-start.1 = (f32[32,128]{1,0:T(8,128)S(1)}, f32[32,128]{1,0:T(8,128)S(1)}, u32[]{:S(2)}, u32[]{:S(2)}) collective-permute-start(f32[32,128]{1,0:T(8,128)S(1)} %fisher.1), channel_id=1, source_target_pairs={{0,3},{1,2},{2,1},{3,0},{4,7},{5,6},{6,5},{7,4},{8,11},{9,10},{10,... | collective-permute-start | bytes 49160 | tf_op jit(solution)/shard_map/ppermute | solution.py:23
  13.0 1.0 %examples.1 = f32[16,1024]{1,0:T(8,128)S(1)} custom-call(bf16[16,512]{1,0:T(8,128)(2,1)S(1)} %get-tuple-element.30.member_ref, f32[16,128]{1,0:T(8,128)S(1)} %get-tuple-element.31.count_ref, f32[64,512]{1,0:T(8,128)S(1)} %project.1.after_ref.own_ref, f32[64,512]{1,0:T(8,128)S(1)} %collective-permute-done.other_ref), custom_call_target="tpu_custom_call" | custom-call | flops 2000000000 | bytes 1000000 | tf_op jit(solution)/shard_map/examples/pallas_call | solution.py:154
  14.0 0.8 %collective-permute-done.1 = f32[32,128]{1,0:T(8,128)S(1)} collective-permute-done((f32[32,128]{1,0:T(8,128)S(1)}, f32[32,128]{1,0:T(8,128)S(1)}, u32[]{:S(2)}, u32[]{:S(2)}) %collective-permute-start.1) | collective-permute-done | bytes 16416 | tf_op jit(solution)/shard_map/ppermute | solution.py:23
  14.8 1.7 %collective-permute-start.2 = (f32[1,16,1024]{2,1,0:T(8,128)S(1)}, f32[1,16,1024]{2,1,0:T(8,128)S(1)}, u32[]{:S(2)}, u32[]{:S(2)}) collective-permute-start(f32[1,16,1024]{2,1,0:T(8,128)S(1)} %bitcast.5), channel_id=1, source_target_pairs={{0,3},{1,2},{2,1},{3,0},{4,7},{5,6},{6,5},{7,4},{8,11},{9,10},{10,... | collective-permute-start | bytes 196616 | tf_op jit(solution)/shard_map/ppermute | solution.py:23
  16.5 0.9 %collective-permute-start.6 = (f32[32,128]{1,0:T(8,128)S(1)}, f32[32,128]{1,0:T(8,128)S(1)}, u32[]{:S(2)}, u32[]{:S(2)}) collective-permute-start(f32[32,128]{1,0:T(8,128)S(1)} %add.6), channel_id=1, source_target_pairs={{0,5},{1,4},{2,7},{3,6},{4,1},{5,0},{6,3},{7,2},{8,13},{9,12},{10,... | collective-permute-start | bytes 49160 | tf_op jit(solution)/shard_map/ppermute | solution.py:23
  17.4 2.2 %collective-permute-done.6 = f32[32,128]{1,0:T(8,128)S(1)} collective-permute-done((f32[32,128]{1,0:T(8,128)S(1)}, f32[32,128]{1,0:T(8,128)S(1)}, u32[]{:S(2)}, u32[]{:S(2)}) %collective-permute-start.6) | collective-permute-done | bytes 16416 | tf_op jit(solution)/shard_map/ppermute | solution.py:23
  19.7 1.6 %collective-permute-start.8 = (f32[32,1024]{1,0:T(8,128)S(1)}, f32[32,1024]{1,0:T(8,128)S(1)}, u32[]{:S(2)}, u32[]{:S(2)}) collective-permute-start(f32[32,1024]{1,0:T(8,128)S(1)} %collective-permute-done.4), channel_id=1, source_target_pairs={{0,16},{1,17},{2,18},{3,19},{4,20},{5,21},{6,22},{7,23},{8,24},{9,... | collective-permute-start | bytes 393224 | tf_op jit(solution)/shard_map/ppermute | solution.py:23
  21.2 1.9 %collective-permute-start.7 = (f32[32,128]{1,0:T(8,128)S(1)}, f32[32,128]{1,0:T(8,128)S(1)}, u32[]{:S(2)}, u32[]{:S(2)}) collective-permute-start(f32[32,128]{1,0:T(8,128)S(1)} %add.7.own_ref), channel_id=1, source_target_pairs={{0,9},{1,8},{2,11},{3,10},{4,13},{5,12},{6,15},{7,14},{8,1},{9,0},... | collective-permute-start | bytes 49160 | tf_op jit(solution)/shard_map/ppermute | solution.py:23
  23.1 0.5 %collective-permute-start.9 = (f32[32,1024]{1,0:T(8,128)S(1)}, f32[32,1024]{1,0:T(8,128)S(1)}, u32[]{:S(2)}, u32[]{:S(2)}) collective-permute-start(f32[32,1024]{1,0:T(8,128)S(1)} %collective-permute-done.5), channel_id=1, source_target_pairs={{0,16},{1,17},{2,18},{3,19},{4,20},{5,21},{6,22},{7,23},{8,24},{9,... | collective-permute-start | bytes 393224 | tf_op jit(solution)/shard_map/ppermute | solution.py:23
  23.6 0.6 %arrange_examples.1 = (bf16[128,256]{1,0:T(8,128)(2,1)S(1)}, bf16[128,256]{1,0:T(8,128)(2,1)S(1)}, bf16[128,256]{1,0:T(8,128)(2,1)S(1)}) custom-call(f32[2,16,1024]{2,1,0:T(8,128)S(1)} %pad_maximum_fusion.2.blocks_ref), custom_call_target="tpu_custom_call" | custom-call | tf_op jit(solution)/shard_map/arrange_examples/pallas_call | solution.py:198
  24.2 1.3 %collective-permute-done.7.other_ref = f32[32,128]{1,0:T(8,128)S(1)} collective-permute-done((f32[32,128]{1,0:T(8,128)S(1)}, f32[32,128]{1,0:T(8,128)S(1)}, u32[]{:S(2)}, u32[]{:S(2)}) %collective-permute-start.7) | collective-permute-done | bytes 16416 | tf_op jit(solution)/shard_map/ppermute | solution.py:23
  25.5 1.6 %inverses.1 = (bf16[3,256,256]{2,1,0:T(8,128)(2,1)S(1)}, bf16[3,256,256]{2,1,0:T(8,128)(2,1)S(1)}) custom-call(f32[32,128]{1,0:T(8,128)S(1)} %add.7.own_ref, f32[32,128]{1,0:T(8,128)S(1)} %collective-permute-done.7.other_ref), custom_call_target="tpu_custom_call" | custom-call | tf_op jit(solution)/shard_map/inverses/pallas_call | solution.py:302
  27.1 1.8 %collective-permute-done.9 = f32[32,1024]{1,0:T(8,128)S(1)} collective-permute-done((f32[32,1024]{1,0:T(8,128)S(1)}, f32[32,1024]{1,0:T(8,128)S(1)}, u32[]{:S(2)}, u32[]{:S(2)}) %collective-permute-start.9) | collective-permute-done | bytes 131104 | tf_op jit(solution)/shard_map/ppermute | solution.py:23
  29.0 0.2 split_queries.1
  29.2 1.6 %score.1.kept_ref = f32[32,256]{1,0:T(8,128)S(1)} custom-call(bf16[128,256]{1,0:T(8,128)(2,1)S(1)} %get-tuple-element.40.high_ref, bf16[128,256]{1,0:T(8,128)(2,1)S(1)} %get-tuple-element.41.middle_ref, bf16[128,256]{1,0:T(8,128)(2,1)S(1)} %get-tuple-element.42.low_ref, bf16[3,256,256]{2,1,0:T(8,128)(2,1)S(1)} %get-tuple-element.46.in_ref, ...), custom_call_target="tpu_custom_call" | custom-call | tf_op jit(solution)/shard_map/score/pallas_call | solution.py:341
  30.9 1.2 %collective-permute-done.10.received_ref = f32[32,256]{1,0:T(8,128)S(1)} collective-permute-done((f32[32,256]{1,0:T(8,128)S(1)}, f32[32,256]{1,0:T(8,128)S(1)}, u32[]{:S(2)}, u32[]{:S(2)}) %collective-permute-start.10) | collective-permute-done | bytes 32800 | tf_op jit(solution)/shard_map/ppermute | solution.py:23
  32.1 0.7 %place.1 = f32[32,512]{1,0:T(8,128)} custom-call(f32[32,256]{1,0:T(8,128)S(1)} %score.1.kept_ref, f32[32,256]{1,0:T(8,128)S(1)} %collective-permute-done.10.received_ref), custom_call_target="tpu_custom_call" | custom-call | tf_op jit(solution)/shard_map/place/pallas_call | solution.py:364
  (25 shorter events, 0.2 us)
Async XLA Ops:
  0.0 7.0 %copy-start.3 = (bf16[7168,32]{0,1:T(8,128)(2,1)S(1)}, bf16[7168,32]{0,1:T(8,128)(2,1)}, u32[]{:S(2)}) copy-start(bf16[7168,32]{0,1:T(8,128)(2,1)} %param.9) | copy-start | bytes 1376260
  0.0 7.0 %copy-start.4 = (bf16[2048,32]{0,1:T(8,128)(2,1)S(1)}, bf16[2048,32]{0,1:T(8,128)(2,1)}, u32[]{:S(2)}) copy-start(bf16[2048,32]{0,1:T(8,128)(2,1)} %param.8) | copy-start | bytes 393220
  0.0 7.0 %copy-start = (bf16[512,7168]{1,0:T(8,128)(2,1)S(1)}, bf16[512,7168]{1,0:T(8,128)(2,1)}, u32[]{:S(2)}) copy-start(bf16[512,7168]{1,0:T(8,128)(2,1)} %g_ref.1) | copy-start | bytes 22020100
  0.0 7.0 %copy-start.1 = (bf16[512,2048]{1,0:T(8,128)(2,1)S(1)}, bf16[512,2048]{1,0:T(8,128)(2,1)}, u32[]{:S(2)}) copy-start(bf16[512,2048]{1,0:T(8,128)(2,1)} %a_ref.1) | copy-start | bytes 6291460
  1.2 8.8 %copy-start.5 = (s32[1,17]{1,0:T(1,128)S(1)}, s32[1,17]{1,0:T(1,128)}, u32[]{:S(2)}) copy-start(s32[1,17]{1,0:T(1,128)} %lengths_ref.1) | copy-start | bytes 208
  1.2 18.5 %collective-permute-start.5 = (f32[32,1024]{1,0:T(8,128)S(1)}, f32[32,1024]{1,0:T(8,128)S(1)}, u32[]{:S(2)}, u32[]{:S(2)}) collective-permute-start(f32[32,1024]{1,0:T(8,128)S(1)} %get-tuple-element.43), channel_id=1, source_target_pairs={{0,12},{1,13},{2,14},{3,15},{4,8},{5,9},{6,10},{7,11},{8,4},{9,5},... | collective-permute-start | bytes 393224 | tf_op jit(solution)/shard_map/ppermute | solution.py:23
  6.3 13.3 %collective-permute-start.4 = (f32[32,1024]{1,0:T(8,128)S(1)}, f32[32,1024]{1,0:T(8,128)S(1)}, u32[]{:S(2)}, u32[]{:S(2)}) collective-permute-start(f32[32,1024]{1,0:T(8,128)S(1)} %get-tuple-element.43), channel_id=1, source_target_pairs={{0,8},{1,9},{2,10},{3,11},{4,12},{5,13},{6,14},{7,15},{8,0},{9,1},... | collective-permute-start | bytes 393224 | tf_op jit(solution)/shard_map/ppermute | solution.py:23
  6.3 13.3 %collective-permute-start.3 = (f32[64,1024]{1,0:T(8,128)S(1)}, f32[64,1024]{1,0:T(8,128)S(1)}, u32[]{:S(2)}, u32[]{:S(2)}) collective-permute-start(f32[64,1024]{1,0:T(8,128)S(1)} %get-tuple-element.29.after_ref), channel_id=1, source_target_pairs={{0,4},{1,5},{2,6},{3,7},{4,0},{5,1},{6,2},{7,3},{8,12},{9,13},{10,... | collective-permute-start | bytes 786440 | tf_op jit(solution)/shard_map/ppermute | solution.py:23
  9.8 19.1 %copy-start.2 = (f32[1,128,1024]{2,1,0:T(8,128)S(1)}, f32[1,128,1024]{2,1,0:T(8,128)}, u32[]{:S(2)}) copy-start(f32[1,128,1024]{2,1,0:T(8,128)} %own_ref.1) | copy-start | bytes 1572868
  9.9 1.4 %collective-permute-start = (f32[64,512]{1,0:T(8,128)S(1)}, f32[64,512]{1,0:T(8,128)S(1)}, u32[]{:S(2)}, u32[]{:S(2)}) collective-permute-start(f32[64,512]{1,0:T(8,128)S(1)} %project.1.after_ref.own_ref), channel_id=1, source_target_pairs={{0,1},{1,0},{2,3},{3,2},{4,5},{5,4},{6,7},{7,6},{8,9},{9,8},{10,11... | collective-permute-start | bytes 393224 | tf_op jit(solution)/shard_map/ppermute | solution.py:23
  11.5 3.2 %collective-permute-start.1 = (f32[32,128]{1,0:T(8,128)S(1)}, f32[32,128]{1,0:T(8,128)S(1)}, u32[]{:S(2)}, u32[]{:S(2)}) collective-permute-start(f32[32,128]{1,0:T(8,128)S(1)} %fisher.1), channel_id=1, source_target_pairs={{0,3},{1,2},{2,1},{3,0},{4,7},{5,6},{6,5},{7,4},{8,11},{9,10},{10,... | collective-permute-start | bytes 49160 | tf_op jit(solution)/shard_map/ppermute | solution.py:23
  14.8 8.8 %collective-permute-start.2 = (f32[1,16,1024]{2,1,0:T(8,128)S(1)}, f32[1,16,1024]{2,1,0:T(8,128)S(1)}, u32[]{:S(2)}, u32[]{:S(2)}) collective-permute-start(f32[1,16,1024]{2,1,0:T(8,128)S(1)} %bitcast.5), channel_id=1, source_target_pairs={{0,3},{1,2},{2,1},{3,0},{4,7},{5,6},{6,5},{7,4},{8,11},{9,10},{10,... | collective-permute-start | bytes 196616 | tf_op jit(solution)/shard_map/ppermute | solution.py:23
  16.5 3.2 %collective-permute-start.6 = (f32[32,128]{1,0:T(8,128)S(1)}, f32[32,128]{1,0:T(8,128)S(1)}, u32[]{:S(2)}, u32[]{:S(2)}) collective-permute-start(f32[32,128]{1,0:T(8,128)S(1)} %add.6), channel_id=1, source_target_pairs={{0,5},{1,4},{2,7},{3,6},{4,1},{5,0},{6,3},{7,2},{8,13},{9,12},{10,... | collective-permute-start | bytes 49160 | tf_op jit(solution)/shard_map/ppermute | solution.py:23
  19.7 7.5 %collective-permute-start.8 = (f32[32,1024]{1,0:T(8,128)S(1)}, f32[32,1024]{1,0:T(8,128)S(1)}, u32[]{:S(2)}, u32[]{:S(2)}) collective-permute-start(f32[32,1024]{1,0:T(8,128)S(1)} %collective-permute-done.4), channel_id=1, source_target_pairs={{0,16},{1,17},{2,18},{3,19},{4,20},{5,21},{6,22},{7,23},{8,24},{9,... | collective-permute-start | bytes 393224 | tf_op jit(solution)/shard_map/ppermute | solution.py:23
  21.2 4.2 %collective-permute-start.7 = (f32[32,128]{1,0:T(8,128)S(1)}, f32[32,128]{1,0:T(8,128)S(1)}, u32[]{:S(2)}, u32[]{:S(2)}) collective-permute-start(f32[32,128]{1,0:T(8,128)S(1)} %add.7.own_ref), channel_id=1, source_target_pairs={{0,9},{1,8},{2,11},{3,10},{4,13},{5,12},{6,15},{7,14},{8,1},{9,0},... | collective-permute-start | bytes 49160 | tf_op jit(solution)/shard_map/ppermute | solution.py:23
  23.1 5.8 %collective-permute-start.9 = (f32[32,1024]{1,0:T(8,128)S(1)}, f32[32,1024]{1,0:T(8,128)S(1)}, u32[]{:S(2)}, u32[]{:S(2)}) collective-permute-start(f32[32,1024]{1,0:T(8,128)S(1)} %collective-permute-done.5), channel_id=1, source_target_pairs={{0,16},{1,17},{2,18},{3,19},{4,20},{5,21},{6,22},{7,23},{8,24},{9,... | collective-permute-start | bytes 393224 | tf_op jit(solution)/shard_map/ppermute | solution.py:23
  30.8 1.3 %collective-permute-start.10 = (f32[32,256]{1,0:T(8,128)S(1)}, f32[32,256]{1,0:T(8,128)S(1)}, u32[]{:S(2)}, u32[]{:S(2)}) collective-permute-start(f32[32,256]{1,0:T(8,128)S(1)} %score.1.kept_ref), channel_id=1, source_target_pairs={{0,1},{1,0},{2,3},{3,2},{4,5},{5,4},{6,7},{7,6},{8,9},{9,8},{10,11... | collective-permute-start | bytes 98312 | tf_op jit(solution)/shard_map/ppermute | solution.py:23

commit v4 on v3

--- a/solution.py
+++ b/solution.py
@@ -318,35 +318,52 @@
     return by_high[0:rows] + (by_high[rows : 2 * rows] + by_middle[0:rows] + small)
 
 
-def score_kernel(high_ref, middle_ref, low_ref, in_ref, out_ref, q_high_ref, q_low_ref, scores_ref, scratch):
+def condition_kernel(high_ref, middle_ref, low_ref, in_ref, out_ref, both_ref, scratch):
     columns, count = scratch.shape
-    width = math.isqrt(columns)
     left = times_blocks(high_ref[...], middle_ref[...], low_ref[...], out_ref)
-    turned = turn_pairs(lambda c: left[c * count : (c + 1) * count], scratch, width)
+    turned = turn_pairs(lambda c: left[c * count : (c + 1) * count], scratch, math.isqrt(columns))
     high, low = split2(times_blocks(*split3(turned), in_ref))
+    for c in range(columns // CHUNK):
+        both_ref[c, 0:count] = high[c * count : (c + 1) * count]
+        both_ref[c, count:] = low[c * count : (c + 1) * count]
+
+
+def condition(pieces, in_blocks, out_blocks, columns):
+    count = pieces[0].shape[0] * CHUNK // columns
+    return pl.pallas_call(
+        condition_kernel,
+        out_shape=jax.ShapeDtypeStruct((columns // CHUNK, 2 * count, CHUNK), BF16),
+        in_specs=[pl.BlockSpec(memory_space=pltpu.VMEM)] * 5,
+        out_specs=pl.BlockSpec(memory_space=pltpu.VMEM),
+        scratch_shapes=[pltpu.VMEM((columns, count), F32)],
+        compiler_params=pltpu.CompilerParams(vmem_limit_bytes=8 * MIB),
+        cost_estimate=pl.CostEstimate(flops=2 * 10**9, bytes_accessed=10**6, transcendentals=0),
+        name="condition",
+    )(*pieces, in_blocks, out_blocks)
+
+
+def score_kernel(both_ref, q_high_ref, q_low_ref, scores_ref):
+    chunks, count = both_ref.shape[0], both_ref.shape[1] // 2
     total = None
-    for c in range(columns // CHUNK):
-        at, cols = slice(c * count, (c + 1) * count), slice(c * CHUNK, (c + 1) * CHUNK)
-        both = jnp.concatenate([high[at], low[at]], axis=0)
-        by_high = lax.dot_general(both, q_high_ref[:, cols], NT, preferred_element_type=F32)
-        by_low = lax.dot_general(high[at], q_low_ref[:, cols], NT, preferred_element_type=F32)
+    for c in range(chunks):
+        cols = slice(c * CHUNK, (c + 1) * CHUNK)
+        by_high = lax.dot_general(both_ref[c], q_high_ref[:, cols], NT, preferred_element_type=F32)
+        by_low = lax.dot_general(both_ref[c, 0:count], q_low_ref[:, cols], NT, preferred_element_type=F32)
         part = by_high[0:count] + (by_high[count:] + by_low)
         total = part if total is None else total + part
-    scores_ref[...] = total * (1.0 / width)
-
-
-def score(pieces, in_blocks, out_blocks, high, low):
-    rows, columns = high.shape
-    count = pieces[0].shape[0] * CHUNK // columns
+    scores_ref[...] = total * (1.0 / math.isqrt(chunks * CHUNK))
+
+
+def score(both, high, low):
+    rows = high.shape[0]
     return pl.pallas_call(
         score_kernel,
-        out_shape=jax.ShapeDtypeStruct((count, rows), F32),
-        in_specs=[pl.BlockSpec(memory_space=pltpu.VMEM)] * 7,
-        out_specs=pl.BlockSpec(memory_space=pltpu.VMEM),
-        scratch_shapes=[pltpu.VMEM((columns, count), F32)],
+        out_shape=jax.ShapeDtypeStruct((both.shape[1] // 2, rows), F32),
+        in_specs=[pl.BlockSpec(memory_space=pltpu.VMEM)] * 3,
+        out_specs=pl.BlockSpec(memory_space=pltpu.VMEM),
         compiler_params=pltpu.CompilerParams(vmem_limit_bytes=(6 + rows // 128) * MIB),
         name="score",
-    )(*pieces, in_blocks, out_blocks, high, low)
+    )(both, high, low)
 
 
 def place_kernel(half, kept_ref, received_ref, out_ref):
@@ -371,9 +388,25 @@
     )(kept, received)
 
 
+def hold_kernel(value_ref, after_ref, out_ref):
+    out_ref[...] = value_ref[...]
+
+
+def hold(value, after):
+    return pl.pallas_call(
+        hold_kernel,
+        out_shape=jax.ShapeDtypeStruct(value.shape, value.dtype),
+        in_specs=[pl.BlockSpec(memory_space=pltpu.VMEM), pl.BlockSpec(memory_space=pl.ANY)],
+        out_specs=pl.BlockSpec(memory_space=pltpu.VMEM),
+        compiler_params=pltpu.CompilerParams(vmem_limit_bytes=4 * MIB),
+        cost_estimate=pl.CostEstimate(flops=10**9, bytes_accessed=10**6, transcendentals=0),
+        name="hold",
+    )(value, after)
+
+
 ORDER = "x12"
 E_STAGE = 1
-Y_STAGE = 2
+Y_STAGES = (1, 2)
 
 
 def body(mesh, activations, out_grads, proj_in, proj_out, lengths, queries):
@@ -401,24 +434,27 @@
     def beside(stage, factor, blocks, fetched):
         i = stage - E_STAGE
         if 0 <= i < len(query_bits):
-            blocks, factor = lax.optimization_barrier((blocks, factor))
+            blocks = hold(blocks, factor)
             blocks = jnp.concatenate([blocks, swap(blocks, mesh, query_bits[i] | core_bit)], axis=0)
-        if stage == Y_STAGE:
-            fetched, factor = lax.optimization_barrier((fetched, factor))
-            for bit in group_bits:
-                fetched = fetched[:1] + [jnp.concatenate([p, swap(p, mesh, bit)], axis=0) for p in fetched[1:]]
-        return factor, blocks, fetched
+        if stage in Y_STAGES:
+            first, end = ((1, 2), (2, n_dp - 1))[Y_STAGES.index(stage)]
+            for r in range(first, end):
+                fetched[r] = hold(fetched[r], factor)
+                for bit in group_bits:
+                    fetched[r] = jnp.concatenate([fetched[r], swap(fetched[r], mesh, bit)], axis=0)
+        return blocks
 
     for step, mask in enumerate(steps):
-        factor, blocks, fetched = beside(step, factor, blocks, fetched)
+        blocks = beside(step, factor, blocks, fetched)
         received = swap(factor, mesh, mask)
         if step < len(steps) - 1:
             factor = factor + received
-    in_blocks, out_blocks = inverses(factor, received)
-
     arranged = arrange_examples(blocks, n_query)
+    arranged, received = lax.optimization_barrier((arranged, received))
+    both = condition(arranged, *inverses(factor, received), queries.shape[2])
+
     high, low = split_queries(groups, queries, fetched)
-    scores = score(arranged, in_blocks, out_blocks, high, low)
+    scores = score(both, high, low)
     return place(queries.shape[1] // 2, scores, swap(scores, mesh, core_bit))
 
 

time: 32.9 us -> 29.4 us (0.89)
  waiting for transfers between devices: 8.1 us -> 3.62 us
  starting transfers between devices: 13.9 us -> 15 us
    ppermute x11, waiting for transfers between devices: 8.1 us -> 3.62 us  [swap(): return lax.ppermute(value, AXES, [(i, i ^ mask) for i in range(count)])]
    ppermute x11, starting transfers between devices: 13.9 us -> 15 us  [swap(): return lax.ppermute(value, AXES, [(i, i ^ mask) for i in range(count)])]
    pallas_call x1 -> x5, Pallas kernels: 1.64 us -> 1.57 us  [the longest x1 1.16 us: condition(): pl.pallas_call(condition_kernel, out_shape=jax.ShapeDtypeStruct((columns...]
  transfers between devices with their start and end apart: 11 -> 11, of which waited for: 6 -> 5; matrix products, arithmetic and copies ran while one was open for 0% -> 0% of each run, Pallas kernels for 21% -> 27%
where the time goes in v4:
time: 29.4 us; the launch traced here: 29.3 us
  starting transfers between devices  15 us (51%)
  Pallas kernels  10.5 us (36%)
  waiting for transfers between devices  3.62 us (12%)
    ppermute x11, starting transfers between devices, swap(): return lax.ppermute(value, AXES, [(i, i ^ mask) for i in range(count)])  15 us
    ppermute x11, waiting for transfers between devices, swap(): return lax.ppermute(value, AXES, [(i, i ^ mask) for i in range(count)])  3.62 us
    pallas_call x1, Pallas kernels, project(): pl.pallas_call(project_kernel, out_shape=jax.ShapeDtypeStruct((2 * proj_i...  2.88 us
    pallas_call x1, Pallas kernels, inverses(): pl.pallas_call(inverses_kernel, out_shape=(shape, shape), in_specs=[pl.Bl...  1.63 us
    pallas_call x1, Pallas kernels, condition(): pl.pallas_call(condition_kernel, out_shape=jax.ShapeDtypeStruct((columns...  1.16 us
    pallas_call x1, Pallas kernels, pick_queries(): pl.pallas_call(functools.partial(pick_kernel, groups), out_shape=tuple((j...  1.15 us
    pallas_call x1, Pallas kernels, example_grads(): pl.pallas_call(examples_kernel, out_shape=jax.ShapeDtypeStruct((member.sh...  0.96 us
    pallas_call x1, Pallas kernels, place(): pl.pallas_call(functools.partial(place_kernel, half), out_shape=jax.Shape...  0.72 us
  transfers between devices with their start and end apart: 11, of which 5 were waited for; matrix products, arithmetic and copies ran while one was open for 0% of the time, Pallas kernels for 27%

profile of v4, /device:TPU:0, one launch (start us, length us, event | category | flops | bytes accessed | tf_op | source)
XLA Modules:
  0.0 29.3 jit_solution(12830584969586543193)
XLA Ops:
  0.0 1.2 %pick_queries.1 = (f32[64,1024]{1,0:T(8,128)S(1)}, f32[32,1024]{1,0:T(8,128)S(1)}) custom-call(f32[1,128,1024]{2,1,0:T(8,128)} %own_ref.1), custom_call_target="tpu_custom_call" | custom-call | flops 4000000000 | bytes 1000000 | tf_op jit(solution)/shard_map/pick_queries/pallas_call | solution.py:46
  1.2 4.1 %collective-permute-start.6 = (f32[32,1024]{1,0:T(8,128)S(1)}, f32[32,1024]{1,0:T(8,128)S(1)}, u32[]{:S(2)}, u32[]{:S(2)}) collective-permute-start(f32[32,1024]{1,0:T(8,128)S(1)} %get-tuple-element.46), channel_id=1, source_target_pairs={{0,8},{1,9},{2,10},{3,11},{4,12},{5,13},{6,14},{7,15},{8,0},{9,1},... | collective-permute-start | bytes 393224 | tf_op jit(solution)/shard_map/ppermute | solution.py:23
  5.3 1.3 %collective-permute-start.8 = (f32[32,1024]{1,0:T(8,128)S(1)}, f32[32,1024]{1,0:T(8,128)S(1)}, u32[]{:S(2)}, u32[]{:S(2)}) collective-permute-start(f32[32,1024]{1,0:T(8,128)S(1)} %get-tuple-element.46), channel_id=1, source_target_pairs={{0,12},{1,13},{2,14},{3,15},{4,8},{5,9},{6,10},{7,11},{8,4},{9,5},... | collective-permute-start | bytes 393224 | tf_op jit(solution)/shard_map/ppermute | solution.py:23
  6.7 0.2 collective-permute-start.5
  6.9 2.9 %project.1.after_ref.own_ref = f32[64,512]{1,0:T(8,128)S(1)} custom-call(bf16[512,2048]{1,0:T(8,128)(2,1)S(1)} %copy-done.1, bf16[512,7168]{1,0:T(8,128)(2,1)S(1)} %copy-done, bf16[32,2048]{1,0:T(8,128)(2,1)S(1)} %bitcast.4, bf16[32,7168]{1,0:T(8,128)(2,1)S(1)} %bitcast.3, f32[64,1024]{1,0:T(8,128)S(1)} %get-tuple-element.27.after_ref), custom_call_target="tpu_custom_call" | custom-call | tf_op jit(solution)/shard_map/project/pallas_call | solution.py:65
  9.8 0.6 %masks.1 = (bf16[16,512]{1,0:T(8,128)(2,1)S(1)}, f32[8,512]{1,0:T(8,128)S(1)}, f32[16,128]{1,0:T(8,128)S(1)}) custom-call(s32[1,17]{1,0:T(1,128)S(1)} %copy-done.5, f32[64,512]{1,0:T(8,128)S(1)} %project.1.after_ref.own_ref), custom_call_target="tpu_custom_call" | custom-call | flops 2000000000 | bytes 1000000 | tf_op jit(solution)/shard_map/masks/pallas_call | solution.py:94
  10.4 0.8 %collective-permute-done.other_ref = f32[64,512]{1,0:T(8,128)S(1)} collective-permute-done((f32[64,512]{1,0:T(8,128)S(1)}, f32[64,512]{1,0:T(8,128)S(1)}, u32[]{:S(2)}, u32[]{:S(2)}) %collective-permute-start) | collective-permute-done | bytes 131104 | tf_op jit(solution)/shard_map/ppermute | solution.py:23
  11.1 0.3 fisher.1
  11.4 1.3 %collective-permute-start.1 = (f32[32,128]{1,0:T(8,128)S(1)}, f32[32,128]{1,0:T(8,128)S(1)}, u32[]{:S(2)}, u32[]{:S(2)}) collective-permute-start(f32[32,128]{1,0:T(8,128)S(1)} %fisher.1), channel_id=1, source_target_pairs={{0,3},{1,2},{2,1},{3,0},{4,7},{5,6},{6,5},{7,4},{8,11},{9,10},{10,... | collective-permute-start | bytes 49160 | tf_op jit(solution)/shard_map/ppermute | solution.py:23
  12.7 1.0 %examples.1 = f32[16,1024]{1,0:T(8,128)S(1)} custom-call(bf16[16,512]{1,0:T(8,128)(2,1)S(1)} %get-tuple-element.28.member_ref, f32[16,128]{1,0:T(8,128)S(1)} %get-tuple-element.29.count_ref, f32[64,512]{1,0:T(8,128)S(1)} %project.1.after_ref.own_ref, f32[64,512]{1,0:T(8,128)S(1)} %collective-permute-done.other_ref), custom_call_target="tpu_custom_call" | custom-call | flops 2000000000 | bytes 1000000 | tf_op jit(solution)/shard_map/examples/pallas_call | solution.py:154
  13.7 1.0 %collective-permute-done.1 = f32[32,128]{1,0:T(8,128)S(1)} collective-permute-done((f32[32,128]{1,0:T(8,128)S(1)}, f32[32,128]{1,0:T(8,128)S(1)}, u32[]{:S(2)}, u32[]{:S(2)}) %collective-permute-start.1) | collective-permute-done | bytes 16416 | tf_op jit(solution)/shard_map/ppermute | solution.py:23
  14.6 1.8 %collective-permute-start.3 = (f32[32,128]{1,0:T(8,128)S(1)}, f32[32,128]{1,0:T(8,128)S(1)}, u32[]{:S(2)}, u32[]{:S(2)}) collective-permute-start(f32[32,128]{1,0:T(8,128)S(1)} %add.6.after_ref), channel_id=1, source_target_pairs={{0,5},{1,4},{2,7},{3,6},{4,1},{5,0},{6,3},{7,2},{8,13},{9,12},{10,... | collective-permute-start | bytes 49160 | tf_op jit(solution)/shard_map/ppermute | solution.py:23
  16.5 1.2 %collective-permute-start.2 = (f32[1,16,1024]{2,1,0:T(8,128)S(1)}, f32[1,16,1024]{2,1,0:T(8,128)S(1)}, u32[]{:S(2)}, u32[]{:S(2)}) collective-permute-start(f32[1,16,1024]{2,1,0:T(8,128)S(1)} %hold.3), channel_id=1, source_target_pairs={{0,3},{1,2},{2,1},{3,0},{4,7},{5,6},{6,5},{7,4},{8,11},{9,10},{10,... | collective-permute-start | bytes 196616 | tf_op jit(solution)/shard_map/ppermute | solution.py:23
  17.7 1.6 %collective-permute-start.7 = (f32[32,1024]{1,0:T(8,128)S(1)}, f32[32,1024]{1,0:T(8,128)S(1)}, u32[]{:S(2)}, u32[]{:S(2)}) collective-permute-start(f32[32,1024]{1,0:T(8,128)S(1)} %hold.4), channel_id=1, source_target_pairs={{0,16},{1,17},{2,18},{3,19},{4,20},{5,21},{6,22},{7,23},{8,24},{9,... | collective-permute-start | bytes 393224 | tf_op jit(solution)/shard_map/ppermute | solution.py:23
  19.3 1.6 %collective-permute-start.4 = (f32[32,128]{1,0:T(8,128)S(1)}, f32[32,128]{1,0:T(8,128)S(1)}, u32[]{:S(2)}, u32[]{:S(2)}) collective-permute-start(f32[32,128]{1,0:T(8,128)S(1)} %add.7.own_ref.after_ref), channel_id=1, source_target_pairs={{0,9},{1,8},{2,11},{3,10},{4,13},{5,12},{6,15},{7,14},{8,1},{9,0},... | collective-permute-start | bytes 49160 | tf_op jit(solution)/shard_map/ppermute | solution.py:23
  21.0 1.6 %collective-permute-start.9 = (f32[32,1024]{1,0:T(8,128)S(1)}, f32[32,1024]{1,0:T(8,128)S(1)}, u32[]{:S(2)}, u32[]{:S(2)}) collective-permute-start(f32[32,1024]{1,0:T(8,128)S(1)} %hold.5), channel_id=1, source_target_pairs={{0,16},{1,17},{2,18},{3,19},{4,20},{5,21},{6,22},{7,23},{8,24},{9,... | collective-permute-start | bytes 393224 | tf_op jit(solution)/shard_map/ppermute | solution.py:23
  22.6 0.6 %arrange_examples.1 = (bf16[128,256]{1,0:T(8,128)(2,1)S(1)}, bf16[128,256]{1,0:T(8,128)(2,1)S(1)}, bf16[128,256]{1,0:T(8,128)(2,1)S(1)}) custom-call(f32[2,16,1024]{2,1,0:T(8,128)S(1)} %pad_maximum_fusion.2.blocks_ref), custom_call_target="tpu_custom_call" | custom-call | tf_op jit(solution)/shard_map/arrange_examples/pallas_call | solution.py:198
  23.2 0.3 %collective-permute-done.4.other_ref = f32[32,128]{1,0:T(8,128)S(1)} collective-permute-done((f32[32,128]{1,0:T(8,128)S(1)}, f32[32,128]{1,0:T(8,128)S(1)}, u32[]{:S(2)}, u32[]{:S(2)}) %collective-permute-start.4) | collective-permute-done | bytes 16416 | tf_op jit(solution)/shard_map/ppermute | solution.py:23
  23.5 1.6 %inverses.1 = (bf16[3,256,256]{2,1,0:T(8,128)(2,1)S(1)}, bf16[3,256,256]{2,1,0:T(8,128)(2,1)S(1)}) custom-call(f32[32,128]{1,0:T(8,128)S(1)} %add.7.own_ref.after_ref, f32[32,128]{1,0:T(8,128)S(1)} %collective-permute-done.4.other_ref), custom_call_target="tpu_custom_call" | custom-call | tf_op jit(solution)/shard_map/inverses/pallas_call | solution.py:302
  25.1 1.2 %condition.1.both_ref = bf16[4,64,256]{2,1,0:T(8,128)(2,1)S(1)} custom-call(bf16[128,256]{1,0:T(8,128)(2,1)S(1)} %get-tuple-element.40.high_ref, bf16[128,256]{1,0:T(8,128)(2,1)S(1)} %get-tuple-element.41.middle_ref, bf16[128,256]{1,0:T(8,128)(2,1)S(1)} %get-tuple-element.42.low_ref, bf16[3,256,256]{2,1,0:T(8,128)(2,1)S(1)} %get-tuple-element.44.in_ref, ...), custom_call_target="tpu_custom_call" | custom-call | flops 2000000000 | bytes 1000000 | tf_op jit(solution)/shard_map/condition/pallas_call | solution.py:333
  26.3 0.4 %collective-permute-done.9 = f32[32,1024]{1,0:T(8,128)S(1)} collective-permute-done((f32[32,1024]{1,0:T(8,128)S(1)}, f32[32,1024]{1,0:T(8,128)S(1)}, u32[]{:S(2)}, u32[]{:S(2)}) %collective-permute-start.9) | collective-permute-done | bytes 131104 | tf_op jit(solution)/shard_map/ppermute | solution.py:23
  26.9 0.4 %score.1.kept_ref = f32[32,256]{1,0:T(8,128)S(1)} custom-call(bf16[4,64,256]{2,1,0:T(8,128)(2,1)S(1)} %condition.1.both_ref, bf16[256,1024]{1,0:T(8,128)(2,1)S(1)} %get-tuple-element.47.q_high_ref, bf16[256,1024]{1,0:T(8,128)(2,1)S(1)} %get-tuple-element.48.q_low_ref), custom_call_target="tpu_custom_call" | custom-call | tf_op jit(solution)/shard_map/score/pallas_call | solution.py:359
  27.4 1.2 %collective-permute-done.10.received_ref = f32[32,256]{1,0:T(8,128)S(1)} collective-permute-done((f32[32,256]{1,0:T(8,128)S(1)}, f32[32,256]{1,0:T(8,128)S(1)}, u32[]{:S(2)}, u32[]{:S(2)}) %collective-permute-start.10) | collective-permute-done | bytes 32800 | tf_op jit(solution)/shard_map/ppermute | solution.py:23
  28.6 0.7 %place.1 = f32[32,512]{1,0:T(8,128)} custom-call(f32[32,256]{1,0:T(8,128)S(1)} %score.1.kept_ref, f32[32,256]{1,0:T(8,128)S(1)} %collective-permute-done.10.received_ref), custom_call_target="tpu_custom_call" | custom-call | tf_op jit(solution)/shard_map/place/pallas_call | solution.py:381
  (29 shorter events, 0.4 us)
Async XLA Ops:
  0.0 6.9 %copy-start.1 = (bf16[512,2048]{1,0:T(8,128)(2,1)S(1)}, bf16[512,2048]{1,0:T(8,128)(2,1)}, u32[]{:S(2)}) copy-start(bf16[512,2048]{1,0:T(8,128)(2,1)} %a_ref.1) | copy-start | bytes 6291460
  0.0 6.9 %copy-start = (bf16[512,7168]{1,0:T(8,128)(2,1)S(1)}, bf16[512,7168]{1,0:T(8,128)(2,1)}, u32[]{:S(2)}) copy-start(bf16[512,7168]{1,0:T(8,128)(2,1)} %g_ref.1) | copy-start | bytes 22020100
  0.0 6.9 %copy-start.4 = (bf16[2048,32]{0,1:T(8,128)(2,1)S(1)}, bf16[2048,32]{0,1:T(8,128)(2,1)}, u32[]{:S(2)}) copy-start(bf16[2048,32]{0,1:T(8,128)(2,1)} %param.8) | copy-start | bytes 393220
  0.0 6.9 %copy-start.3 = (bf16[7168,32]{0,1:T(8,128)(2,1)S(1)}, bf16[7168,32]{0,1:T(8,128)(2,1)}, u32[]{:S(2)}) copy-start(bf16[7168,32]{0,1:T(8,128)(2,1)} %param.9) | copy-start | bytes 1376260
  1.2 8.6 %copy-start.5 = (s32[1,17]{1,0:T(1,128)S(1)}, s32[1,17]{1,0:T(1,128)}, u32[]{:S(2)}) copy-start(s32[1,17]{1,0:T(1,128)} %lengths_ref.1) | copy-start | bytes 208
  1.2 16.5 %collective-permute-start.6 = (f32[32,1024]{1,0:T(8,128)S(1)}, f32[32,1024]{1,0:T(8,128)S(1)}, u32[]{:S(2)}, u32[]{:S(2)}) collective-permute-start(f32[32,1024]{1,0:T(8,128)S(1)} %get-tuple-element.46), channel_id=1, source_target_pairs={{0,8},{1,9},{2,10},{3,11},{4,12},{5,13},{6,14},{7,15},{8,0},{9,1},... | collective-permute-start | bytes 393224 | tf_op jit(solution)/shard_map/ppermute | solution.py:23
  5.3 15.7 %collective-permute-start.8 = (f32[32,1024]{1,0:T(8,128)S(1)}, f32[32,1024]{1,0:T(8,128)S(1)}, u32[]{:S(2)}, u32[]{:S(2)}) collective-permute-start(f32[32,1024]{1,0:T(8,128)S(1)} %get-tuple-element.46), channel_id=1, source_target_pairs={{0,12},{1,13},{2,14},{3,15},{4,8},{5,9},{6,10},{7,11},{8,4},{9,5},... | collective-permute-start | bytes 393224 | tf_op jit(solution)/shard_map/ppermute | solution.py:23
  6.7 20.1 %collective-permute-start.5 = (f32[64,1024]{1,0:T(8,128)S(1)}, f32[64,1024]{1,0:T(8,128)S(1)}, u32[]{:S(2)}, u32[]{:S(2)}) collective-permute-start(f32[64,1024]{1,0:T(8,128)S(1)} %get-tuple-element.27.after_ref), channel_id=1, source_target_pairs={{0,4},{1,5},{2,6},{3,7},{4,0},{5,1},{6,2},{7,3},{8,12},{9,13},{10,... | collective-permute-start | bytes 786440 | tf_op jit(solution)/shard_map/ppermute | solution.py:23
  9.8 1.4 %collective-permute-start = (f32[64,512]{1,0:T(8,128)S(1)}, f32[64,512]{1,0:T(8,128)S(1)}, u32[]{:S(2)}, u32[]{:S(2)}) collective-permute-start(f32[64,512]{1,0:T(8,128)S(1)} %project.1.after_ref.own_ref), channel_id=1, source_target_pairs={{0,1},{1,0},{2,3},{3,2},{4,5},{5,4},{6,7},{7,6},{8,9},{9,8},{10,11... | collective-permute-start | bytes 393224 | tf_op jit(solution)/shard_map/ppermute | solution.py:23
  11.4 3.2 %collective-permute-start.1 = (f32[32,128]{1,0:T(8,128)S(1)}, f32[32,128]{1,0:T(8,128)S(1)}, u32[]{:S(2)}, u32[]{:S(2)}) collective-permute-start(f32[32,128]{1,0:T(8,128)S(1)} %fisher.1), channel_id=1, source_target_pairs={{0,3},{1,2},{2,1},{3,0},{4,7},{5,6},{6,5},{7,4},{8,11},{9,10},{10,... | collective-permute-start | bytes 49160 | tf_op jit(solution)/shard_map/ppermute | solution.py:23
  14.6 4.7 %collective-permute-start.3 = (f32[32,128]{1,0:T(8,128)S(1)}, f32[32,128]{1,0:T(8,128)S(1)}, u32[]{:S(2)}, u32[]{:S(2)}) collective-permute-start(f32[32,128]{1,0:T(8,128)S(1)} %add.6.after_ref), channel_id=1, source_target_pairs={{0,5},{1,4},{2,7},{3,6},{4,1},{5,0},{6,3},{7,2},{8,13},{9,12},{10,... | collective-permute-start | bytes 49160 | tf_op jit(solution)/shard_map/ppermute | solution.py:23
  16.5 10.2 %copy-start.2 = (f32[1,128,1024]{2,1,0:T(8,128)S(1)}, f32[1,128,1024]{2,1,0:T(8,128)}, u32[]{:S(2)}) copy-start(f32[1,128,1024]{2,1,0:T(8,128)} %own_ref.1) | copy-start | bytes 1572868
  16.5 6.1 %collective-permute-start.2 = (f32[1,16,1024]{2,1,0:T(8,128)S(1)}, f32[1,16,1024]{2,1,0:T(8,128)S(1)}, u32[]{:S(2)}, u32[]{:S(2)}) collective-permute-start(f32[1,16,1024]{2,1,0:T(8,128)S(1)} %hold.3), channel_id=1, source_target_pairs={{0,3},{1,2},{2,1},{3,0},{4,7},{5,6},{6,5},{7,4},{8,11},{9,10},{10,... | collective-permute-start | bytes 196616 | tf_op jit(solution)/shard_map/ppermute | solution.py:23
  17.7 8.5 %collective-permute-start.7 = (f32[32,1024]{1,0:T(8,128)S(1)}, f32[32,1024]{1,0:T(8,128)S(1)}, u32[]{:S(2)}, u32[]{:S(2)}) collective-permute-start(f32[32,1024]{1,0:T(8,128)S(1)} %hold.4), channel_id=1, source_target_pairs={{0,16},{1,17},{2,18},{3,19},{4,20},{5,21},{6,22},{7,23},{8,24},{9,... | collective-permute-start | bytes 393224 | tf_op jit(solution)/shard_map/ppermute | solution.py:23
  19.3 4.1 %collective-permute-start.4 = (f32[32,128]{1,0:T(8,128)S(1)}, f32[32,128]{1,0:T(8,128)S(1)}, u32[]{:S(2)}, u32[]{:S(2)}) collective-permute-start(f32[32,128]{1,0:T(8,128)S(1)} %add.7.own_ref.after_ref), channel_id=1, source_target_pairs={{0,9},{1,8},{2,11},{3,10},{4,13},{5,12},{6,15},{7,14},{8,1},{9,0},... | collective-permute-start | bytes 49160 | tf_op jit(solution)/shard_map/ppermute | solution.py:23
  21.0 5.7 %collective-permute-start.9 = (f32[32,1024]{1,0:T(8,128)S(1)}, f32[32,1024]{1,0:T(8,128)S(1)}, u32[]{:S(2)}, u32[]{:S(2)}) collective-permute-start(f32[32,1024]{1,0:T(8,128)S(1)} %hold.5), channel_id=1, source_target_pairs={{0,16},{1,17},{2,18},{3,19},{4,20},{5,21},{6,22},{7,23},{8,24},{9,... | collective-permute-start | bytes 393224 | tf_op jit(solution)/shard_map/ppermute | solution.py:23
  27.3 1.3 %collective-permute-start.10 = (f32[32,256]{1,0:T(8,128)S(1)}, f32[32,256]{1,0:T(8,128)S(1)}, u32[]{:S(2)}, u32[]{:S(2)}) collective-permute-start(f32[32,256]{1,0:T(8,128)S(1)} %score.1.kept_ref), channel_id=1, source_target_pairs={{0,1},{1,0},{2,3},{3,2},{4,5},{5,4},{6,7},{7,6},{8,9},{9,8},{10,11... | collective-permute-start | bytes 98312 | tf_op jit(solution)/shard_map/ppermute | solution.py:23

commit v5 on v4

--- a/solution.py
+++ b/solution.py
@@ -57,8 +57,8 @@
 
 def project_kernel(a_ref, g_ref, p_in_ref, p_out_ref, after_ref, out_ref):
     width = p_in_ref.shape[0]
-    out_ref[0:width, :] = lax.dot_general(p_in_ref[...], a_ref[...], NT, preferred_element_type=F32)
-    out_ref[width : 2 * width, :] = lax.dot_general(p_out_ref[...], g_ref[...], NT, preferred_element_type=F32)
+    out_ref[0:width, :] = lax.dot_general(a_ref[...], p_in_ref[...], NT, preferred_element_type=F32).T
+    out_ref[width : 2 * width, :] = lax.dot_general(g_ref[...], p_out_ref[...], NT, preferred_element_type=F32).T
 
 
 def project(activations, out_grads, proj_in, proj_out, after):
@@ -206,9 +206,7 @@
     )(blocks)
 
 
-def split_queries_kernel(groups, own_ref, *refs):
-    fetched_refs, (high_ref, low_ref) = refs[:-2], refs[-2:]
-    half = own_ref.shape[1] // 2
+def put_queries(first, groups, refs, high_ref, low_ref, half):
     piece = half // groups
     place, group, core = lax.axis_index("dp"), lax.axis_index("grp"), lax.axis_index("proj")
 
@@ -216,27 +214,14 @@
         at = pl.ds(pl.multiple_of(start, 16), value.shape[0])
         high_ref[at, :], low_ref[at, :] = split2(value)
 
-    put(place * half, own_ref[0, pl.ds(pl.multiple_of(core * half, 8), half), :])
-    for r, ref in enumerate(fetched_refs, 1):
-        if r == 1:
+    for r, ref in enumerate(refs, first):
+        if r == 0:
+            put(place * half, ref[0, pl.ds(pl.multiple_of(core * half, 8), half), :])
+        elif r == 1:
             put((place ^ r) * half, ref[...])
-            continue
-        for g in range(groups):
-            put((place ^ r) * half + (group ^ g) * piece, ref[g * piece : (g + 1) * piece, :])
-
-
-def split_queries(groups, own, fetched):
-    parts = 1 + len(fetched)
-    rows, columns = own.shape[1:]
-    shape = jax.ShapeDtypeStruct((parts * rows // 2, columns), BF16)
-    return pl.pallas_call(
-        functools.partial(split_queries_kernel, groups),
-        out_shape=(shape, shape),
-        in_specs=[pl.BlockSpec(memory_space=pltpu.VMEM)] * parts,
-        out_specs=(pl.BlockSpec(memory_space=pltpu.VMEM),) * 2,
-        compiler_params=pltpu.CompilerParams(vmem_limit_bytes=(4 + parts) * MIB),
-        name="split_queries",
-    )(own, *fetched)
+        else:
+            for g in range(groups):
+                put((place ^ r) * half + (group ^ g) * piece, ref[g * piece : (g + 1) * piece, :])
 
 
 def inverse_tiled(fisher_sum):
@@ -342,7 +327,9 @@
     )(*pieces, in_blocks, out_blocks)
 
 
-def score_kernel(both_ref, q_high_ref, q_low_ref, scores_ref):
+def score_kernel(parts, groups, half, both_ref, *refs):
+    query_refs, (scores_ref, q_high_ref, q_low_ref) = refs[:parts], refs[parts:]
+    put_queries(0, groups, query_refs, q_high_ref, q_low_ref, half)
     chunks, count = both_ref.shape[0], both_ref.shape[1] // 2
     total = None
     for c in range(chunks):
@@ -354,16 +341,18 @@
     scores_ref[...] = total * (1.0 / math.isqrt(chunks * CHUNK))
 
 
-def score(both, high, low):
-    rows = high.shape[0]
-    return pl.pallas_call(
-        score_kernel,
-        out_shape=jax.ShapeDtypeStruct((both.shape[1] // 2, rows), F32),
-        in_specs=[pl.BlockSpec(memory_space=pltpu.VMEM)] * 3,
-        out_specs=pl.BlockSpec(memory_space=pltpu.VMEM),
-        compiler_params=pltpu.CompilerParams(vmem_limit_bytes=(6 + rows // 128) * MIB),
+def score(groups, both, own, fetched):
+    parts = 1 + len(fetched)
+    half, columns = own.shape[1] // 2, own.shape[2]
+    return pl.pallas_call(
+        functools.partial(score_kernel, parts, groups, half),
+        out_shape=jax.ShapeDtypeStruct((both.shape[1] // 2, parts * half), F32),
+        in_specs=[pl.BlockSpec(memory_space=pltpu.VMEM)] * (1 + parts),
+        out_specs=pl.BlockSpec(memory_space=pltpu.VMEM),
+        scratch_shapes=[pltpu.VMEM((parts * half, columns), BF16)] * 2,
+        compiler_params=pltpu.CompilerParams(vmem_limit_bytes=(6 + parts) * MIB),
         name="score",
-    )(both, high, low)
+    )(both, own, *fetched)
 
 
 def place_kernel(half, kept_ref, received_ref, out_ref):
@@ -404,9 +393,9 @@
     )(value, after)
 
 
-ORDER = "x12"
-E_STAGE = 1
-Y_STAGES = (1, 2)
+ORDER = "x21"
+E_STAGE = 0
+Y_STAGES = (1,)
 
 
 def body(mesh, activations, out_grads, proj_in, proj_out, lengths, queries):
@@ -437,7 +426,7 @@
             blocks = hold(blocks, factor)
             blocks = jnp.concatenate([blocks, swap(blocks, mesh, query_bits[i] | core_bit)], axis=0)
         if stage in Y_STAGES:
-            first, end = ((1, 2), (2, n_dp - 1))[Y_STAGES.index(stage)]
+            first, end = (1, n_dp - 1)
             for r in range(first, end):
                 fetched[r] = hold(fetched[r], factor)
                 for bit in group_bits:
@@ -453,8 +442,7 @@
     arranged, received = lax.optimization_barrier((arranged, received))
     both = condition(arranged, *inverses(factor, received), queries.shape[2])
 
-    high, low = split_queries(groups, queries, fetched)
-    scores = score(both, high, low)
+    scores = score(groups, both, queries, fetched)
     return place(queries.shape[1] // 2, scores, swap(scores, mesh, core_bit))
 
 

time: 29.4 us -> 28.4 us (0.966)
  starting transfers between devices: 15 us -> 13.6 us
  waiting for transfers between devices: 3.62 us -> 4.21 us
    ppermute x11, starting transfers between devices: 15 us -> 13.6 us  [swap(): return lax.ppermute(value, AXES, [(i, i ^ mask) for i in range(count)])]
    ppermute x11, waiting for transfers between devices: 3.62 us -> 4.21 us  [swap(): return lax.ppermute(value, AXES, [(i, i ^ mask) for i in range(count)])]
    pallas_call x2 -> x1, Pallas kernels: 0.55 us -> 0.6 us  [score(): pl.pallas_call(functools.partial(score_kernel, parts, groups, half), out_...]
where the time goes in v5:
time: 28.4 us; the launch traced here: 28.3 us
  starting transfers between devices  13.6 us (48%)
  Pallas kernels  10.3 us (36%)
  waiting for transfers between devices  4.21 us (15%)
    ppermute x11, starting transfers between devices, swap(): return lax.ppermute(value, AXES, [(i, i ^ mask) for i in range(count)])  13.6 us
    ppermute x11, waiting for transfers between devices, swap(): return lax.ppermute(value, AXES, [(i, i ^ mask) for i in range(count)])  4.21 us
    pallas_call x1, Pallas kernels, project(): pl.pallas_call(project_kernel, out_shape=jax.ShapeDtypeStruct((2 * proj_i...  2.61 us
    pallas_call x1, Pallas kernels, inverses(): pl.pallas_call(inverses_kernel, out_shape=(shape, shape), in_specs=[pl.Bl...  1.63 us
    pallas_call x1, Pallas kernels, pick_queries(): pl.pallas_call(functools.partial(pick_kernel, groups), out_shape=tuple((j...  1.15 us
    pallas_call x1, Pallas kernels, condition(): pl.pallas_call(condition_kernel, out_shape=jax.ShapeDtypeStruct((columns...  1.15 us
    pallas_call x1, Pallas kernels, example_grads(): pl.pallas_call(examples_kernel, out_shape=jax.ShapeDtypeStruct((member.sh...  0.96 us
    pallas_call x1, Pallas kernels, place(): pl.pallas_call(functools.partial(place_kernel, half), out_shape=jax.Shape...  0.72 us
  transfers between devices with their start and end apart: 11, of which 5 were waited for; matrix products, arithmetic and copies ran while one was open for 0% of the time, Pallas kernels for 27%

profile of v5, /device:TPU:0, one launch (start us, length us, event | category | flops | bytes accessed | tf_op | source)
XLA Modules:
  0.0 28.3 jit_solution(18238222020466534037)
XLA Ops:
  0.0 1.2 %pick_queries.1 = (f32[64,1024]{1,0:T(8,128)S(1)}, f32[32,1024]{1,0:T(8,128)S(1)}) custom-call(f32[1,128,1024]{2,1,0:T(8,128)} %refs_0_.1), custom_call_target="tpu_custom_call" | custom-call | flops 4000000000 | bytes 1000000 | tf_op jit(solution)/shard_map/pick_queries/pallas_call | solution.py:46
  1.2 4.1 %collective-permute-start.6 = (f32[32,1024]{1,0:T(8,128)S(1)}, f32[32,1024]{1,0:T(8,128)S(1)}, u32[]{:S(2)}, u32[]{:S(2)}) collective-permute-start(f32[32,1024]{1,0:T(8,128)S(1)} %get-tuple-element.44), channel_id=1, source_target_pairs={{0,8},{1,9},{2,10},{3,11},{4,12},{5,13},{6,14},{7,15},{8,0},{9,1},... | collective-permute-start | bytes 393224 | tf_op jit(solution)/shard_map/ppermute | solution.py:23
  5.3 1.3 %collective-permute-start.8 = (f32[32,1024]{1,0:T(8,128)S(1)}, f32[32,1024]{1,0:T(8,128)S(1)}, u32[]{:S(2)}, u32[]{:S(2)}) collective-permute-start(f32[32,1024]{1,0:T(8,128)S(1)} %get-tuple-element.44), channel_id=1, source_target_pairs={{0,12},{1,13},{2,14},{3,15},{4,8},{5,9},{6,10},{7,11},{8,4},{9,5},... | collective-permute-start | bytes 393224 | tf_op jit(solution)/shard_map/ppermute | solution.py:23
  6.7 0.2 collective-permute-start.5
  6.9 2.6 %project.1.after_ref.own_ref = f32[64,512]{1,0:T(8,128)S(1)} custom-call(bf16[512,2048]{1,0:T(8,128)(2,1)S(1)} %copy-done.1, bf16[512,7168]{1,0:T(8,128)(2,1)S(1)} %copy-done, bf16[32,2048]{1,0:T(8,128)(2,1)S(1)} %bitcast.4, bf16[32,7168]{1,0:T(8,128)(2,1)S(1)} %bitcast.3, f32[64,1024]{1,0:T(8,128)S(1)} %get-tuple-element.25.after_ref), custom_call_target="tpu_custom_call" | custom-call | tf_op jit(solution)/shard_map/project/pallas_call | solution.py:65
  9.6 0.6 %masks.1 = (bf16[16,512]{1,0:T(8,128)(2,1)S(1)}, f32[8,512]{1,0:T(8,128)S(1)}, f32[16,128]{1,0:T(8,128)S(1)}) custom-call(s32[1,17]{1,0:T(1,128)S(1)} %copy-done.5, f32[64,512]{1,0:T(8,128)S(1)} %project.1.after_ref.own_ref), custom_call_target="tpu_custom_call" | custom-call | flops 2000000000 | bytes 1000000 | tf_op jit(solution)/shard_map/masks/pallas_call | solution.py:94
  10.1 0.8 %collective-permute-done.other_ref = f32[64,512]{1,0:T(8,128)S(1)} collective-permute-done((f32[64,512]{1,0:T(8,128)S(1)}, f32[64,512]{1,0:T(8,128)S(1)}, u32[]{:S(2)}, u32[]{:S(2)}) %collective-permute-start) | collective-permute-done | bytes 131104 | tf_op jit(solution)/shard_map/ppermute | solution.py:23
  10.9 0.3 fisher.1.after_ref
  11.2 1.3 %collective-permute-start.2 = (f32[32,128]{1,0:T(8,128)S(1)}, f32[32,128]{1,0:T(8,128)S(1)}, u32[]{:S(2)}, u32[]{:S(2)}) collective-permute-start(f32[32,128]{1,0:T(8,128)S(1)} %fisher.1.after_ref), channel_id=1, source_target_pairs={{0,3},{1,2},{2,1},{3,0},{4,7},{5,6},{6,5},{7,4},{8,11},{9,10},{10,... | collective-permute-start | bytes 49160 | tf_op jit(solution)/shard_map/ppermute | solution.py:23
  12.5 1.0 %examples.1 = f32[16,1024]{1,0:T(8,128)S(1)} custom-call(bf16[16,512]{1,0:T(8,128)(2,1)S(1)} %get-tuple-element.26.member_ref, f32[16,128]{1,0:T(8,128)S(1)} %get-tuple-element.27.count_ref, f32[64,512]{1,0:T(8,128)S(1)} %project.1.after_ref.own_ref, f32[64,512]{1,0:T(8,128)S(1)} %collective-permute-done.other_ref), custom_call_target="tpu_custom_call" | custom-call | flops 2000000000 | bytes 1000000 | tf_op jit(solution)/shard_map/examples/pallas_call | solution.py:154
  13.5 0.6 %collective-permute-start.1 = (f32[1,16,1024]{2,1,0:T(8,128)S(1)}, f32[1,16,1024]{2,1,0:T(8,128)S(1)}, u32[]{:S(2)}, u32[]{:S(2)}) collective-permute-start(f32[1,16,1024]{2,1,0:T(8,128)S(1)} %hold.3), channel_id=1, source_target_pairs={{0,3},{1,2},{2,1},{3,0},{4,7},{5,6},{6,5},{7,4},{8,11},{9,10},{10,... | collective-permute-start | bytes 196616 | tf_op jit(solution)/shard_map/ppermute | solution.py:23
  14.0 0.4 %collective-permute-done.2 = f32[32,128]{1,0:T(8,128)S(1)} collective-permute-done((f32[32,128]{1,0:T(8,128)S(1)}, f32[32,128]{1,0:T(8,128)S(1)}, u32[]{:S(2)}, u32[]{:S(2)}) %collective-permute-start.2) | collective-permute-done | bytes 16416 | tf_op jit(solution)/shard_map/ppermute | solution.py:23
  14.4 2.9 %collective-permute-start.3 = (f32[32,128]{1,0:T(8,128)S(1)}, f32[32,128]{1,0:T(8,128)S(1)}, u32[]{:S(2)}, u32[]{:S(2)}) collective-permute-start(f32[32,128]{1,0:T(8,128)S(1)} %add.6.after_ref), channel_id=1, source_target_pairs={{0,9},{1,8},{2,11},{3,10},{4,13},{5,12},{6,15},{7,14},{8,1},{9,0},... | collective-permute-start | bytes 49160 | tf_op jit(solution)/shard_map/ppermute | solution.py:23
  17.3 1.6 %collective-permute-start.7 = (f32[32,1024]{1,0:T(8,128)S(1)}, f32[32,1024]{1,0:T(8,128)S(1)}, u32[]{:S(2)}, u32[]{:S(2)}) collective-permute-start(f32[32,1024]{1,0:T(8,128)S(1)} %hold.4), channel_id=1, source_target_pairs={{0,16},{1,17},{2,18},{3,19},{4,20},{5,21},{6,22},{7,23},{8,24},{9,... | collective-permute-start | bytes 393224 | tf_op jit(solution)/shard_map/ppermute | solution.py:23
  18.9 0.6 %collective-permute-start.9 = (f32[32,1024]{1,0:T(8,128)S(1)}, f32[32,1024]{1,0:T(8,128)S(1)}, u32[]{:S(2)}, u32[]{:S(2)}) collective-permute-start(f32[32,1024]{1,0:T(8,128)S(1)} %hold.5), channel_id=1, source_target_pairs={{0,16},{1,17},{2,18},{3,19},{4,20},{5,21},{6,22},{7,23},{8,24},{9,... | collective-permute-start | bytes 393224 | tf_op jit(solution)/shard_map/ppermute | solution.py:23
  19.5 0.9 %collective-permute-start.4 = (f32[32,128]{1,0:T(8,128)S(1)}, f32[32,128]{1,0:T(8,128)S(1)}, u32[]{:S(2)}, u32[]{:S(2)}) collective-permute-start(f32[32,128]{1,0:T(8,128)S(1)} %add.7.own_ref), channel_id=1, source_target_pairs={{0,5},{1,4},{2,7},{3,6},{4,1},{5,0},{6,3},{7,2},{8,13},{9,12},{10,... | collective-permute-start | bytes 49160 | tf_op jit(solution)/shard_map/ppermute | solution.py:23
  20.3 0.6 %arrange_examples.1 = (bf16[128,256]{1,0:T(8,128)(2,1)S(1)}, bf16[128,256]{1,0:T(8,128)(2,1)S(1)}, bf16[128,256]{1,0:T(8,128)(2,1)S(1)}) custom-call(f32[2,16,1024]{2,1,0:T(8,128)S(1)} %pad_maximum_fusion.2.blocks_ref), custom_call_target="tpu_custom_call" | custom-call | tf_op jit(solution)/shard_map/arrange_examples/pallas_call | solution.py:198
  20.9 1.8 %collective-permute-done.4.other_ref = f32[32,128]{1,0:T(8,128)S(1)} collective-permute-done((f32[32,128]{1,0:T(8,128)S(1)}, f32[32,128]{1,0:T(8,128)S(1)}, u32[]{:S(2)}, u32[]{:S(2)}) %collective-permute-start.4) | collective-permute-done | bytes 16416 | tf_op jit(solution)/shard_map/ppermute | solution.py:23
  22.7 1.6 %inverses.1 = (bf16[3,256,256]{2,1,0:T(8,128)(2,1)S(1)}, bf16[3,256,256]{2,1,0:T(8,128)(2,1)S(1)}) custom-call(f32[32,128]{1,0:T(8,128)S(1)} %add.7.own_ref, f32[32,128]{1,0:T(8,128)S(1)} %collective-permute-done.4.other_ref), custom_call_target="tpu_custom_call" | custom-call | tf_op jit(solution)/shard_map/inverses/pallas_call | solution.py:287
  24.3 1.2 %condition.1.both_ref = bf16[4,64,256]{2,1,0:T(8,128)(2,1)S(1)} custom-call(bf16[128,256]{1,0:T(8,128)(2,1)S(1)} %get-tuple-element.38.high_ref, bf16[128,256]{1,0:T(8,128)(2,1)S(1)} %get-tuple-element.39.middle_ref, bf16[128,256]{1,0:T(8,128)(2,1)S(1)} %get-tuple-element.40.low_ref, bf16[3,256,256]{2,1,0:T(8,128)(2,1)S(1)} %get-tuple-element.42.in_ref, ...), custom_call_target="tpu_custom_call" | custom-call | flops 2000000000 | bytes 1000000 | tf_op jit(solution)/shard_map/condition/pallas_call | solution.py:318
  25.5 0.1 collective-permute-done.9
  25.7 0.6 %score.1.kept_ref = f32[32,256]{1,0:T(8,128)S(1)} custom-call(bf16[4,64,256]{2,1,0:T(8,128)(2,1)S(1)} %condition.1.both_ref, f32[1,128,1024]{2,1,0:T(8,128)S(1)} %copy-done.2, f32[64,1024]{1,0:T(8,128)S(1)} %collective-permute-done.5.refs_1_, f32[64,1024]{1,0:T(8,128)S(1)} %pad_maximum_fusion.refs_2_, f32[64,1024]{1,0:T(8,128)S(1)} %pad_maximum_fusion.1.refs_3_), custom_call_target="tpu_custom_call" | custom-call | tf_op jit(solution)/shard_map/score/pallas_call | solution.py:347
  26.4 1.2 %collective-permute-done.10.received_ref = f32[32,256]{1,0:T(8,128)S(1)} collective-permute-done((f32[32,256]{1,0:T(8,128)S(1)}, f32[32,256]{1,0:T(8,128)S(1)}, u32[]{:S(2)}, u32[]{:S(2)}) %collective-permute-start.10) | collective-permute-done | bytes 32800 | tf_op jit(solution)/shard_map/ppermute | solution.py:23
  27.6 0.7 %place.1 = f32[32,512]{1,0:T(8,128)} custom-call(f32[32,256]{1,0:T(8,128)S(1)} %score.1.kept_ref, f32[32,256]{1,0:T(8,128)S(1)} %collective-permute-done.10.received_ref), custom_call_target="tpu_custom_call" | custom-call | tf_op jit(solution)/shard_map/place/pallas_call | solution.py:370
  (28 shorter events, 0.3 us)
Async XLA Ops:
  0.0 6.9 %copy-start.1 = (bf16[512,2048]{1,0:T(8,128)(2,1)S(1)}, bf16[512,2048]{1,0:T(8,128)(2,1)}, u32[]{:S(2)}) copy-start(bf16[512,2048]{1,0:T(8,128)(2,1)} %a_ref.1) | copy-start | bytes 6291460
  0.0 6.9 %copy-start = (bf16[512,7168]{1,0:T(8,128)(2,1)S(1)}, bf16[512,7168]{1,0:T(8,128)(2,1)}, u32[]{:S(2)}) copy-start(bf16[512,7168]{1,0:T(8,128)(2,1)} %g_ref.1) | copy-start | bytes 22020100
  0.0 6.9 %copy-start.4 = (bf16[2048,32]{0,1:T(8,128)(2,1)S(1)}, bf16[2048,32]{0,1:T(8,128)(2,1)}, u32[]{:S(2)}) copy-start(bf16[2048,32]{0,1:T(8,128)(2,1)} %param.8) | copy-start | bytes 393220
  0.0 6.9 %copy-start.3 = (bf16[7168,32]{0,1:T(8,128)(2,1)S(1)}, bf16[7168,32]{0,1:T(8,128)(2,1)}, u32[]{:S(2)}) copy-start(bf16[7168,32]{0,1:T(8,128)(2,1)} %param.9) | copy-start | bytes 1376260
  1.2 8.4 %copy-start.5 = (s32[1,17]{1,0:T(1,128)S(1)}, s32[1,17]{1,0:T(1,128)}, u32[]{:S(2)}) copy-start(s32[1,17]{1,0:T(1,128)} %lengths_ref.1) | copy-start | bytes 208
  1.2 16.1 %collective-permute-start.6 = (f32[32,1024]{1,0:T(8,128)S(1)}, f32[32,1024]{1,0:T(8,128)S(1)}, u32[]{:S(2)}, u32[]{:S(2)}) collective-permute-start(f32[32,1024]{1,0:T(8,128)S(1)} %get-tuple-element.44), channel_id=1, source_target_pairs={{0,8},{1,9},{2,10},{3,11},{4,12},{5,13},{6,14},{7,15},{8,0},{9,1},... | collective-permute-start | bytes 393224 | tf_op jit(solution)/shard_map/ppermute | solution.py:23
  5.3 13.6 %collective-permute-start.8 = (f32[32,1024]{1,0:T(8,128)S(1)}, f32[32,1024]{1,0:T(8,128)S(1)}, u32[]{:S(2)}, u32[]{:S(2)}) collective-permute-start(f32[32,1024]{1,0:T(8,128)S(1)} %get-tuple-element.44), channel_id=1, source_target_pairs={{0,12},{1,13},{2,14},{3,15},{4,8},{5,9},{6,10},{7,11},{8,4},{9,5},... | collective-permute-start | bytes 393224 | tf_op jit(solution)/shard_map/ppermute | solution.py:23
  6.7 19.0 %collective-permute-start.5 = (f32[64,1024]{1,0:T(8,128)S(1)}, f32[64,1024]{1,0:T(8,128)S(1)}, u32[]{:S(2)}, u32[]{:S(2)}) collective-permute-start(f32[64,1024]{1,0:T(8,128)S(1)} %get-tuple-element.25.after_ref), channel_id=1, source_target_pairs={{0,4},{1,5},{2,6},{3,7},{4,0},{5,1},{6,2},{7,3},{8,12},{9,13},{10,... | collective-permute-start | bytes 786440 | tf_op jit(solution)/shard_map/ppermute | solution.py:23
  9.5 1.4 %collective-permute-start = (f32[64,512]{1,0:T(8,128)S(1)}, f32[64,512]{1,0:T(8,128)S(1)}, u32[]{:S(2)}, u32[]{:S(2)}) collective-permute-start(f32[64,512]{1,0:T(8,128)S(1)} %project.1.after_ref.own_ref), channel_id=1, source_target_pairs={{0,1},{1,0},{2,3},{3,2},{4,5},{5,4},{6,7},{7,6},{8,9},{9,8},{10,11... | collective-permute-start | bytes 393224 | tf_op jit(solution)/shard_map/ppermute | solution.py:23
  11.2 3.2 %collective-permute-start.2 = (f32[32,128]{1,0:T(8,128)S(1)}, f32[32,128]{1,0:T(8,128)S(1)}, u32[]{:S(2)}, u32[]{:S(2)}) collective-permute-start(f32[32,128]{1,0:T(8,128)S(1)} %fisher.1.after_ref), channel_id=1, source_target_pairs={{0,3},{1,2},{2,1},{3,0},{4,7},{5,6},{6,5},{7,4},{8,11},{9,10},{10,... | collective-permute-start | bytes 49160 | tf_op jit(solution)/shard_map/ppermute | solution.py:23
  13.5 6.9 %collective-permute-start.1 = (f32[1,16,1024]{2,1,0:T(8,128)S(1)}, f32[1,16,1024]{2,1,0:T(8,128)S(1)}, u32[]{:S(2)}, u32[]{:S(2)}) collective-permute-start(f32[1,16,1024]{2,1,0:T(8,128)S(1)} %hold.3), channel_id=1, source_target_pairs={{0,3},{1,2},{2,1},{3,0},{4,7},{5,6},{6,5},{7,4},{8,11},{9,10},{10,... | collective-permute-start | bytes 196616 | tf_op jit(solution)/shard_map/ppermute | solution.py:23
  14.4 11.3 %copy-start.2 = (f32[1,128,1024]{2,1,0:T(8,128)S(1)}, f32[1,128,1024]{2,1,0:T(8,128)}, u32[]{:S(2)}) copy-start(f32[1,128,1024]{2,1,0:T(8,128)} %refs_0_.1) | copy-start | bytes 1572868
  14.4 5.1 %collective-permute-start.3 = (f32[32,128]{1,0:T(8,128)S(1)}, f32[32,128]{1,0:T(8,128)S(1)}, u32[]{:S(2)}, u32[]{:S(2)}) collective-permute-start(f32[32,128]{1,0:T(8,128)S(1)} %add.6.after_ref), channel_id=1, source_target_pairs={{0,9},{1,8},{2,11},{3,10},{4,13},{5,12},{6,15},{7,14},{8,1},{9,0},... | collective-permute-start | bytes 49160 | tf_op jit(solution)/shard_map/ppermute | solution.py:23
  17.3 8.2 %collective-permute-start.7 = (f32[32,1024]{1,0:T(8,128)S(1)}, f32[32,1024]{1,0:T(8,128)S(1)}, u32[]{:S(2)}, u32[]{:S(2)}) collective-permute-start(f32[32,1024]{1,0:T(8,128)S(1)} %hold.4), channel_id=1, source_target_pairs={{0,16},{1,17},{2,18},{3,19},{4,20},{5,21},{6,22},{7,23},{8,24},{9,... | collective-permute-start | bytes 393224 | tf_op jit(solution)/shard_map/ppermute | solution.py:23
  18.9 6.7 %collective-permute-start.9 = (f32[32,1024]{1,0:T(8,128)S(1)}, f32[32,1024]{1,0:T(8,128)S(1)}, u32[]{:S(2)}, u32[]{:S(2)}) collective-permute-start(f32[32,1024]{1,0:T(8,128)S(1)} %hold.5), channel_id=1, source_target_pairs={{0,16},{1,17},{2,18},{3,19},{4,20},{5,21},{6,22},{7,23},{8,24},{9,... | collective-permute-start | bytes 393224 | tf_op jit(solution)/shard_map/ppermute | solution.py:23
  19.5 3.2 %collective-permute-start.4 = (f32[32,128]{1,0:T(8,128)S(1)}, f32[32,128]{1,0:T(8,128)S(1)}, u32[]{:S(2)}, u32[]{:S(2)}) collective-permute-start(f32[32,128]{1,0:T(8,128)S(1)} %add.7.own_ref), channel_id=1, source_target_pairs={{0,5},{1,4},{2,7},{3,6},{4,1},{5,0},{6,3},{7,2},{8,13},{9,12},{10,... | collective-permute-start | bytes 49160 | tf_op jit(solution)/shard_map/ppermute | solution.py:23
  26.3 1.3 %collective-permute-start.10 = (f32[32,256]{1,0:T(8,128)S(1)}, f32[32,256]{1,0:T(8,128)S(1)}, u32[]{:S(2)}, u32[]{:S(2)}) collective-permute-start(f32[32,256]{1,0:T(8,128)S(1)} %score.1.kept_ref), channel_id=1, source_target_pairs={{0,1},{1,0},{2,3},{3,2},{4,5},{5,4},{6,7},{7,6},{8,9},{9,8},{10,11... | collective-permute-start | bytes 98312 | tf_op jit(solution)/shard_map/ppermute | solution.py:23

commit v6 on v5

--- a/solution.py
+++ b/solution.py
@@ -29,7 +29,7 @@
 
 def pick_kernel(groups, queries_hbm, half_ref, piece_ref, sems):
     half, piece = half_ref.shape[0], piece_ref.shape[0]
-    core = lax.axis_index("proj")
+    core = 1 - lax.axis_index("proj")
     index = core * groups + lax.axis_index("grp")
     copies = [
         pltpu.make_async_copy(queries_hbm.at[0, pl.ds(pl.multiple_of(core * half, 8), half)], half_ref, sems.at[0]),
@@ -206,64 +206,89 @@
     )(blocks)
 
 
-def put_queries(first, groups, refs, high_ref, low_ref, half):
-    piece = half // groups
-    place, group, core = lax.axis_index("dp"), lax.axis_index("grp"), lax.axis_index("proj")
-
-    def put(start, value):
-        at = pl.ds(pl.multiple_of(start, 16), value.shape[0])
+def split_near_kernel(own_ref, near_ref, high_ref, low_ref):
+    half = near_ref.shape[0]
+    start = pl.multiple_of(lax.axis_index("proj") * half, 8)
+    for i, value in enumerate((own_ref[0, pl.ds(start, half), :], near_ref[...])):
+        at = slice(i * half, (i + 1) * half)
         high_ref[at, :], low_ref[at, :] = split2(value)
 
-    for r, ref in enumerate(refs, first):
-        if r == 0:
-            put(place * half, ref[0, pl.ds(pl.multiple_of(core * half, 8), half), :])
-        elif r == 1:
-            put((place ^ r) * half, ref[...])
-        else:
-            for g in range(groups):
-                put((place ^ r) * half + (group ^ g) * piece, ref[g * piece : (g + 1) * piece, :])
-
-
-def inverse_tiled(fisher_sum):
+
+def split_near(own, near):
+    half, columns = near.shape
+    shape = jax.ShapeDtypeStruct((2 * half, columns), BF16)
+    return pl.pallas_call(
+        split_near_kernel,
+        out_shape=(shape, shape),
+        in_specs=[pl.BlockSpec(memory_space=pltpu.VMEM)] * 2,
+        out_specs=(pl.BlockSpec(memory_space=pltpu.VMEM),) * 2,
+        compiler_params=pltpu.CompilerParams(vmem_limit_bytes=6 * MIB),
+        name="split_near",
+    )(own, near)
+
+
+def damped(fisher_sum):
     width = fisher_sum.shape[0]
     row = lax.broadcasted_iota(jnp.int32, (width, width), 0)
     column = lax.broadcasted_iota(jnp.int32, (width, width), 1)
     trace = jnp.sum(jnp.where(row == column, fisher_sum, 0.0), keepdims=True)
-    damped = fisher_sum * (width / trace) + jnp.where(row == column, 1.0, 0.0)
-    state = jnp.concatenate([damped] * (128 // width), axis=1)
-    lane = lax.broadcasted_iota(jnp.int32, state.shape, 1) % width
-    sublane = lax.broadcasted_iota(jnp.int32, state.shape, 0)
-    top = lane[0:1]
-
-    def apply(m, x, y):
-        return m[0][0] * x + m[0][1] * y, m[1][0] * x + m[1][1] * y
-
-    def invert(m):
-        scale = 1.0 / (m[0][0] * m[1][1] - m[0][1] * m[1][0])
-        return (m[1][1] * scale, -m[0][1] * scale), (-m[1][0] * scale, m[0][0] * scale)
-
+    return fisher_sum * (width / trace) + jnp.where(row == column, 1.0, 0.0)
+
+
+def inverse_pair(pair):
+    width, group = pair.shape[0], 8
+    both = jnp.concatenate([damped(pair[:, 0:width]), damped(pair[:, width : 2 * width])], axis=1)
+    state = jnp.concatenate([both] * (128 // (2 * width)), axis=1)
+    state = [state[i : i + group] for i in range(0, width, group)]
+    lane = lax.broadcasted_iota(jnp.int32, (group, 128), 1)
+    own = lane % width
+    first = lane - own
+    sublane = lax.broadcasted_iota(jnp.int32, (group, 128), 0)
+
+    def spread(value, index):
+        return jnp.take_along_axis(value, index, axis=1, mode="promise_in_bounds")
+
+    columns = [[spread(part, first + c) for c in range(4)] for part in state]
     for k in range(0, width, 4):
-        columns = [jnp.broadcast_to(state[:, k + c : k + c + 1], state.shape) for c in range(4)]
-        pivot = [[columns[c][k + r : k + r + 1, :] for c in range(4)] for r in range(4)]
-        inside = (top >= k) & (top < k + 4)
-        rows = [
-            jnp.where(top == k + r, 1.0, jnp.where(inside, 0.0, state[k + r : k + r + 1, :])) for r in range(4)
-        ]
-        corner = invert((pivot[0][0:2], pivot[1][0:2]))
-        upper = apply(corner, rows[0], rows[1])
-        right = [apply(corner, pivot[0][c], pivot[1][c]) for c in (2, 3)]
-        schur = [
-            [pivot[r][c] - pivot[r][0] * right[c - 2][0] - pivot[r][1] * right[c - 2][1] for c in (2, 3)] for r in (2, 3)
-        ]
-        lower = apply(
-            invert(schur), *(rows[r] - pivot[r][0] * upper[0] - pivot[r][1] * upper[1] for r in (2, 3))
-        )
-        solved = [upper[r] - right[0][r] * lower[0] - right[1][r] * lower[1] for r in range(2)] + list(lower)
-        change = columns[0] * solved[0] + columns[1] * solved[1] + columns[2] * solved[2] + columns[3] * solved[3]
-        state = jnp.where((lane >= k) & (lane < k + 4), 0.0, state) - change
-        for r in range(4):
-            state = jnp.where(sublane == k + r, solved[r], state)
-    return state
+        at, offset = k // group, k % group
+        more = k + 4 < width
+        ahead = [[spread(part, first + (k + 4 + c)) for c in range(4)] for part in state] if more else None
+        inside = (own >= k) & (own < k + 4)
+
+        def row(value, r):
+            return value[offset + r : offset + r + 1, :]
+
+        p = [[row(columns[at][c], r) for c in range(4)] for r in range(4)]
+        scale = 1.0 / (p[0][0] * p[1][1] - p[0][1] * p[1][0])
+        a = ((p[1][1] * scale, -p[0][1] * scale), (-p[1][0] * scale, p[0][0] * scale))
+        right = [[a[r][0] * p[0][c] + a[r][1] * p[1][c] for r in range(2)] for c in (2, 3)]
+        s = [[p[r][c] - (p[r][0] * right[c - 2][0] + p[r][1] * right[c - 2][1]) for c in (2, 3)] for r in (2, 3)]
+        scale = 1.0 / (s[0][0] * s[1][1] - s[0][1] * s[1][0])
+        d = ((s[1][1] * scale, -s[0][1] * scale), (-s[1][0] * scale, s[0][0] * scale))
+
+        def solve(q):
+            upper = [a[r][0] * q[0] + a[r][1] * q[1] for r in range(2)]
+            rest = [q[r] - (p[r][0] * upper[0] + p[r][1] * upper[1]) for r in (2, 3)]
+            lower = [d[r][0] * rest[0] + d[r][1] * rest[1] for r in range(2)]
+            return [upper[r] - (right[0][r] * lower[0] + right[1][r] * lower[1]) for r in range(2)] + lower
+
+        def step(i, value, solved):
+            c = columns[i]
+            value = value - ((c[0] * solved[0] + c[1] * solved[1]) + (c[2] * solved[2] + c[3] * solved[3]))
+            if i == at:
+                for r in range(4):
+                    value = jnp.where(sublane == offset + r, solved[r], value)
+            return value
+
+        rows = [jnp.where(own[0:1] == k + r, 1.0, jnp.where(inside[0:1], 0.0, row(state[at], r))) for r in range(4)]
+        solved = solve(rows)
+        following = columns
+        if more:
+            solved_ahead = [solve([row(ahead[at][c], r) for r in range(4)]) for c in range(4)]
+            following = [[step(i, ahead[i][c], solved_ahead[c]) for c in range(4)] for i in range(len(state))]
+        state = [step(i, jnp.where(inside, 0.0, part), solved) for i, part in enumerate(state)]
+        columns = following
+    return [jnp.concatenate([spread(part, own + start) for part in state], axis=0) for start in (0, width)]
 
 
 def block_diagonal(tiled):
@@ -277,8 +302,8 @@
 def inverses_kernel(own_ref, other_ref, in_ref, out_ref):
     width = own_ref.shape[0]
     total = own_ref[...] + other_ref[...]
-    for ref, fisher_sum in ((in_ref, total[:, 0:width]), (out_ref, total[:, width : 2 * width])):
-        for piece, value in enumerate(split3(block_diagonal(inverse_tiled(fisher_sum)))):
+    for ref, inverse in zip((in_ref, out_ref), inverse_pair(total[:, 0 : 2 * width])):
+        for piece, value in enumerate(split3(block_diagonal(inverse))):
             ref[piece] = value
 
 
@@ -327,32 +352,39 @@
     )(*pieces, in_blocks, out_blocks)
 
 
-def score_kernel(parts, groups, half, both_ref, *refs):
-    query_refs, (scores_ref, q_high_ref, q_low_ref) = refs[:parts], refs[parts:]
-    put_queries(0, groups, query_refs, q_high_ref, q_low_ref, half)
+def score_kernel(groups, both_ref, near_high_ref, near_low_ref, *refs):
+    fetched_refs, (scores_ref, high_ref, low_ref) = refs[:-3], refs[-3:]
     chunks, count = both_ref.shape[0], both_ref.shape[1] // 2
-    total = None
-    for c in range(chunks):
-        cols = slice(c * CHUNK, (c + 1) * CHUNK)
-        by_high = lax.dot_general(both_ref[c], q_high_ref[:, cols], NT, preferred_element_type=F32)
-        by_low = lax.dot_general(both_ref[c, 0:count], q_low_ref[:, cols], NT, preferred_element_type=F32)
-        part = by_high[0:count] + (by_high[count:] + by_low)
-        total = part if total is None else total + part
-    scores_ref[...] = total * (1.0 / math.isqrt(chunks * CHUNK))
-
-
-def score(groups, both, own, fetched):
-    parts = 1 + len(fetched)
-    half, columns = own.shape[1] // 2, own.shape[2]
-    return pl.pallas_call(
-        functools.partial(score_kernel, parts, groups, half),
-        out_shape=jax.ShapeDtypeStruct((both.shape[1] // 2, parts * half), F32),
-        in_specs=[pl.BlockSpec(memory_space=pltpu.VMEM)] * (1 + parts),
-        out_specs=pl.BlockSpec(memory_space=pltpu.VMEM),
-        scratch_shapes=[pltpu.VMEM((parts * half, columns), BF16)] * 2,
-        compiler_params=pltpu.CompilerParams(vmem_limit_bytes=(6 + parts) * MIB),
+    near = near_high_ref.shape[0]
+    half = fetched_refs[0].shape[0]
+    piece = half // groups
+    group = lax.axis_index("grp")
+    for i, ref in enumerate(fetched_refs):
+        for g in range(groups):
+            at = pl.ds(pl.multiple_of(i * half + (group ^ g) * piece, 16), piece)
+            high_ref[at, :], low_ref[at, :] = split2(ref[g * piece : (g + 1) * piece, :])
+    for start, q_high_ref, q_low_ref in ((0, near_high_ref, near_low_ref), (near, high_ref, low_ref)):
+        total = None
+        for c in range(chunks):
+            cols = slice(c * CHUNK, (c + 1) * CHUNK)
+            by_high = lax.dot_general(both_ref[c], q_high_ref[:, cols], NT, preferred_element_type=F32)
+            by_low = lax.dot_general(both_ref[c, 0:count], q_low_ref[:, cols], NT, preferred_element_type=F32)
+            part = by_high[0:count] + (by_high[count:] + by_low)
+            total = part if total is None else total + part
+        scores_ref[:, start : start + total.shape[1]] = total * (1.0 / math.isqrt(chunks * CHUNK))
+
+
+def score(groups, both, near, fetched):
+    rows, columns = len(fetched) * fetched[0].shape[0], fetched[0].shape[1]
+    return pl.pallas_call(
+        functools.partial(score_kernel, groups),
+        out_shape=jax.ShapeDtypeStruct((both.shape[1] // 2, near[0].shape[0] + rows), F32),
+        in_specs=[pl.BlockSpec(memory_space=pltpu.VMEM)] * (3 + len(fetched)),
+        out_specs=pl.BlockSpec(memory_space=pltpu.VMEM),
+        scratch_shapes=[pltpu.VMEM((rows, columns), BF16)] * 2,
+        compiler_params=pltpu.CompilerParams(vmem_limit_bytes=(8 + len(fetched)) * MIB),
         name="score",
-    )(both, own, *fetched)
+    )(both, *near, *fetched)
 
 
 def place_kernel(half, kept_ref, received_ref, out_ref):
@@ -360,9 +392,10 @@
     kept, received = kept_ref[...], received_ref[...]
     first = jnp.where(core == 0, kept, received)
     second = jnp.where(core == 0, received, kept)
-    for k in range(kept.shape[1] // half):
-        at = slice(k * half, (k + 1) * half)
-        out_ref[:, 2 * k * half : 2 * (k + 1) * half] = jnp.concatenate([first[:, at], second[:, at]], axis=1)
+    for r in range(kept.shape[1] // half):
+        at = slice(r * half, (r + 1) * half)
+        start = pl.multiple_of((lax.axis_index("dp") ^ r) * 2 * half, 128)
+        out_ref[:, pl.ds(start, 2 * half)] = jnp.concatenate([first[:, at], second[:, at]], axis=1)
 
 
 def place(half, kept, received):
@@ -407,7 +440,7 @@
     group_bits = [b * unit * n_dp for b in bits_of(groups)]
 
     half, piece = pick_queries(queries, groups)
-    fetched = [swap(half if r == 1 else piece, mesh, r * unit) for r in range(1, n_dp)]
+    fetched = [swap(half if r == 1 else piece, mesh, r * unit | core_bit) for r in range(1, n_dp)]
 
     own = project(activations, out_grads, proj_in, proj_out, half)
     member, live, count = masks(lengths, own)
@@ -439,10 +472,11 @@
         if step < len(steps) - 1:
             factor = factor + received
     arranged = arrange_examples(blocks, n_query)
-    arranged, received = lax.optimization_barrier((arranged, received))
+    near = split_near(queries, fetched[0])
+    arranged, near, received = lax.optimization_barrier((arranged, near, received))
     both = condition(arranged, *inverses(factor, received), queries.shape[2])
 
-    scores = score(groups, both, queries, fetched)
+    scores = score(groups, both, near, fetched[1:])
     return place(queries.shape[1] // 2, scores, swap(scores, mesh, core_bit))
 
 

time: 28.4 us -> 27.8 us (0.979)
  Pallas kernels: 10.3 us -> 9.89 us
  starting transfers between devices: 13.6 us -> 13.2 us
    pallas_call x1, Pallas kernels: 1.63 us -> 1.3 us  [inverses(): pl.pallas_call(inverses_kernel, out_shape=(shape, shape), in_specs=[pl.Bl...]
    ppermute x11, starting transfers between devices: 13.6 us -> 13.2 us  [swap(): return lax.ppermute(value, AXES, [(i, i ^ mask) for i in range(count)])]
    pallas_call x1 -> x2, Pallas kernels: 0.6 us -> 0.56 us  [the longest x1 0.49 us: score(): pl.pallas_call(functools.partial(score_kernel, groups), out_shape=jax.Sha...]
where the time goes in v6:
time: 27.8 us; the launch traced here: 27.6 us
  starting transfers between devices  13.2 us (47%)
  Pallas kernels  9.89 us (36%)
  waiting for transfers between devices  4.23 us (15%)
    ppermute x11, starting transfers between devices, swap(): return lax.ppermute(value, AXES, [(i, i ^ mask) for i in range(count)])  13.2 us
    ppermute x11, waiting for transfers between devices, swap(): return lax.ppermute(value, AXES, [(i, i ^ mask) for i in range(count)])  4.23 us
    pallas_call x1, Pallas kernels, project(): pl.pallas_call(project_kernel, out_shape=jax.ShapeDtypeStruct((2 * proj_i...  2.61 us
    pallas_call x1, Pallas kernels, inverses(): pl.pallas_call(inverses_kernel, out_shape=(shape, shape), in_specs=[pl.Bl...  1.3 us
    pallas_call x1, Pallas kernels, pick_queries(): pl.pallas_call(functools.partial(pick_kernel, groups), out_shape=tuple((j...  1.16 us
    pallas_call x1, Pallas kernels, condition(): pl.pallas_call(condition_kernel, out_shape=jax.ShapeDtypeStruct((columns...  1.15 us
    pallas_call x1, Pallas kernels, example_grads(): pl.pallas_call(examples_kernel, out_shape=jax.ShapeDtypeStruct((member.sh...  0.97 us
    pallas_call x1, Pallas kernels, place(): pl.pallas_call(functools.partial(place_kernel, half), out_shape=jax.Shape...  0.72 us
  transfers between devices with their start and end apart: 11, of which 5 were waited for; matrix products, arithmetic and copies ran while one was open for 0% of the time, Pallas kernels for 27%

profile of v6, /device:TPU:0, one launch (start us, length us, event | category | flops | bytes accessed | tf_op | source)
XLA Modules:
  0.0 27.6 jit_solution(10327315634492953527)
XLA Ops:
  0.0 1.2 %pick_queries.1 = (f32[64,1024]{1,0:T(8,128)S(1)}, f32[32,1024]{1,0:T(8,128)S(1)}) custom-call(f32[1,128,1024]{2,1,0:T(8,128)} %own_ref.1), custom_call_target="tpu_custom_call" | custom-call | flops 4000000000 | bytes 1000000 | tf_op jit(solution)/shard_map/pick_queries/pallas_call | solution.py:46
  1.2 3.6 %collective-permute-start.6 = (f32[32,1024]{1,0:T(8,128)S(1)}, f32[32,1024]{1,0:T(8,128)S(1)}, u32[]{:S(2)}, u32[]{:S(2)}) collective-permute-start(f32[32,1024]{1,0:T(8,128)S(1)} %get-tuple-element.52), channel_id=1, source_target_pairs={{0,9},{1,8},{2,11},{3,10},{4,13},{5,12},{6,15},{7,14},{8,1},{9,0},... | collective-permute-start | bytes 393224 | tf_op jit(solution)/shard_map/ppermute | solution.py:23
  4.7 1.6 %collective-permute-start.8 = (f32[32,1024]{1,0:T(8,128)S(1)}, f32[32,1024]{1,0:T(8,128)S(1)}, u32[]{:S(2)}, u32[]{:S(2)}) collective-permute-start(f32[32,1024]{1,0:T(8,128)S(1)} %get-tuple-element.52), channel_id=1, source_target_pairs={{0,13},{1,12},{2,15},{3,14},{4,9},{5,8},{6,11},{7,10},{8,5},{9,4},... | collective-permute-start | bytes 393224 | tf_op jit(solution)/shard_map/ppermute | solution.py:23
  6.4 0.2 collective-permute-start.2
  6.6 2.6 %project.1.after_ref.own_ref = f32[64,512]{1,0:T(8,128)S(1)} custom-call(bf16[512,2048]{1,0:T(8,128)(2,1)S(1)} %copy-done.1, bf16[512,7168]{1,0:T(8,128)(2,1)S(1)} %copy-done, bf16[32,2048]{1,0:T(8,128)(2,1)S(1)} %bitcast.4, bf16[32,7168]{1,0:T(8,128)(2,1)S(1)} %bitcast.3, f32[64,1024]{1,0:T(8,128)S(1)} %get-tuple-element.29.after_ref), custom_call_target="tpu_custom_call" | custom-call | tf_op jit(solution)/shard_map/project/pallas_call | solution.py:65
  9.3 0.6 %masks.1 = (bf16[16,512]{1,0:T(8,128)(2,1)S(1)}, f32[8,512]{1,0:T(8,128)S(1)}, f32[16,128]{1,0:T(8,128)S(1)}) custom-call(s32[1,17]{1,0:T(1,128)S(1)} %copy-done.5, f32[64,512]{1,0:T(8,128)S(1)} %project.1.after_ref.own_ref), custom_call_target="tpu_custom_call" | custom-call | flops 2000000000 | bytes 1000000 | tf_op jit(solution)/shard_map/masks/pallas_call | solution.py:94
  9.9 0.8 %collective-permute-done.other_ref = f32[64,512]{1,0:T(8,128)S(1)} collective-permute-done((f32[64,512]{1,0:T(8,128)S(1)}, f32[64,512]{1,0:T(8,128)S(1)}, u32[]{:S(2)}, u32[]{:S(2)}) %collective-permute-start) | collective-permute-done | bytes 131104 | tf_op jit(solution)/shard_map/ppermute | solution.py:23
  10.6 0.3 fisher.1.after_ref
  10.9 1.3 %collective-permute-start.3 = (f32[32,128]{1,0:T(8,128)S(1)}, f32[32,128]{1,0:T(8,128)S(1)}, u32[]{:S(2)}, u32[]{:S(2)}) collective-permute-start(f32[32,128]{1,0:T(8,128)S(1)} %fisher.1.after_ref), channel_id=1, source_target_pairs={{0,3},{1,2},{2,1},{3,0},{4,7},{5,6},{6,5},{7,4},{8,11},{9,10},{10,... | collective-permute-start | bytes 49160 | tf_op jit(solution)/shard_map/ppermute | solution.py:23
  12.2 1.0 %examples.1 = f32[16,1024]{1,0:T(8,128)S(1)} custom-call(bf16[16,512]{1,0:T(8,128)(2,1)S(1)} %get-tuple-element.30.member_ref, f32[16,128]{1,0:T(8,128)S(1)} %get-tuple-element.31.count_ref, f32[64,512]{1,0:T(8,128)S(1)} %project.1.after_ref.own_ref, f32[64,512]{1,0:T(8,128)S(1)} %collective-permute-done.other_ref), custom_call_target="tpu_custom_call" | custom-call | flops 2000000000 | bytes 1000000 | tf_op jit(solution)/shard_map/examples/pallas_call | solution.py:154
  13.2 0.6 %collective-permute-start.1 = (f32[1,16,1024]{2,1,0:T(8,128)S(1)}, f32[1,16,1024]{2,1,0:T(8,128)S(1)}, u32[]{:S(2)}, u32[]{:S(2)}) collective-permute-start(f32[1,16,1024]{2,1,0:T(8,128)S(1)} %hold.3), channel_id=1, source_target_pairs={{0,3},{1,2},{2,1},{3,0},{4,7},{5,6},{6,5},{7,4},{8,11},{9,10},{10,... | collective-permute-start | bytes 196616 | tf_op jit(solution)/shard_map/ppermute | solution.py:23
  13.8 0.4 %collective-permute-done.3 = f32[32,128]{1,0:T(8,128)S(1)} collective-permute-done((f32[32,128]{1,0:T(8,128)S(1)}, f32[32,128]{1,0:T(8,128)S(1)}, u32[]{:S(2)}, u32[]{:S(2)}) %collective-permute-start.3) | collective-permute-done | bytes 16416 | tf_op jit(solution)/shard_map/ppermute | solution.py:23
  14.1 2.8 %collective-permute-start.4 = (f32[32,128]{1,0:T(8,128)S(1)}, f32[32,128]{1,0:T(8,128)S(1)}, u32[]{:S(2)}, u32[]{:S(2)}) collective-permute-start(f32[32,128]{1,0:T(8,128)S(1)} %add.6.after_ref), channel_id=1, source_target_pairs={{0,9},{1,8},{2,11},{3,10},{4,13},{5,12},{6,15},{7,14},{8,1},{9,0},... | collective-permute-start | bytes 49160 | tf_op jit(solution)/shard_map/ppermute | solution.py:23
  17.0 1.6 %collective-permute-start.7 = (f32[32,1024]{1,0:T(8,128)S(1)}, f32[32,1024]{1,0:T(8,128)S(1)}, u32[]{:S(2)}, u32[]{:S(2)}) collective-permute-start(f32[32,1024]{1,0:T(8,128)S(1)} %hold.4), channel_id=1, source_target_pairs={{0,16},{1,17},{2,18},{3,19},{4,20},{5,21},{6,22},{7,23},{8,24},{9,... | collective-permute-start | bytes 393224 | tf_op jit(solution)/shard_map/ppermute | solution.py:23
  18.6 0.6 %collective-permute-start.9 = (f32[32,1024]{1,0:T(8,128)S(1)}, f32[32,1024]{1,0:T(8,128)S(1)}, u32[]{:S(2)}, u32[]{:S(2)}) collective-permute-start(f32[32,1024]{1,0:T(8,128)S(1)} %hold.5), channel_id=1, source_target_pairs={{0,16},{1,17},{2,18},{3,19},{4,20},{5,21},{6,22},{7,23},{8,24},{9,... | collective-permute-start | bytes 393224 | tf_op jit(solution)/shard_map/ppermute | solution.py:23
  19.1 0.9 %collective-permute-start.5 = (f32[32,128]{1,0:T(8,128)S(1)}, f32[32,128]{1,0:T(8,128)S(1)}, u32[]{:S(2)}, u32[]{:S(2)}) collective-permute-start(f32[32,128]{1,0:T(8,128)S(1)} %add.7.own_ref), channel_id=1, source_target_pairs={{0,5},{1,4},{2,7},{3,6},{4,1},{5,0},{6,3},{7,2},{8,13},{9,12},{10,... | collective-permute-start | bytes 49160 | tf_op jit(solution)/shard_map/ppermute | solution.py:23
  20.0 0.6 %arrange_examples.1 = (bf16[128,256]{1,0:T(8,128)(2,1)S(1)}, bf16[128,256]{1,0:T(8,128)(2,1)S(1)}, bf16[128,256]{1,0:T(8,128)(2,1)S(1)}) custom-call(f32[2,16,1024]{2,1,0:T(8,128)S(1)} %pad_maximum_fusion.2.blocks_ref), custom_call_target="tpu_custom_call" | custom-call | tf_op jit(solution)/shard_map/arrange_examples/pallas_call | solution.py:198
  20.7 1.7 %collective-permute-done.5.other_ref = f32[32,128]{1,0:T(8,128)S(1)} collective-permute-done((f32[32,128]{1,0:T(8,128)S(1)}, f32[32,128]{1,0:T(8,128)S(1)}, u32[]{:S(2)}, u32[]{:S(2)}) %collective-permute-start.5) | collective-permute-done | bytes 16416 | tf_op jit(solution)/shard_map/ppermute | solution.py:23
  22.4 1.3 %inverses.1 = (bf16[3,256,256]{2,1,0:T(8,128)(2,1)S(1)}, bf16[3,256,256]{2,1,0:T(8,128)(2,1)S(1)}) custom-call(f32[32,128]{1,0:T(8,128)S(1)} %add.7.own_ref, f32[32,128]{1,0:T(8,128)S(1)} %collective-permute-done.5.other_ref), custom_call_target="tpu_custom_call" | custom-call | tf_op jit(solution)/shard_map/inverses/pallas_call | solution.py:312
  23.7 1.1 %condition.1.both_ref = bf16[4,64,256]{2,1,0:T(8,128)(2,1)S(1)} custom-call(bf16[128,256]{1,0:T(8,128)(2,1)S(1)} %get-tuple-element.44.high_ref, bf16[128,256]{1,0:T(8,128)(2,1)S(1)} %get-tuple-element.45.middle_ref, bf16[128,256]{1,0:T(8,128)(2,1)S(1)} %get-tuple-element.46.low_ref, bf16[3,256,256]{2,1,0:T(8,128)(2,1)S(1)} %get-tuple-element.48.in_ref, ...), custom_call_target="tpu_custom_call" | custom-call | flops 2000000000 | bytes 1000000 | tf_op jit(solution)/shard_map/condition/pallas_call | solution.py:343
  24.9 0.2 collective-permute-done.9
  25.1 0.5 %score.1.kept_ref = f32[32,256]{1,0:T(8,128)S(1)} custom-call(bf16[4,64,256]{2,1,0:T(8,128)(2,1)S(1)} %condition.1.both_ref, bf16[128,1024]{1,0:T(8,128)(2,1)S(1)} %get-tuple-element.50.near_high_ref, bf16[128,1024]{1,0:T(8,128)(2,1)S(1)} %get-tuple-element.51.near_low_ref, f32[64,1024]{1,0:T(8,128)S(1)} %pad_maximum_fusion.refs_0_, ...), custom_call_target="tpu_custom_call" | custom-call | tf_op jit(solution)/shard_map/score/pallas_call | solution.py:379
  25.7 1.2 %collective-permute-done.10.received_ref = f32[32,256]{1,0:T(8,128)S(1)} collective-permute-done((f32[32,256]{1,0:T(8,128)S(1)}, f32[32,256]{1,0:T(8,128)S(1)}, u32[]{:S(2)}, u32[]{:S(2)}) %collective-permute-start.10) | collective-permute-done | bytes 32800 | tf_op jit(solution)/shard_map/ppermute | solution.py:23
  26.9 0.7 %place.1 = f32[32,512]{1,0:T(8,128)} custom-call(f32[32,256]{1,0:T(8,128)S(1)} %score.1.kept_ref, f32[32,256]{1,0:T(8,128)S(1)} %collective-permute-done.10.received_ref), custom_call_target="tpu_custom_call" | custom-call | tf_op jit(solution)/shard_map/place/pallas_call | solution.py:403
  (29 shorter events, 0.3 us)
Async XLA Ops:
  0.0 6.6 %copy-start.1 = (bf16[512,2048]{1,0:T(8,128)(2,1)S(1)}, bf16[512,2048]{1,0:T(8,128)(2,1)}, u32[]{:S(2)}) copy-start(bf16[512,2048]{1,0:T(8,128)(2,1)} %a_ref.1) | copy-start | bytes 6291460
  0.0 6.6 %copy-start = (bf16[512,7168]{1,0:T(8,128)(2,1)S(1)}, bf16[512,7168]{1,0:T(8,128)(2,1)}, u32[]{:S(2)}) copy-start(bf16[512,7168]{1,0:T(8,128)(2,1)} %g_ref.1) | copy-start | bytes 22020100
  0.0 6.6 %copy-start.4 = (bf16[2048,32]{0,1:T(8,128)(2,1)S(1)}, bf16[2048,32]{0,1:T(8,128)(2,1)}, u32[]{:S(2)}) copy-start(bf16[2048,32]{0,1:T(8,128)(2,1)} %param.8) | copy-start | bytes 393220
  0.0 6.6 %copy-start.3 = (bf16[7168,32]{0,1:T(8,128)(2,1)S(1)}, bf16[7168,32]{0,1:T(8,128)(2,1)}, u32[]{:S(2)}) copy-start(bf16[7168,32]{0,1:T(8,128)(2,1)} %param.9) | copy-start | bytes 1376260
  1.2 8.1 %copy-start.5 = (s32[1,17]{1,0:T(1,128)S(1)}, s32[1,17]{1,0:T(1,128)}, u32[]{:S(2)}) copy-start(s32[1,17]{1,0:T(1,128)} %lengths_ref.1) | copy-start | bytes 208
  1.2 15.8 %collective-permute-start.6 = (f32[32,1024]{1,0:T(8,128)S(1)}, f32[32,1024]{1,0:T(8,128)S(1)}, u32[]{:S(2)}, u32[]{:S(2)}) collective-permute-start(f32[32,1024]{1,0:T(8,128)S(1)} %get-tuple-element.52), channel_id=1, source_target_pairs={{0,9},{1,8},{2,11},{3,10},{4,13},{5,12},{6,15},{7,14},{8,1},{9,0},... | collective-permute-start | bytes 393224 | tf_op jit(solution)/shard_map/ppermute | solution.py:23
  4.7 13.8 %collective-permute-start.8 = (f32[32,1024]{1,0:T(8,128)S(1)}, f32[32,1024]{1,0:T(8,128)S(1)}, u32[]{:S(2)}, u32[]{:S(2)}) collective-permute-start(f32[32,1024]{1,0:T(8,128)S(1)} %get-tuple-element.52), channel_id=1, source_target_pairs={{0,13},{1,12},{2,15},{3,14},{4,9},{5,8},{6,11},{7,10},{8,5},{9,4},... | collective-permute-start | bytes 393224 | tf_op jit(solution)/shard_map/ppermute | solution.py:23
  6.4 14.2 %collective-permute-start.2 = (f32[64,1024]{1,0:T(8,128)S(1)}, f32[64,1024]{1,0:T(8,128)S(1)}, u32[]{:S(2)}, u32[]{:S(2)}) collective-permute-start(f32[64,1024]{1,0:T(8,128)S(1)} %get-tuple-element.29.after_ref), channel_id=1, source_target_pairs={{0,5},{1,4},{2,7},{3,6},{4,1},{5,0},{6,3},{7,2},{8,13},{9,12},{10,... | collective-permute-start | bytes 786440 | tf_op jit(solution)/shard_map/ppermute | solution.py:23
  9.2 1.4 %collective-permute-start = (f32[64,512]{1,0:T(8,128)S(1)}, f32[64,512]{1,0:T(8,128)S(1)}, u32[]{:S(2)}, u32[]{:S(2)}) collective-permute-start(f32[64,512]{1,0:T(8,128)S(1)} %project.1.after_ref.own_ref), channel_id=1, source_target_pairs={{0,1},{1,0},{2,3},{3,2},{4,5},{5,4},{6,7},{7,6},{8,9},{9,8},{10,11... | collective-permute-start | bytes 393224 | tf_op jit(solution)/shard_map/ppermute | solution.py:23
  10.9 3.2 %collective-permute-start.3 = (f32[32,128]{1,0:T(8,128)S(1)}, f32[32,128]{1,0:T(8,128)S(1)}, u32[]{:S(2)}, u32[]{:S(2)}) collective-permute-start(f32[32,128]{1,0:T(8,128)S(1)} %fisher.1.after_ref), channel_id=1, source_target_pairs={{0,3},{1,2},{2,1},{3,0},{4,7},{5,6},{6,5},{7,4},{8,11},{9,10},{10,... | collective-permute-start | bytes 49160 | tf_op jit(solution)/shard_map/ppermute | solution.py:23
  13.2 7.4 %copy-start.2 = (f32[1,128,1024]{2,1,0:T(8,128)S(1)}, f32[1,128,1024]{2,1,0:T(8,128)}, u32[]{:S(2)}) copy-start(f32[1,128,1024]{2,1,0:T(8,128)} %own_ref.1) | copy-start | bytes 1572868
  13.2 6.8 %collective-permute-start.1 = (f32[1,16,1024]{2,1,0:T(8,128)S(1)}, f32[1,16,1024]{2,1,0:T(8,128)S(1)}, u32[]{:S(2)}, u32[]{:S(2)}) collective-permute-start(f32[1,16,1024]{2,1,0:T(8,128)S(1)} %hold.3), channel_id=1, source_target_pairs={{0,3},{1,2},{2,1},{3,0},{4,7},{5,6},{6,5},{7,4},{8,11},{9,10},{10,... | collective-permute-start | bytes 196616 | tf_op jit(solution)/shard_map/ppermute | solution.py:23
  14.1 5.0 %collective-permute-start.4 = (f32[32,128]{1,0:T(8,128)S(1)}, f32[32,128]{1,0:T(8,128)S(1)}, u32[]{:S(2)}, u32[]{:S(2)}) collective-permute-start(f32[32,128]{1,0:T(8,128)S(1)} %add.6.after_ref), channel_id=1, source_target_pairs={{0,9},{1,8},{2,11},{3,10},{4,13},{5,12},{6,15},{7,14},{8,1},{9,0},... | collective-permute-start | bytes 49160 | tf_op jit(solution)/shard_map/ppermute | solution.py:23
  17.0 7.9 %collective-permute-start.7 = (f32[32,1024]{1,0:T(8,128)S(1)}, f32[32,1024]{1,0:T(8,128)S(1)}, u32[]{:S(2)}, u32[]{:S(2)}) collective-permute-start(f32[32,1024]{1,0:T(8,128)S(1)} %hold.4), channel_id=1, source_target_pairs={{0,16},{1,17},{2,18},{3,19},{4,20},{5,21},{6,22},{7,23},{8,24},{9,... | collective-permute-start | bytes 393224 | tf_op jit(solution)/shard_map/ppermute | solution.py:23
  18.6 6.5 %collective-permute-start.9 = (f32[32,1024]{1,0:T(8,128)S(1)}, f32[32,1024]{1,0:T(8,128)S(1)}, u32[]{:S(2)}, u32[]{:S(2)}) collective-permute-start(f32[32,1024]{1,0:T(8,128)S(1)} %hold.5), channel_id=1, source_target_pairs={{0,16},{1,17},{2,18},{3,19},{4,20},{5,21},{6,22},{7,23},{8,24},{9,... | collective-permute-start | bytes 393224 | tf_op jit(solution)/shard_map/ppermute | solution.py:23
  19.1 3.2 %collective-permute-start.5 = (f32[32,128]{1,0:T(8,128)S(1)}, f32[32,128]{1,0:T(8,128)S(1)}, u32[]{:S(2)}, u32[]{:S(2)}) collective-permute-start(f32[32,128]{1,0:T(8,128)S(1)} %add.7.own_ref), channel_id=1, source_target_pairs={{0,5},{1,4},{2,7},{3,6},{4,1},{5,0},{6,3},{7,2},{8,13},{9,12},{10,... | collective-permute-start | bytes 49160 | tf_op jit(solution)/shard_map/ppermute | solution.py:23
  25.6 1.3 %collective-permute-start.10 = (f32[32,256]{1,0:T(8,128)S(1)}, f32[32,256]{1,0:T(8,128)S(1)}, u32[]{:S(2)}, u32[]{:S(2)}) collective-permute-start(f32[32,256]{1,0:T(8,128)S(1)} %score.1.kept_ref), channel_id=1, source_target_pairs={{0,1},{1,0},{2,3},{3,2},{4,5},{5,4},{6,7},{7,6},{8,9},{9,8},{10,11... | collective-permute-start | bytes 98312 | tf_op jit(solution)/shard_map/ppermute | solution.py:23

commit v7 on v6

--- a/solution.py
+++ b/solution.py
@@ -299,26 +299,6 @@
     return jnp.where(row == column, value, 0.0)
 
 
-def inverses_kernel(own_ref, other_ref, in_ref, out_ref):
-    width = own_ref.shape[0]
-    total = own_ref[...] + other_ref[...]
-    for ref, inverse in zip((in_ref, out_ref), inverse_pair(total[:, 0 : 2 * width])):
-        for piece, value in enumerate(split3(block_diagonal(inverse))):
-            ref[piece] = value
-
-
-def inverses(own, other):
-    shape = jax.ShapeDtypeStruct((3, CHUNK, CHUNK), BF16)
-    return pl.pallas_call(
-        inverses_kernel,
-        out_shape=(shape, shape),
-        in_specs=[pl.BlockSpec(memory_space=pltpu.VMEM)] * 2,
-        out_specs=(pl.BlockSpec(memory_space=pltpu.VMEM),) * 2,
-        compiler_params=pltpu.CompilerParams(vmem_limit_bytes=8 * MIB),
-        name="inverses",
-    )(own, other)
-
-
 def times_blocks(high, middle, low, blocks_ref):
     rows = high.shape[0]
     by_high = jnp.dot(jnp.concatenate([high, middle, low], axis=0), blocks_ref[0], preferred_element_type=F32)
@@ -328,34 +308,55 @@
     return by_high[0:rows] + (by_high[rows : 2 * rows] + by_middle[0:rows] + small)
 
 
-def condition_kernel(high_ref, middle_ref, low_ref, in_ref, out_ref, both_ref, scratch):
+def times_queries(both_ref, high_ref, low_ref):
+    chunks, count = both_ref.shape[0], both_ref.shape[1] // 2
+    total = None
+    for c in range(chunks):
+        cols = slice(c * CHUNK, (c + 1) * CHUNK)
+        by_high = lax.dot_general(both_ref[c], high_ref[:, cols], NT, preferred_element_type=F32)
+        by_low = lax.dot_general(both_ref[c, 0:count], low_ref[:, cols], NT, preferred_element_type=F32)
+        part = by_high[0:count] + (by_high[count:] + by_low)
+        total = part if total is None else total + part
+    return total * (1.0 / math.isqrt(chunks * CHUNK))
+
+
+def condition_kernel(own_ref, other_ref, high_ref, middle_ref, low_ref, near_high_ref, near_low_ref, both_ref, near_ref, in_ref, out_ref, scratch):
     columns, count = scratch.shape
+    width = own_ref.shape[0]
+    total = own_ref[...] + other_ref[...]
+    for ref, inverse in zip((in_ref, out_ref), inverse_pair(total[:, 0 : 2 * width])):
+        for piece, value in enumerate(split3(block_diagonal(inverse))):
+            ref[piece] = value
     left = times_blocks(high_ref[...], middle_ref[...], low_ref[...], out_ref)
-    turned = turn_pairs(lambda c: left[c * count : (c + 1) * count], scratch, math.isqrt(columns))
+    turned = turn_pairs(lambda c: left[c * count : (c + 1) * count], scratch, width)
     high, low = split2(times_blocks(*split3(turned), in_ref))
     for c in range(columns // CHUNK):
         both_ref[c, 0:count] = high[c * count : (c + 1) * count]
         both_ref[c, count:] = low[c * count : (c + 1) * count]
-
-
-def condition(pieces, in_blocks, out_blocks, columns):
+    near_ref[...] = times_queries(both_ref, near_high_ref, near_low_ref)
+
+
+def condition(own, other, pieces, near):
+    columns = near[0].shape[1]
     count = pieces[0].shape[0] * CHUNK // columns
     return pl.pallas_call(
         condition_kernel,
-        out_shape=jax.ShapeDtypeStruct((columns // CHUNK, 2 * count, CHUNK), BF16),
-        in_specs=[pl.BlockSpec(memory_space=pltpu.VMEM)] * 5,
-        out_specs=pl.BlockSpec(memory_space=pltpu.VMEM),
-        scratch_shapes=[pltpu.VMEM((columns, count), F32)],
-        compiler_params=pltpu.CompilerParams(vmem_limit_bytes=8 * MIB),
-        cost_estimate=pl.CostEstimate(flops=2 * 10**9, bytes_accessed=10**6, transcendentals=0),
+        out_shape=(
+            jax.ShapeDtypeStruct((columns // CHUNK, 2 * count, CHUNK), BF16),
+            jax.ShapeDtypeStruct((count, near[0].shape[0]), F32),
+        ),
+        in_specs=[pl.BlockSpec(memory_space=pltpu.VMEM)] * 7,
+        out_specs=(pl.BlockSpec(memory_space=pltpu.VMEM),) * 2,
+        scratch_shapes=[pltpu.VMEM((3, CHUNK, CHUNK), BF16)] * 2 + [pltpu.VMEM((columns, count), F32)],
+        compiler_params=pltpu.CompilerParams(vmem_limit_bytes=12 * MIB),
+        cost_estimate=pl.CostEstimate(flops=4 * 10**9, bytes_accessed=10**6, transcendentals=0),
         name="condition",
-    )(*pieces, in_blocks, out_blocks)
-
-
-def score_kernel(groups, both_ref, near_high_ref, near_low_ref, *refs):
+    )(own, other, *pieces, *near)
+
+
+def score_kernel(groups, both_ref, near_ref, *refs):
     fetched_refs, (scores_ref, high_ref, low_ref) = refs[:-3], refs[-3:]
-    chunks, count = both_ref.shape[0], both_ref.shape[1] // 2
-    near = near_high_ref.shape[0]
+    near = near_ref.shape[1]
     half = fetched_refs[0].shape[0]
     piece = half // groups
     group = lax.axis_index("grp")
@@ -363,28 +364,21 @@
         for g in range(groups):
             at = pl.ds(pl.multiple_of(i * half + (group ^ g) * piece, 16), piece)
             high_ref[at, :], low_ref[at, :] = split2(ref[g * piece : (g + 1) * piece, :])
-    for start, q_high_ref, q_low_ref in ((0, near_high_ref, near_low_ref), (near, high_ref, low_ref)):
-        total = None
-        for c in range(chunks):
-            cols = slice(c * CHUNK, (c + 1) * CHUNK)
-            by_high = lax.dot_general(both_ref[c], q_high_ref[:, cols], NT, preferred_element_type=F32)
-            by_low = lax.dot_general(both_ref[c, 0:count], q_low_ref[:, cols], NT, preferred_element_type=F32)
-            part = by_high[0:count] + (by_high[count:] + by_low)
-            total = part if total is None else total + part
-        scores_ref[:, start : start + total.shape[1]] = total * (1.0 / math.isqrt(chunks * CHUNK))
+    scores_ref[:, 0:near] = near_ref[...]
+    scores_ref[:, near:] = times_queries(both_ref, high_ref, low_ref)
 
 
 def score(groups, both, near, fetched):
     rows, columns = len(fetched) * fetched[0].shape[0], fetched[0].shape[1]
     return pl.pallas_call(
         functools.partial(score_kernel, groups),
-        out_shape=jax.ShapeDtypeStruct((both.shape[1] // 2, near[0].shape[0] + rows), F32),
-        in_specs=[pl.BlockSpec(memory_space=pltpu.VMEM)] * (3 + len(fetched)),
+        out_shape=jax.ShapeDtypeStruct((near.shape[0], near.shape[1] + rows), F32),
+        in_specs=[pl.BlockSpec(memory_space=pltpu.VMEM)] * (2 + len(fetched)),
         out_specs=pl.BlockSpec(memory_space=pltpu.VMEM),
         scratch_shapes=[pltpu.VMEM((rows, columns), BF16)] * 2,
         compiler_params=pltpu.CompilerParams(vmem_limit_bytes=(8 + len(fetched)) * MIB),
         name="score",
-    )(both, *near, *fetched)
+    )(both, near, *fetched)
 
 
 def place_kernel(half, kept_ref, received_ref, out_ref):
@@ -474,7 +468,7 @@
     arranged = arrange_examples(blocks, n_query)
     near = split_near(queries, fetched[0])
     arranged, near, received = lax.optimization_barrier((arranged, near, received))
-    both = condition(arranged, *inverses(factor, received), queries.shape[2])
+    both, near = condition(factor, received, arranged, near)
 
     scores = score(groups, both, near, fetched[1:])
     return place(queries.shape[1] // 2, scores, swap(scores, mesh, core_bit))

time: 27.8 us -> 27.6 us (level)
    pallas_call x2 -> x1, Pallas kernels: 2.45 us -> 2.54 us  [condition(): pl.pallas_call(condition_kernel, out_shape=(jax.ShapeDtypeStruct((columns...]
  transfers between devices with their start and end apart: 11 -> 11, of which waited for: 5 -> 5; matrix products, arithmetic and copies ran while one was open for 0% -> 0% of each run, Pallas kernels for 27% -> 28%
where the time goes in v7:
time: 27.6 us; the launch traced here: 27.4 us
  starting transfers between devices  13.2 us (48%)
  Pallas kernels  9.83 us (36%)
  waiting for transfers between devices  4.16 us (15%)
    ppermute x11, starting transfers between devices, swap(): return lax.ppermute(value, AXES, [(i, i ^ mask) for i in range(count)])  13.2 us
    ppermute x11, waiting for transfers between devices, swap(): return lax.ppermute(value, AXES, [(i, i ^ mask) for i in range(count)])  4.16 us
    pallas_call x1, Pallas kernels, project(): pl.pallas_call(project_kernel, out_shape=jax.ShapeDtypeStruct((2 * proj_i...  2.61 us
    pallas_call x1, Pallas kernels, condition(): pl.pallas_call(condition_kernel, out_shape=(jax.ShapeDtypeStruct((columns...  2.54 us
    pallas_call x1, Pallas kernels, pick_queries(): pl.pallas_call(functools.partial(pick_kernel, groups), out_shape=tuple((j...  1.16 us
    pallas_call x1, Pallas kernels, example_grads(): pl.pallas_call(examples_kernel, out_shape=jax.ShapeDtypeStruct((member.sh...  0.97 us
    pallas_call x1, Pallas kernels, place(): pl.pallas_call(functools.partial(place_kernel, half), out_shape=jax.Shape...  0.72 us
    pallas_call x1, Pallas kernels, masks(): pl.pallas_call(masks_kernel, out_shape=(jax.ShapeDtypeStruct((examples, s...  0.56 us
  transfers between devices with their start and end apart: 11, of which 5 were waited for; matrix products, arithmetic and copies ran while one was open for 0% of the time, Pallas kernels for 28%

profile of v7, /device:TPU:0, one launch (start us, length us, event | category | flops | bytes accessed | tf_op | source)
XLA Modules:
  0.0 27.4 jit_solution(16307603198680703089)
XLA Ops:
  0.0 1.2 %pick_queries.1 = (f32[64,1024]{1,0:T(8,128)S(1)}, f32[32,1024]{1,0:T(8,128)S(1)}) custom-call(f32[1,128,1024]{2,1,0:T(8,128)} %own_ref.1), custom_call_target="tpu_custom_call" | custom-call | flops 4000000000 | bytes 1000000 | tf_op jit(solution)/shard_map/pick_queries/pallas_call | solution.py:46
  1.2 3.6 %collective-permute-start.6 = (f32[32,1024]{1,0:T(8,128)S(1)}, f32[32,1024]{1,0:T(8,128)S(1)}, u32[]{:S(2)}, u32[]{:S(2)}) collective-permute-start(f32[32,1024]{1,0:T(8,128)S(1)} %get-tuple-element.52), channel_id=1, source_target_pairs={{0,9},{1,8},{2,11},{3,10},{4,13},{5,12},{6,15},{7,14},{8,1},{9,0},... | collective-permute-start | bytes 393224 | tf_op jit(solution)/shard_map/ppermute | solution.py:23
  4.7 1.6 %collective-permute-start.8 = (f32[32,1024]{1,0:T(8,128)S(1)}, f32[32,1024]{1,0:T(8,128)S(1)}, u32[]{:S(2)}, u32[]{:S(2)}) collective-permute-start(f32[32,1024]{1,0:T(8,128)S(1)} %get-tuple-element.52), channel_id=1, source_target_pairs={{0,13},{1,12},{2,15},{3,14},{4,9},{5,8},{6,11},{7,10},{8,5},{9,4},... | collective-permute-start | bytes 393224 | tf_op jit(solution)/shard_map/ppermute | solution.py:23
  6.4 0.2 collective-permute-start.4
  6.6 2.6 %project.1.after_ref.own_ref = f32[64,512]{1,0:T(8,128)S(1)} custom-call(bf16[512,2048]{1,0:T(8,128)(2,1)S(1)} %copy-done.1, bf16[512,7168]{1,0:T(8,128)(2,1)S(1)} %copy-done, bf16[32,2048]{1,0:T(8,128)(2,1)S(1)} %bitcast.4, bf16[32,7168]{1,0:T(8,128)(2,1)S(1)} %bitcast.3, f32[64,1024]{1,0:T(8,128)S(1)} %get-tuple-element.29.after_ref), custom_call_target="tpu_custom_call" | custom-call | tf_op jit(solution)/shard_map/project/pallas_call | solution.py:65
  9.3 0.6 %masks.1 = (bf16[16,512]{1,0:T(8,128)(2,1)S(1)}, f32[8,512]{1,0:T(8,128)S(1)}, f32[16,128]{1,0:T(8,128)S(1)}) custom-call(s32[1,17]{1,0:T(1,128)S(1)} %copy-done.5, f32[64,512]{1,0:T(8,128)S(1)} %project.1.after_ref.own_ref), custom_call_target="tpu_custom_call" | custom-call | flops 2000000000 | bytes 1000000 | tf_op jit(solution)/shard_map/masks/pallas_call | solution.py:94
  9.9 0.8 %collective-permute-done.other_ref = f32[64,512]{1,0:T(8,128)S(1)} collective-permute-done((f32[64,512]{1,0:T(8,128)S(1)}, f32[64,512]{1,0:T(8,128)S(1)}, u32[]{:S(2)}, u32[]{:S(2)}) %collective-permute-start) | collective-permute-done | bytes 131104 | tf_op jit(solution)/shard_map/ppermute | solution.py:23
  10.6 0.3 fisher.1.after_ref
  10.9 1.3 %collective-permute-start.1 = (f32[32,128]{1,0:T(8,128)S(1)}, f32[32,128]{1,0:T(8,128)S(1)}, u32[]{:S(2)}, u32[]{:S(2)}) collective-permute-start(f32[32,128]{1,0:T(8,128)S(1)} %fisher.1.after_ref), channel_id=1, source_target_pairs={{0,3},{1,2},{2,1},{3,0},{4,7},{5,6},{6,5},{7,4},{8,11},{9,10},{10,... | collective-permute-start | bytes 49160 | tf_op jit(solution)/shard_map/ppermute | solution.py:23
  12.2 1.0 %examples.1 = f32[16,1024]{1,0:T(8,128)S(1)} custom-call(bf16[16,512]{1,0:T(8,128)(2,1)S(1)} %get-tuple-element.35.member_ref, f32[16,128]{1,0:T(8,128)S(1)} %get-tuple-element.36.count_ref, f32[64,512]{1,0:T(8,128)S(1)} %project.1.after_ref.own_ref, f32[64,512]{1,0:T(8,128)S(1)} %collective-permute-done.other_ref), custom_call_target="tpu_custom_call" | custom-call | flops 2000000000 | bytes 1000000 | tf_op jit(solution)/shard_map/examples/pallas_call | solution.py:154
  13.2 0.6 %collective-permute-start.3 = (f32[1,16,1024]{2,1,0:T(8,128)S(1)}, f32[1,16,1024]{2,1,0:T(8,128)S(1)}, u32[]{:S(2)}, u32[]{:S(2)}) collective-permute-start(f32[1,16,1024]{2,1,0:T(8,128)S(1)} %hold.3), channel_id=1, source_target_pairs={{0,3},{1,2},{2,1},{3,0},{4,7},{5,6},{6,5},{7,4},{8,11},{9,10},{10,... | collective-permute-start | bytes 196616 | tf_op jit(solution)/shard_map/ppermute | solution.py:23
  13.8 0.4 %collective-permute-done.1 = f32[32,128]{1,0:T(8,128)S(1)} collective-permute-done((f32[32,128]{1,0:T(8,128)S(1)}, f32[32,128]{1,0:T(8,128)S(1)}, u32[]{:S(2)}, u32[]{:S(2)}) %collective-permute-start.1) | collective-permute-done | bytes 16416 | tf_op jit(solution)/shard_map/ppermute | solution.py:23
  14.1 2.8 %collective-permute-start.2 = (f32[32,128]{1,0:T(8,128)S(1)}, f32[32,128]{1,0:T(8,128)S(1)}, u32[]{:S(2)}, u32[]{:S(2)}) collective-permute-start(f32[32,128]{1,0:T(8,128)S(1)} %add.6.after_ref), channel_id=1, source_target_pairs={{0,9},{1,8},{2,11},{3,10},{4,13},{5,12},{6,15},{7,14},{8,1},{9,0},... | collective-permute-start | bytes 49160 | tf_op jit(solution)/shard_map/ppermute | solution.py:23
  17.0 1.6 %collective-permute-start.7 = (f32[32,1024]{1,0:T(8,128)S(1)}, f32[32,1024]{1,0:T(8,128)S(1)}, u32[]{:S(2)}, u32[]{:S(2)}) collective-permute-start(f32[32,1024]{1,0:T(8,128)S(1)} %hold.4), channel_id=1, source_target_pairs={{0,16},{1,17},{2,18},{3,19},{4,20},{5,21},{6,22},{7,23},{8,24},{9,... | collective-permute-start | bytes 393224 | tf_op jit(solution)/shard_map/ppermute | solution.py:23
  18.6 0.6 %collective-permute-start.9 = (f32[32,1024]{1,0:T(8,128)S(1)}, f32[32,1024]{1,0:T(8,128)S(1)}, u32[]{:S(2)}, u32[]{:S(2)}) collective-permute-start(f32[32,1024]{1,0:T(8,128)S(1)} %hold.5), channel_id=1, source_target_pairs={{0,16},{1,17},{2,18},{3,19},{4,20},{5,21},{6,22},{7,23},{8,24},{9,... | collective-permute-start | bytes 393224 | tf_op jit(solution)/shard_map/ppermute | solution.py:23
  19.1 0.9 %collective-permute-start.5 = (f32[32,128]{1,0:T(8,128)S(1)}, f32[32,128]{1,0:T(8,128)S(1)}, u32[]{:S(2)}, u32[]{:S(2)}) collective-permute-start(f32[32,128]{1,0:T(8,128)S(1)} %add.7.own_ref), channel_id=1, source_target_pairs={{0,5},{1,4},{2,7},{3,6},{4,1},{5,0},{6,3},{7,2},{8,13},{9,12},{10,... | collective-permute-start | bytes 49160 | tf_op jit(solution)/shard_map/ppermute | solution.py:23
  20.0 0.6 %arrange_examples.1 = (bf16[128,256]{1,0:T(8,128)(2,1)S(1)}, bf16[128,256]{1,0:T(8,128)(2,1)S(1)}, bf16[128,256]{1,0:T(8,128)(2,1)S(1)}) custom-call(f32[2,16,1024]{2,1,0:T(8,128)S(1)} %pad_maximum_fusion.2.blocks_ref), custom_call_target="tpu_custom_call" | custom-call | tf_op jit(solution)/shard_map/arrange_examples/pallas_call | solution.py:198
  20.6 0.1 split_near.1
  20.7 1.7 %collective-permute-done.5.other_ref = f32[32,128]{1,0:T(8,128)S(1)} collective-permute-done((f32[32,128]{1,0:T(8,128)S(1)}, f32[32,128]{1,0:T(8,128)S(1)}, u32[]{:S(2)}, u32[]{:S(2)}) %collective-permute-start.5) | collective-permute-done | bytes 16416 | tf_op jit(solution)/shard_map/ppermute | solution.py:23
  22.4 2.5 %condition.1 = (bf16[4,64,256]{2,1,0:T(8,128)(2,1)S(1)}, f32[32,128]{1,0:T(8,128)S(1)}) custom-call(f32[32,128]{1,0:T(8,128)S(1)} %add.7.own_ref, f32[32,128]{1,0:T(8,128)S(1)} %collective-permute-done.5.other_ref, bf16[128,256]{1,0:T(8,128)(2,1)S(1)} %get-tuple-element.45.high_ref, bf16[128,256]{1,0:T(8,128)(2,1)S(1)} %get-tuple-element.46.middle_ref, ...), custom_call_target="tpu_custom_call" | custom-call | flops 4000000000 | bytes 1000000 | tf_op jit(solution)/shard_map/condition/pallas_call | solution.py:342
  25.0 0.1 collective-permute-done.9
  25.1 0.3 %score.1.kept_ref = f32[32,256]{1,0:T(8,128)S(1)} custom-call(bf16[4,64,256]{2,1,0:T(8,128)(2,1)S(1)} %get-tuple-element.50.both_ref, f32[32,128]{1,0:T(8,128)S(1)} %get-tuple-element.51.near_ref, f32[64,1024]{1,0:T(8,128)S(1)} %pad_maximum_fusion.refs_0_, f32[64,1024]{1,0:T(8,128)S(1)} %pad_maximum_fusion.1.refs_1_), custom_call_target="tpu_custom_call" | custom-call | tf_op jit(solution)/shard_map/score/pallas_call | solution.py:373
  25.5 1.2 %collective-permute-done.10.received_ref = f32[32,256]{1,0:T(8,128)S(1)} collective-permute-done((f32[32,256]{1,0:T(8,128)S(1)}, f32[32,256]{1,0:T(8,128)S(1)}, u32[]{:S(2)}, u32[]{:S(2)}) %collective-permute-start.10) | collective-permute-done | bytes 32800 | tf_op jit(solution)/shard_map/ppermute | solution.py:23
  26.7 0.7 %place.1 = f32[32,512]{1,0:T(8,128)} custom-call(f32[32,256]{1,0:T(8,128)S(1)} %score.1.kept_ref, f32[32,256]{1,0:T(8,128)S(1)} %collective-permute-done.10.received_ref), custom_call_target="tpu_custom_call" | custom-call | tf_op jit(solution)/shard_map/place/pallas_call | solution.py:397
  (28 shorter events, 0.2 us)
Async XLA Ops:
  0.0 6.6 %copy-start.1 = (bf16[512,2048]{1,0:T(8,128)(2,1)S(1)}, bf16[512,2048]{1,0:T(8,128)(2,1)}, u32[]{:S(2)}) copy-start(bf16[512,2048]{1,0:T(8,128)(2,1)} %a_ref.1) | copy-start | bytes 6291460
  0.0 6.6 %copy-start = (bf16[512,7168]{1,0:T(8,128)(2,1)S(1)}, bf16[512,7168]{1,0:T(8,128)(2,1)}, u32[]{:S(2)}) copy-start(bf16[512,7168]{1,0:T(8,128)(2,1)} %g_ref.1) | copy-start | bytes 22020100
  0.0 6.6 %copy-start.4 = (bf16[2048,32]{0,1:T(8,128)(2,1)S(1)}, bf16[2048,32]{0,1:T(8,128)(2,1)}, u32[]{:S(2)}) copy-start(bf16[2048,32]{0,1:T(8,128)(2,1)} %param.8) | copy-start | bytes 393220
  0.0 6.6 %copy-start.3 = (bf16[7168,32]{0,1:T(8,128)(2,1)S(1)}, bf16[7168,32]{0,1:T(8,128)(2,1)}, u32[]{:S(2)}) copy-start(bf16[7168,32]{0,1:T(8,128)(2,1)} %param.9) | copy-start | bytes 1376260
  1.2 8.1 %copy-start.5 = (s32[1,17]{1,0:T(1,128)S(1)}, s32[1,17]{1,0:T(1,128)}, u32[]{:S(2)}) copy-start(s32[1,17]{1,0:T(1,128)} %lengths_ref.1) | copy-start | bytes 208
  1.2 15.8 %collective-permute-start.6 = (f32[32,1024]{1,0:T(8,128)S(1)}, f32[32,1024]{1,0:T(8,128)S(1)}, u32[]{:S(2)}, u32[]{:S(2)}) collective-permute-start(f32[32,1024]{1,0:T(8,128)S(1)} %get-tuple-element.52), channel_id=1, source_target_pairs={{0,9},{1,8},{2,11},{3,10},{4,13},{5,12},{6,15},{7,14},{8,1},{9,0},... | collective-permute-start | bytes 393224 | tf_op jit(solution)/shard_map/ppermute | solution.py:23
  4.7 13.8 %collective-permute-start.8 = (f32[32,1024]{1,0:T(8,128)S(1)}, f32[32,1024]{1,0:T(8,128)S(1)}, u32[]{:S(2)}, u32[]{:S(2)}) collective-permute-start(f32[32,1024]{1,0:T(8,128)S(1)} %get-tuple-element.52), channel_id=1, source_target_pairs={{0,13},{1,12},{2,15},{3,14},{4,9},{5,8},{6,11},{7,10},{8,5},{9,4},... | collective-permute-start | bytes 393224 | tf_op jit(solution)/shard_map/ppermute | solution.py:23
  6.4 14.2 %collective-permute-start.4 = (f32[64,1024]{1,0:T(8,128)S(1)}, f32[64,1024]{1,0:T(8,128)S(1)}, u32[]{:S(2)}, u32[]{:S(2)}) collective-permute-start(f32[64,1024]{1,0:T(8,128)S(1)} %get-tuple-element.29.after_ref), channel_id=1, source_target_pairs={{0,5},{1,4},{2,7},{3,6},{4,1},{5,0},{6,3},{7,2},{8,13},{9,12},{10,... | collective-permute-start | bytes 786440 | tf_op jit(solution)/shard_map/ppermute | solution.py:23
  9.2 1.4 %collective-permute-start = (f32[64,512]{1,0:T(8,128)S(1)}, f32[64,512]{1,0:T(8,128)S(1)}, u32[]{:S(2)}, u32[]{:S(2)}) collective-permute-start(f32[64,512]{1,0:T(8,128)S(1)} %project.1.after_ref.own_ref), channel_id=1, source_target_pairs={{0,1},{1,0},{2,3},{3,2},{4,5},{5,4},{6,7},{7,6},{8,9},{9,8},{10,11... | collective-permute-start | bytes 393224 | tf_op jit(solution)/shard_map/ppermute | solution.py:23
  10.9 3.2 %collective-permute-start.1 = (f32[32,128]{1,0:T(8,128)S(1)}, f32[32,128]{1,0:T(8,128)S(1)}, u32[]{:S(2)}, u32[]{:S(2)}) collective-permute-start(f32[32,128]{1,0:T(8,128)S(1)} %fisher.1.after_ref), channel_id=1, source_target_pairs={{0,3},{1,2},{2,1},{3,0},{4,7},{5,6},{6,5},{7,4},{8,11},{9,10},{10,... | collective-permute-start | bytes 49160 | tf_op jit(solution)/shard_map/ppermute | solution.py:23
  13.2 7.4 %copy-start.2 = (f32[1,128,1024]{2,1,0:T(8,128)S(1)}, f32[1,128,1024]{2,1,0:T(8,128)}, u32[]{:S(2)}) copy-start(f32[1,128,1024]{2,1,0:T(8,128)} %own_ref.1) | copy-start | bytes 1572868
  13.2 6.8 %collective-permute-start.3 = (f32[1,16,1024]{2,1,0:T(8,128)S(1)}, f32[1,16,1024]{2,1,0:T(8,128)S(1)}, u32[]{:S(2)}, u32[]{:S(2)}) collective-permute-start(f32[1,16,1024]{2,1,0:T(8,128)S(1)} %hold.3), channel_id=1, source_target_pairs={{0,3},{1,2},{2,1},{3,0},{4,7},{5,6},{6,5},{7,4},{8,11},{9,10},{10,... | collective-permute-start | bytes 196616 | tf_op jit(solution)/shard_map/ppermute | solution.py:23
  14.1 5.0 %collective-permute-start.2 = (f32[32,128]{1,0:T(8,128)S(1)}, f32[32,128]{1,0:T(8,128)S(1)}, u32[]{:S(2)}, u32[]{:S(2)}) collective-permute-start(f32[32,128]{1,0:T(8,128)S(1)} %add.6.after_ref), channel_id=1, source_target_pairs={{0,9},{1,8},{2,11},{3,10},{4,13},{5,12},{6,15},{7,14},{8,1},{9,0},... | collective-permute-start | bytes 49160 | tf_op jit(solution)/shard_map/ppermute | solution.py:23
  17.0 8.0 %collective-permute-start.7 = (f32[32,1024]{1,0:T(8,128)S(1)}, f32[32,1024]{1,0:T(8,128)S(1)}, u32[]{:S(2)}, u32[]{:S(2)}) collective-permute-start(f32[32,1024]{1,0:T(8,128)S(1)} %hold.4), channel_id=1, source_target_pairs={{0,16},{1,17},{2,18},{3,19},{4,20},{5,21},{6,22},{7,23},{8,24},{9,... | collective-permute-start | bytes 393224 | tf_op jit(solution)/shard_map/ppermute | solution.py:23
  18.6 6.5 %collective-permute-start.9 = (f32[32,1024]{1,0:T(8,128)S(1)}, f32[32,1024]{1,0:T(8,128)S(1)}, u32[]{:S(2)}, u32[]{:S(2)}) collective-permute-start(f32[32,1024]{1,0:T(8,128)S(1)} %hold.5), channel_id=1, source_target_pairs={{0,16},{1,17},{2,18},{3,19},{4,20},{5,21},{6,22},{7,23},{8,24},{9,... | collective-permute-start | bytes 393224 | tf_op jit(solution)/shard_map/ppermute | solution.py:23
  19.1 3.2 %collective-permute-start.5 = (f32[32,128]{1,0:T(8,128)S(1)}, f32[32,128]{1,0:T(8,128)S(1)}, u32[]{:S(2)}, u32[]{:S(2)}) collective-permute-start(f32[32,128]{1,0:T(8,128)S(1)} %add.7.own_ref), channel_id=1, source_target_pairs={{0,5},{1,4},{2,7},{3,6},{4,1},{5,0},{6,3},{7,2},{8,13},{9,12},{10,... | collective-permute-start | bytes 49160 | tf_op jit(solution)/shard_map/ppermute | solution.py:23
  25.5 1.2 %collective-permute-start.10 = (f32[32,256]{1,0:T(8,128)S(1)}, f32[32,256]{1,0:T(8,128)S(1)}, u32[]{:S(2)}, u32[]{:S(2)}) collective-permute-start(f32[32,256]{1,0:T(8,128)S(1)} %score.1.kept_ref), channel_id=1, source_target_pairs={{0,1},{1,0},{2,3},{3,2},{4,5},{5,4},{6,7},{7,6},{8,9},{9,8},{10,11... | collective-permute-start | bytes 98312 | tf_op jit(solution)/shard_map/ppermute | solution.py:23

commit v8 on v7

--- a/solution.py
+++ b/solution.py
@@ -74,19 +74,15 @@
 
 def masks_kernel(lengths_ref, after_ref, member_ref, live_ref, count_ref):
     examples, slots = member_ref.shape
-    index = lax.broadcasted_iota(jnp.int32, (examples, 1), 0)
-    starts = jnp.zeros((examples, 1), jnp.int32)
-    counts = jnp.zeros((examples, 1), jnp.int32)
-    begin = jnp.int32(0)
-    for e in range(examples):
-        length = lengths_ref[0, e]
-        starts = jnp.where(index == e, begin, starts)
-        counts = jnp.where(index == e, length, counts)
-        begin = begin + length
-    slot = lax.broadcasted_iota(jnp.int32, (examples, slots), 1)
-    member_ref[...] = jnp.where((slot >= starts) & (slot < starts + counts), 1.0, 0.0).astype(BF16)
-    live_ref[...] = jnp.where(slot[0:8] < begin, 1.0, 0.0)
-    count_ref[...] = jnp.broadcast_to(counts.astype(F32), count_ref.shape)
+    length = jnp.broadcast_to(lengths_ref[...].astype(F32), (examples, lengths_ref.shape[1]))
+    example = lax.broadcasted_iota(jnp.int32, length.shape, 0)
+    entry = lax.broadcasted_iota(jnp.int32, length.shape, 1)
+    begin = jnp.sum(jnp.where(entry < example, length, 0.0), axis=1, keepdims=True)
+    end = jnp.sum(jnp.where(entry <= example, length, 0.0), axis=1, keepdims=True)
+    slot = lax.broadcasted_iota(jnp.int32, (examples, slots), 1).astype(F32)
+    member_ref[...] = jnp.where((slot >= begin) & (slot < end), 1.0, 0.0).astype(BF16)
+    live_ref[...] = jnp.where(slot[0:8] < end[examples - 1 : examples], 1.0, 0.0)
+    count_ref[...] = jnp.broadcast_to(end - begin, count_ref.shape)
 
 
 def masks(lengths, after):
@@ -98,7 +94,7 @@
             jax.ShapeDtypeStruct((8, slots), F32),
             jax.ShapeDtypeStruct((examples, 128), F32),
         ),
-        in_specs=[pl.BlockSpec(memory_space=pltpu.SMEM), pl.BlockSpec(memory_space=pl.ANY)],
+        in_specs=[pl.BlockSpec(memory_space=pltpu.VMEM), pl.BlockSpec(memory_space=pl.ANY)],
         out_specs=(pl.BlockSpec(memory_space=pltpu.VMEM),) * 3,
         compiler_params=pltpu.CompilerParams(vmem_limit_bytes=4 * MIB),
         cost_estimate=pl.CostEstimate(flops=2 * 10**9, bytes_accessed=10**6, transcendentals=0),
@@ -434,9 +430,11 @@
     group_bits = [b * unit * n_dp for b in bits_of(groups)]
 
     half, piece = pick_queries(queries, groups)
-    fetched = [swap(half if r == 1 else piece, mesh, r * unit | core_bit) for r in range(1, n_dp)]
+    fetched = [swap(piece, mesh, r * unit | core_bit) for r in range(2, n_dp)]
 
     own = project(activations, out_grads, proj_in, proj_out, half)
+    half, own = lax.optimization_barrier((half, own))
+    fetched = [swap(half, mesh, unit | core_bit)] + fetched
     member, live, count = masks(lengths, own)
     other = swap(own, mesh, core_bit)
     own, other, live = lax.optimization_barrier((own, other, live))

time: 27.6 us -> 26.8 us (0.971)
  waiting for transfers between devices: 4.16 us -> 3.22 us
  starting transfers between devices: 13.2 us -> 13.9 us
  Pallas kernels: 9.83 us -> 9.34 us
    ppermute x11, waiting for transfers between devices: 4.16 us -> 3.22 us  [swap(): return lax.ppermute(value, AXES, [(i, i ^ mask) for i in range(count)])]
    ppermute x11, starting transfers between devices: 13.2 us -> 13.9 us  [swap(): return lax.ppermute(value, AXES, [(i, i ^ mask) for i in range(count)])]
    pallas_call x1, Pallas kernels: 0.56 us -> 0.09 us  [masks(): pl.pallas_call(masks_kernel, out_shape=(jax.ShapeDtypeStruct((examples, s...]
  transfers between devices with their start and end apart: 11 -> 11, of which waited for: 5 -> 6; matrix products, arithmetic and copies ran while one was open for 0% -> 0% of each run, Pallas kernels for 28% -> 27%
where the time goes in v8:
time: 26.8 us; the launch traced here: 26.6 us
  starting transfers between devices  13.9 us (52%)
  Pallas kernels  9.34 us (35%)
  waiting for transfers between devices  3.22 us (12%)
    ppermute x11, starting transfers between devices, swap(): return lax.ppermute(value, AXES, [(i, i ^ mask) for i in range(count)])  13.9 us
    ppermute x11, waiting for transfers between devices, swap(): return lax.ppermute(value, AXES, [(i, i ^ mask) for i in range(count)])  3.22 us
    pallas_call x1, Pallas kernels, project(): pl.pallas_call(project_kernel, out_shape=jax.ShapeDtypeStruct((2 * proj_i...  2.6 us
    pallas_call x1, Pallas kernels, condition(): pl.pallas_call(condition_kernel, out_shape=(jax.ShapeDtypeStruct((columns...  2.54 us
    pallas_call x1, Pallas kernels, pick_queries(): pl.pallas_call(functools.partial(pick_kernel, groups), out_shape=tuple((j...  1.16 us
    pallas_call x1, Pallas kernels, example_grads(): pl.pallas_call(examples_kernel, out_shape=jax.ShapeDtypeStruct((member.sh...  0.96 us
    pallas_call x1, Pallas kernels, place(): pl.pallas_call(functools.partial(place_kernel, half), out_shape=jax.Shape...  0.72 us
    pallas_call x1, Pallas kernels, arrange_examples(): pl.pallas_call(functools.partial(arrange_examples_kernel, n_query), out_s...  0.56 us
  transfers between devices with their start and end apart: 11, of which 6 were waited for; matrix products, arithmetic and copies ran while one was open for 0% of the time, Pallas kernels for 27%

profile of v8, /device:TPU:0, one launch (start us, length us, event | category | flops | bytes accessed | tf_op | source)
XLA Modules:
  0.0 26.6 jit_solution(14868945528051969640)
XLA Ops:
  0.0 1.2 %pick_queries.1 = (f32[64,1024]{1,0:T(8,128)S(1)}, f32[32,1024]{1,0:T(8,128)S(1)}) custom-call(f32[1,128,1024]{2,1,0:T(8,128)} %own_ref.1), custom_call_target="tpu_custom_call" | custom-call | flops 4000000000 | bytes 1000000 | tf_op jit(solution)/shard_map/pick_queries/pallas_call | solution.py:46
  1.2 3.6 %collective-permute-start.6 = (f32[32,1024]{1,0:T(8,128)S(1)}, f32[32,1024]{1,0:T(8,128)S(1)}, u32[]{:S(2)}, u32[]{:S(2)}) collective-permute-start(f32[32,1024]{1,0:T(8,128)S(1)} %get-tuple-element.56), channel_id=1, source_target_pairs={{0,9},{1,8},{2,11},{3,10},{4,13},{5,12},{6,15},{7,14},{8,1},{9,0},... | collective-permute-start | bytes 393224 | tf_op jit(solution)/shard_map/ppermute | solution.py:23
  4.7 1.6 %collective-permute-start.8 = (f32[32,1024]{1,0:T(8,128)S(1)}, f32[32,1024]{1,0:T(8,128)S(1)}, u32[]{:S(2)}, u32[]{:S(2)}) collective-permute-start(f32[32,1024]{1,0:T(8,128)S(1)} %get-tuple-element.56), channel_id=1, source_target_pairs={{0,13},{1,12},{2,15},{3,14},{4,9},{5,8},{6,11},{7,10},{8,5},{9,4},... | collective-permute-start | bytes 393224 | tf_op jit(solution)/shard_map/ppermute | solution.py:23
  6.4 2.6 %project.1.after_ref.own_ref = f32[64,512]{1,0:T(8,128)S(1)} custom-call(bf16[512,2048]{1,0:T(8,128)(2,1)S(1)} %copy-done.1, bf16[512,7168]{1,0:T(8,128)(2,1)S(1)} %copy-done, bf16[32,2048]{1,0:T(8,128)(2,1)S(1)} %bitcast.4, bf16[32,7168]{1,0:T(8,128)(2,1)S(1)} %bitcast.3, f32[64,1024]{1,0:T(8,128)S(1)} %get-tuple-element.45.after_ref), custom_call_target="tpu_custom_call" | custom-call | tf_op jit(solution)/shard_map/project/pallas_call | solution.py:65
  9.0 0.2 collective-permute-start
  9.2 0.5 %collective-permute-start.4 = (f32[64,1024]{1,0:T(8,128)S(1)}, f32[64,1024]{1,0:T(8,128)S(1)}, u32[]{:S(2)}, u32[]{:S(2)}) collective-permute-start(f32[64,1024]{1,0:T(8,128)S(1)} %get-tuple-element.45.after_ref), channel_id=1, source_target_pairs={{0,5},{1,4},{2,7},{3,6},{4,1},{5,0},{6,3},{7,2},{8,13},{9,12},{10,... | collective-permute-start | bytes 786440 | tf_op jit(solution)/shard_map/ppermute | solution.py:23
  9.8 0.6 %collective-permute-done.other_ref = f32[64,512]{1,0:T(8,128)S(1)} collective-permute-done((f32[64,512]{1,0:T(8,128)S(1)}, f32[64,512]{1,0:T(8,128)S(1)}, u32[]{:S(2)}, u32[]{:S(2)}) %collective-permute-start) | collective-permute-done | bytes 131104 | tf_op jit(solution)/shard_map/ppermute | solution.py:23
  10.4 0.3 fisher.1.after_ref
  10.7 1.3 %collective-permute-start.1 = (f32[32,128]{1,0:T(8,128)S(1)}, f32[32,128]{1,0:T(8,128)S(1)}, u32[]{:S(2)}, u32[]{:S(2)}) collective-permute-start(f32[32,128]{1,0:T(8,128)S(1)} %fisher.1.after_ref), channel_id=1, source_target_pairs={{0,3},{1,2},{2,1},{3,0},{4,7},{5,6},{6,5},{7,4},{8,11},{9,10},{10,... | collective-permute-start | bytes 49160 | tf_op jit(solution)/shard_map/ppermute | solution.py:23
  12.0 1.0 %examples.1 = f32[16,1024]{1,0:T(8,128)S(1)} custom-call(bf16[16,512]{1,0:T(8,128)(2,1)S(1)} %get-tuple-element.38.member_ref, f32[16,128]{1,0:T(8,128)S(1)} %get-tuple-element.39.count_ref, f32[64,512]{1,0:T(8,128)S(1)} %project.1.after_ref.own_ref, f32[64,512]{1,0:T(8,128)S(1)} %collective-permute-done.other_ref), custom_call_target="tpu_custom_call" | custom-call | flops 2000000000 | bytes 1000000 | tf_op jit(solution)/shard_map/examples/pallas_call | solution.py:150
  13.0 0.6 %collective-permute-start.3 = (f32[1,16,1024]{2,1,0:T(8,128)S(1)}, f32[1,16,1024]{2,1,0:T(8,128)S(1)}, u32[]{:S(2)}, u32[]{:S(2)}) collective-permute-start(f32[1,16,1024]{2,1,0:T(8,128)S(1)} %hold.3), channel_id=1, source_target_pairs={{0,3},{1,2},{2,1},{3,0},{4,7},{5,6},{6,5},{7,4},{8,11},{9,10},{10,... | collective-permute-start | bytes 196616 | tf_op jit(solution)/shard_map/ppermute | solution.py:23
  13.5 0.4 %collective-permute-done.1 = f32[32,128]{1,0:T(8,128)S(1)} collective-permute-done((f32[32,128]{1,0:T(8,128)S(1)}, f32[32,128]{1,0:T(8,128)S(1)}, u32[]{:S(2)}, u32[]{:S(2)}) %collective-permute-start.1) | collective-permute-done | bytes 16416 | tf_op jit(solution)/shard_map/ppermute | solution.py:23
  13.9 2.0 %collective-permute-start.2 = (f32[32,128]{1,0:T(8,128)S(1)}, f32[32,128]{1,0:T(8,128)S(1)}, u32[]{:S(2)}, u32[]{:S(2)}) collective-permute-start(f32[32,128]{1,0:T(8,128)S(1)} %add.6.after_ref), channel_id=1, source_target_pairs={{0,9},{1,8},{2,11},{3,10},{4,13},{5,12},{6,15},{7,14},{8,1},{9,0},... | collective-permute-start | bytes 49160 | tf_op jit(solution)/shard_map/ppermute | solution.py:23
  15.9 1.6 %collective-permute-start.7 = (f32[32,1024]{1,0:T(8,128)S(1)}, f32[32,1024]{1,0:T(8,128)S(1)}, u32[]{:S(2)}, u32[]{:S(2)}) collective-permute-start(f32[32,1024]{1,0:T(8,128)S(1)} %hold.4), channel_id=1, source_target_pairs={{0,16},{1,17},{2,18},{3,19},{4,20},{5,21},{6,22},{7,23},{8,24},{9,... | collective-permute-start | bytes 393224 | tf_op jit(solution)/shard_map/ppermute | solution.py:23
  17.5 0.6 %collective-permute-start.9 = (f32[32,1024]{1,0:T(8,128)S(1)}, f32[32,1024]{1,0:T(8,128)S(1)}, u32[]{:S(2)}, u32[]{:S(2)}) collective-permute-start(f32[32,1024]{1,0:T(8,128)S(1)} %hold.5), channel_id=1, source_target_pairs={{0,16},{1,17},{2,18},{3,19},{4,20},{5,21},{6,22},{7,23},{8,24},{9,... | collective-permute-start | bytes 393224 | tf_op jit(solution)/shard_map/ppermute | solution.py:23
  18.1 1.6 %collective-permute-start.5 = (f32[32,128]{1,0:T(8,128)S(1)}, f32[32,128]{1,0:T(8,128)S(1)}, u32[]{:S(2)}, u32[]{:S(2)}) collective-permute-start(f32[32,128]{1,0:T(8,128)S(1)} %add.7.own_ref), channel_id=1, source_target_pairs={{0,5},{1,4},{2,7},{3,6},{4,1},{5,0},{6,3},{7,2},{8,13},{9,12},{10,... | collective-permute-start | bytes 49160 | tf_op jit(solution)/shard_map/ppermute | solution.py:23
  19.7 0.6 %arrange_examples.1 = (bf16[128,256]{1,0:T(8,128)(2,1)S(1)}, bf16[128,256]{1,0:T(8,128)(2,1)S(1)}, bf16[128,256]{1,0:T(8,128)(2,1)S(1)}) custom-call(f32[2,16,1024]{2,1,0:T(8,128)S(1)} %pad_maximum_fusion.2.blocks_ref), custom_call_target="tpu_custom_call" | custom-call | tf_op jit(solution)/shard_map/arrange_examples/pallas_call | solution.py:194
  20.4 0.9 %collective-permute-done.5.other_ref = f32[32,128]{1,0:T(8,128)S(1)} collective-permute-done((f32[32,128]{1,0:T(8,128)S(1)}, f32[32,128]{1,0:T(8,128)S(1)}, u32[]{:S(2)}, u32[]{:S(2)}) %collective-permute-start.5) | collective-permute-done | bytes 16416 | tf_op jit(solution)/shard_map/ppermute | solution.py:23
  21.3 2.5 %condition.1 = (bf16[4,64,256]{2,1,0:T(8,128)(2,1)S(1)}, f32[32,128]{1,0:T(8,128)S(1)}) custom-call(f32[32,128]{1,0:T(8,128)S(1)} %add.7.own_ref, f32[32,128]{1,0:T(8,128)S(1)} %collective-permute-done.5.other_ref, bf16[128,256]{1,0:T(8,128)(2,1)S(1)} %get-tuple-element.49.high_ref, bf16[128,256]{1,0:T(8,128)(2,1)S(1)} %get-tuple-element.50.middle_ref, ...), custom_call_target="tpu_custom_call" | custom-call | flops 4000000000 | bytes 1000000 | tf_op jit(solution)/shard_map/condition/pallas_call | solution.py:338
  23.9 0.4 %collective-permute-done.9 = f32[32,1024]{1,0:T(8,128)S(1)} collective-permute-done((f32[32,1024]{1,0:T(8,128)S(1)}, f32[32,1024]{1,0:T(8,128)S(1)}, u32[]{:S(2)}, u32[]{:S(2)}) %collective-permute-start.9) | collective-permute-done | bytes 131104 | tf_op jit(solution)/shard_map/ppermute | solution.py:23
  24.4 0.3 %score.1.kept_ref = f32[32,256]{1,0:T(8,128)S(1)} custom-call(bf16[4,64,256]{2,1,0:T(8,128)(2,1)S(1)} %get-tuple-element.54.both_ref, f32[32,128]{1,0:T(8,128)S(1)} %get-tuple-element.55.near_ref, f32[64,1024]{1,0:T(8,128)S(1)} %pad_maximum_fusion.refs_0_, f32[64,1024]{1,0:T(8,128)S(1)} %pad_maximum_fusion.1.refs_1_), custom_call_target="tpu_custom_call" | custom-call | tf_op jit(solution)/shard_map/score/pallas_call | solution.py:369
  24.7 0.4 %collective-permute-start.10 = (f32[32,256]{1,0:T(8,128)S(1)}, f32[32,256]{1,0:T(8,128)S(1)}, u32[]{:S(2)}, u32[]{:S(2)}) collective-permute-start(f32[32,256]{1,0:T(8,128)S(1)} %score.1.kept_ref), channel_id=1, source_target_pairs={{0,1},{1,0},{2,3},{3,2},{4,5},{5,4},{6,7},{7,6},{8,9},{9,8},{10,11... | collective-permute-start | bytes 98312 | tf_op jit(solution)/shard_map/ppermute | solution.py:23
  25.1 0.9 %collective-permute-done.10.received_ref = f32[32,256]{1,0:T(8,128)S(1)} collective-permute-done((f32[32,256]{1,0:T(8,128)S(1)}, f32[32,256]{1,0:T(8,128)S(1)}, u32[]{:S(2)}, u32[]{:S(2)}) %collective-permute-start.10) | collective-permute-done | bytes 32800 | tf_op jit(solution)/shard_map/ppermute | solution.py:23
  25.9 0.7 %place.1 = f32[32,512]{1,0:T(8,128)} custom-call(f32[32,256]{1,0:T(8,128)S(1)} %score.1.kept_ref, f32[32,256]{1,0:T(8,128)S(1)} %collective-permute-done.10.received_ref), custom_call_target="tpu_custom_call" | custom-call | tf_op jit(solution)/shard_map/place/pallas_call | solution.py:393
  (28 shorter events, 0.4 us)
Async XLA Ops:
  0.0 6.4 %copy-start.1 = (bf16[512,2048]{1,0:T(8,128)(2,1)S(1)}, bf16[512,2048]{1,0:T(8,128)(2,1)}, u32[]{:S(2)}) copy-start(bf16[512,2048]{1,0:T(8,128)(2,1)} %a_ref.1) | copy-start | bytes 6291460
  0.0 6.4 %copy-start = (bf16[512,7168]{1,0:T(8,128)(2,1)S(1)}, bf16[512,7168]{1,0:T(8,128)(2,1)}, u32[]{:S(2)}) copy-start(bf16[512,7168]{1,0:T(8,128)(2,1)} %g_ref.1) | copy-start | bytes 22020100
  0.0 6.4 %copy-start.4 = (bf16[2048,32]{0,1:T(8,128)(2,1)S(1)}, bf16[2048,32]{0,1:T(8,128)(2,1)}, u32[]{:S(2)}) copy-start(bf16[2048,32]{0,1:T(8,128)(2,1)} %param.8) | copy-start | bytes 393220
  0.0 6.4 %copy-start.3 = (bf16[7168,32]{0,1:T(8,128)(2,1)S(1)}, bf16[7168,32]{0,1:T(8,128)(2,1)}, u32[]{:S(2)}) copy-start(bf16[7168,32]{0,1:T(8,128)(2,1)} %param.9) | copy-start | bytes 1376260
  1.2 8.6 %copy-start.5 = (s32[1,17]{1,0:T(1,128)S(1)}, s32[1,17]{1,0:T(1,128)}, u32[]{:S(2)}) copy-start(s32[1,17]{1,0:T(1,128)} %lengths_ref.1) | copy-start | bytes 208
  1.2 14.7 %collective-permute-start.6 = (f32[32,1024]{1,0:T(8,128)S(1)}, f32[32,1024]{1,0:T(8,128)S(1)}, u32[]{:S(2)}, u32[]{:S(2)}) collective-permute-start(f32[32,1024]{1,0:T(8,128)S(1)} %get-tuple-element.56), channel_id=1, source_target_pairs={{0,9},{1,8},{2,11},{3,10},{4,13},{5,12},{6,15},{7,14},{8,1},{9,0},... | collective-permute-start | bytes 393224 | tf_op jit(solution)/shard_map/ppermute | solution.py:23
  4.7 12.7 %collective-permute-start.8 = (f32[32,1024]{1,0:T(8,128)S(1)}, f32[32,1024]{1,0:T(8,128)S(1)}, u32[]{:S(2)}, u32[]{:S(2)}) collective-permute-start(f32[32,1024]{1,0:T(8,128)S(1)} %get-tuple-element.56), channel_id=1, source_target_pairs={{0,13},{1,12},{2,15},{3,14},{4,9},{5,8},{6,11},{7,10},{8,5},{9,4},... | collective-permute-start | bytes 393224 | tf_op jit(solution)/shard_map/ppermute | solution.py:23
  9.0 1.4 %collective-permute-start = (f32[64,512]{1,0:T(8,128)S(1)}, f32[64,512]{1,0:T(8,128)S(1)}, u32[]{:S(2)}, u32[]{:S(2)}) collective-permute-start(f32[64,512]{1,0:T(8,128)S(1)} %project.1.after_ref.own_ref), channel_id=1, source_target_pairs={{0,1},{1,0},{2,3},{3,2},{4,5},{5,4},{6,7},{7,6},{8,9},{9,8},{10,11... | collective-permute-start | bytes 393224 | tf_op jit(solution)/shard_map/ppermute | solution.py:23
  9.2 11.1 %collective-permute-start.4 = (f32[64,1024]{1,0:T(8,128)S(1)}, f32[64,1024]{1,0:T(8,128)S(1)}, u32[]{:S(2)}, u32[]{:S(2)}) collective-permute-start(f32[64,1024]{1,0:T(8,128)S(1)} %get-tuple-element.45.after_ref), channel_id=1, source_target_pairs={{0,5},{1,4},{2,7},{3,6},{4,1},{5,0},{6,3},{7,2},{8,13},{9,12},{10,... | collective-permute-start | bytes 786440 | tf_op jit(solution)/shard_map/ppermute | solution.py:23
  10.7 3.2 %collective-permute-start.1 = (f32[32,128]{1,0:T(8,128)S(1)}, f32[32,128]{1,0:T(8,128)S(1)}, u32[]{:S(2)}, u32[]{:S(2)}) collective-permute-start(f32[32,128]{1,0:T(8,128)S(1)} %fisher.1.after_ref), channel_id=1, source_target_pairs={{0,3},{1,2},{2,1},{3,0},{4,7},{5,6},{6,5},{7,4},{8,11},{9,10},{10,... | collective-permute-start | bytes 49160 | tf_op jit(solution)/shard_map/ppermute | solution.py:23
  12.9 7.4 %copy-start.2 = (f32[1,128,1024]{2,1,0:T(8,128)S(1)}, f32[1,128,1024]{2,1,0:T(8,128)}, u32[]{:S(2)}) copy-start(f32[1,128,1024]{2,1,0:T(8,128)} %own_ref.1) | copy-start | bytes 1572868
  13.0 6.7 %collective-permute-start.3 = (f32[1,16,1024]{2,1,0:T(8,128)S(1)}, f32[1,16,1024]{2,1,0:T(8,128)S(1)}, u32[]{:S(2)}, u32[]{:S(2)}) collective-permute-start(f32[1,16,1024]{2,1,0:T(8,128)S(1)} %hold.3), channel_id=1, source_target_pairs={{0,3},{1,2},{2,1},{3,0},{4,7},{5,6},{6,5},{7,4},{8,11},{9,10},{10,... | collective-permute-start | bytes 196616 | tf_op jit(solution)/shard_map/ppermute | solution.py:23
  13.9 4.2 %collective-permute-start.2 = (f32[32,128]{1,0:T(8,128)S(1)}, f32[32,128]{1,0:T(8,128)S(1)}, u32[]{:S(2)}, u32[]{:S(2)}) collective-permute-start(f32[32,128]{1,0:T(8,128)S(1)} %add.6.after_ref), channel_id=1, source_target_pairs={{0,9},{1,8},{2,11},{3,10},{4,13},{5,12},{6,15},{7,14},{8,1},{9,0},... | collective-permute-start | bytes 49160 | tf_op jit(solution)/shard_map/ppermute | solution.py:23
  15.9 8.0 %collective-permute-start.7 = (f32[32,1024]{1,0:T(8,128)S(1)}, f32[32,1024]{1,0:T(8,128)S(1)}, u32[]{:S(2)}, u32[]{:S(2)}) collective-permute-start(f32[32,1024]{1,0:T(8,128)S(1)} %hold.4), channel_id=1, source_target_pairs={{0,16},{1,17},{2,18},{3,19},{4,20},{5,21},{6,22},{7,23},{8,24},{9,... | collective-permute-start | bytes 393224 | tf_op jit(solution)/shard_map/ppermute | solution.py:23
  17.5 6.8 %collective-permute-start.9 = (f32[32,1024]{1,0:T(8,128)S(1)}, f32[32,1024]{1,0:T(8,128)S(1)}, u32[]{:S(2)}, u32[]{:S(2)}) collective-permute-start(f32[32,1024]{1,0:T(8,128)S(1)} %hold.5), channel_id=1, source_target_pairs={{0,16},{1,17},{2,18},{3,19},{4,20},{5,21},{6,22},{7,23},{8,24},{9,... | collective-permute-start | bytes 393224 | tf_op jit(solution)/shard_map/ppermute | solution.py:23
  18.1 3.2 %collective-permute-start.5 = (f32[32,128]{1,0:T(8,128)S(1)}, f32[32,128]{1,0:T(8,128)S(1)}, u32[]{:S(2)}, u32[]{:S(2)}) collective-permute-start(f32[32,128]{1,0:T(8,128)S(1)} %add.7.own_ref), channel_id=1, source_target_pairs={{0,5},{1,4},{2,7},{3,6},{4,1},{5,0},{6,3},{7,2},{8,13},{9,12},{10,... | collective-permute-start | bytes 49160 | tf_op jit(solution)/shard_map/ppermute | solution.py:23
  24.7 1.2 %collective-permute-start.10 = (f32[32,256]{1,0:T(8,128)S(1)}, f32[32,256]{1,0:T(8,128)S(1)}, u32[]{:S(2)}, u32[]{:S(2)}) collective-permute-start(f32[32,256]{1,0:T(8,128)S(1)} %score.1.kept_ref), channel_id=1, source_target_pairs={{0,1},{1,0},{2,3},{3,2},{4,5},{5,4},{6,7},{7,6},{8,9},{9,8},{10,11... | collective-permute-start | bytes 98312 | tf_op jit(solution)/shard_map/ppermute | solution.py:23

commit v9 on v8

--- a/solution.py
+++ b/solution.py
@@ -29,8 +29,9 @@
 
 def pick_kernel(groups, queries_hbm, half_ref, piece_ref, sems):
     half, piece = half_ref.shape[0], piece_ref.shape[0]
-    core = 1 - lax.axis_index("proj")
-    index = core * groups + lax.axis_index("grp")
+    group = lax.axis_index("grp")
+    core = (lax.axis_index("proj") + group + 1) % 2
+    index = core * groups + group
     copies = [
         pltpu.make_async_copy(queries_hbm.at[0, pl.ds(pl.multiple_of(core * half, 8), half)], half_ref, sems.at[0]),
         pltpu.make_async_copy(queries_hbm.at[0, pl.ds(pl.multiple_of(index * piece, 8), piece)], piece_ref, sems.at[1]),
@@ -204,7 +205,7 @@
 
 def split_near_kernel(own_ref, near_ref, high_ref, low_ref):
     half = near_ref.shape[0]
-    start = pl.multiple_of(lax.axis_index("proj") * half, 8)
+    start = pl.multiple_of((lax.axis_index("proj") + lax.axis_index("grp")) % 2 * half, 8)
     for i, value in enumerate((own_ref[0, pl.ds(start, half), :], near_ref[...])):
         at = slice(i * half, (i + 1) * half)
         high_ref[at, :], low_ref[at, :] = split2(value)
@@ -378,7 +379,7 @@
 
 
 def place_kernel(half, kept_ref, received_ref, out_ref):
-    core = lax.axis_index("proj")
+    core = (lax.axis_index("proj") + lax.axis_index("grp")) % 2
     kept, received = kept_ref[...], received_ref[...]
     first = jnp.where(core == 0, kept, received)
     second = jnp.where(core == 0, received, kept)
@@ -455,7 +456,7 @@
             for r in range(first, end):
                 fetched[r] = hold(fetched[r], factor)
                 for bit in group_bits:
-                    fetched[r] = jnp.concatenate([fetched[r], swap(fetched[r], mesh, bit)], axis=0)
+                    fetched[r] = jnp.concatenate([fetched[r], swap(fetched[r], mesh, bit | (core_bit if bit == group_bits[0] else 0))], axis=0)
         return blocks
 
     for step, mask in enumerate(steps):

time: 26.8 us -> 27 us (level)
  no operation moved by 1% of the time
where the time goes in v9:
time: 27 us; the launch traced here: 26.6 us
  starting transfers between devices  14 us (52%)
  Pallas kernels  9.35 us (35%)
  waiting for transfers between devices  3.08 us (11%)
    ppermute x11, starting transfers between devices, swap(): return lax.ppermute(value, AXES, [(i, i ^ mask) for i in range(count)])  14 us
    ppermute x11, waiting for transfers between devices, swap(): return lax.ppermute(value, AXES, [(i, i ^ mask) for i in range(count)])  3.08 us
    pallas_call x1, Pallas kernels, project(): pl.pallas_call(project_kernel, out_shape=jax.ShapeDtypeStruct((2 * proj_i...  2.6 us
    pallas_call x1, Pallas kernels, condition(): pl.pallas_call(condition_kernel, out_shape=(jax.ShapeDtypeStruct((columns...  2.54 us
    pallas_call x1, Pallas kernels, pick_queries(): pl.pallas_call(functools.partial(pick_kernel, groups), out_shape=tuple((j...  1.16 us
    pallas_call x1, Pallas kernels, example_grads(): pl.pallas_call(examples_kernel, out_shape=jax.ShapeDtypeStruct((member.sh...  0.96 us
    pallas_call x1, Pallas kernels, place(): pl.pallas_call(functools.partial(place_kernel, half), out_shape=jax.Shape...  0.72 us
    pallas_call x1, Pallas kernels, arrange_examples(): pl.pallas_call(functools.partial(arrange_examples_kernel, n_query), out_s...  0.56 us
  transfers between devices with their start and end apart: 11, of which 6 were waited for; matrix products, arithmetic and copies ran while one was open for 0% of the time, Pallas kernels for 27%

profile of v9, /device:TPU:0, one launch (start us, length us, event | category | flops | bytes accessed | tf_op | source)
XLA Modules:
  0.0 26.6 jit_solution(5226106094775767403)
XLA Ops:
  0.0 1.2 %pick_queries.1 = (f32[64,1024]{1,0:T(8,128)S(1)}, f32[32,1024]{1,0:T(8,128)S(1)}) custom-call(f32[1,128,1024]{2,1,0:T(8,128)} %own_ref.1), custom_call_target="tpu_custom_call" | custom-call | flops 4000000000 | bytes 1000000 | tf_op jit(solution)/shard_map/pick_queries/pallas_call | solution.py:47
  1.2 3.6 %collective-permute-start.6 = (f32[32,1024]{1,0:T(8,128)S(1)}, f32[32,1024]{1,0:T(8,128)S(1)}, u32[]{:S(2)}, u32[]{:S(2)}) collective-permute-start(f32[32,1024]{1,0:T(8,128)S(1)} %get-tuple-element.56), channel_id=1, source_target_pairs={{0,9},{1,8},{2,11},{3,10},{4,13},{5,12},{6,15},{7,14},{8,1},{9,0},... | collective-permute-start | bytes 393224 | tf_op jit(solution)/shard_map/ppermute | solution.py:23
  4.7 1.6 %collective-permute-start.8 = (f32[32,1024]{1,0:T(8,128)S(1)}, f32[32,1024]{1,0:T(8,128)S(1)}, u32[]{:S(2)}, u32[]{:S(2)}) collective-permute-start(f32[32,1024]{1,0:T(8,128)S(1)} %get-tuple-element.56), channel_id=1, source_target_pairs={{0,13},{1,12},{2,15},{3,14},{4,9},{5,8},{6,11},{7,10},{8,5},{9,4},... | collective-permute-start | bytes 393224 | tf_op jit(solution)/shard_map/ppermute | solution.py:23
  6.4 2.6 %project.1.after_ref.own_ref = f32[64,512]{1,0:T(8,128)S(1)} custom-call(bf16[512,2048]{1,0:T(8,128)(2,1)S(1)} %copy-done.1, bf16[512,7168]{1,0:T(8,128)(2,1)S(1)} %copy-done, bf16[32,2048]{1,0:T(8,128)(2,1)S(1)} %bitcast.4, bf16[32,7168]{1,0:T(8,128)(2,1)S(1)} %bitcast.3, f32[64,1024]{1,0:T(8,128)S(1)} %get-tuple-element.45.after_ref), custom_call_target="tpu_custom_call" | custom-call | tf_op jit(solution)/shard_map/project/pallas_call | solution.py:66
  9.2 0.5 %collective-permute-start.4 = (f32[64,1024]{1,0:T(8,128)S(1)}, f32[64,1024]{1,0:T(8,128)S(1)}, u32[]{:S(2)}, u32[]{:S(2)}) collective-permute-start(f32[64,1024]{1,0:T(8,128)S(1)} %get-tuple-element.45.after_ref), channel_id=1, source_target_pairs={{0,5},{1,4},{2,7},{3,6},{4,1},{5,0},{6,3},{7,2},{8,13},{9,12},{10,... | collective-permute-start | bytes 786440 | tf_op jit(solution)/shard_map/ppermute | solution.py:23
  9.8 0.6 %collective-permute-done.other_ref = f32[64,512]{1,0:T(8,128)S(1)} collective-permute-done((f32[64,512]{1,0:T(8,128)S(1)}, f32[64,512]{1,0:T(8,128)S(1)}, u32[]{:S(2)}, u32[]{:S(2)}) %collective-permute-start) | collective-permute-done | bytes 131104 | tf_op jit(solution)/shard_map/ppermute | solution.py:23
  10.4 0.3 fisher.1.after_ref
  10.7 1.3 %collective-permute-start.1 = (f32[32,128]{1,0:T(8,128)S(1)}, f32[32,128]{1,0:T(8,128)S(1)}, u32[]{:S(2)}, u32[]{:S(2)}) collective-permute-start(f32[32,128]{1,0:T(8,128)S(1)} %fisher.1.after_ref), channel_id=1, source_target_pairs={{0,3},{1,2},{2,1},{3,0},{4,7},{5,6},{6,5},{7,4},{8,11},{9,10},{10,... | collective-permute-start | bytes 49160 | tf_op jit(solution)/shard_map/ppermute | solution.py:23
  12.0 1.0 %examples.1 = f32[16,1024]{1,0:T(8,128)S(1)} custom-call(bf16[16,512]{1,0:T(8,128)(2,1)S(1)} %get-tuple-element.38.member_ref, f32[16,128]{1,0:T(8,128)S(1)} %get-tuple-element.39.count_ref, f32[64,512]{1,0:T(8,128)S(1)} %project.1.after_ref.own_ref, f32[64,512]{1,0:T(8,128)S(1)} %collective-permute-done.other_ref), custom_call_target="tpu_custom_call" | custom-call | flops 2000000000 | bytes 1000000 | tf_op jit(solution)/shard_map/examples/pallas_call | solution.py:151
  13.0 0.6 %collective-permute-start.3 = (f32[1,16,1024]{2,1,0:T(8,128)S(1)}, f32[1,16,1024]{2,1,0:T(8,128)S(1)}, u32[]{:S(2)}, u32[]{:S(2)}) collective-permute-start(f32[1,16,1024]{2,1,0:T(8,128)S(1)} %hold.3), channel_id=1, source_target_pairs={{0,3},{1,2},{2,1},{3,0},{4,7},{5,6},{6,5},{7,4},{8,11},{9,10},{10,... | collective-permute-start | bytes 196616 | tf_op jit(solution)/shard_map/ppermute | solution.py:23
  13.5 0.4 %collective-permute-done.1 = f32[32,128]{1,0:T(8,128)S(1)} collective-permute-done((f32[32,128]{1,0:T(8,128)S(1)}, f32[32,128]{1,0:T(8,128)S(1)}, u32[]{:S(2)}, u32[]{:S(2)}) %collective-permute-start.1) | collective-permute-done | bytes 16416 | tf_op jit(solution)/shard_map/ppermute | solution.py:23
  13.9 2.0 %collective-permute-start.2 = (f32[32,128]{1,0:T(8,128)S(1)}, f32[32,128]{1,0:T(8,128)S(1)}, u32[]{:S(2)}, u32[]{:S(2)}) collective-permute-start(f32[32,128]{1,0:T(8,128)S(1)} %add.6.after_ref), channel_id=1, source_target_pairs={{0,9},{1,8},{2,11},{3,10},{4,13},{5,12},{6,15},{7,14},{8,1},{9,0},... | collective-permute-start | bytes 49160 | tf_op jit(solution)/shard_map/ppermute | solution.py:23
  15.9 1.4 %collective-permute-start.7 = (f32[32,1024]{1,0:T(8,128)S(1)}, f32[32,1024]{1,0:T(8,128)S(1)}, u32[]{:S(2)}, u32[]{:S(2)}) collective-permute-start(f32[32,1024]{1,0:T(8,128)S(1)} %hold.4), channel_id=1, source_target_pairs={{0,17},{1,16},{2,19},{3,18},{4,21},{5,20},{6,23},{7,22},{8,25},{9,... | collective-permute-start | bytes 393224 | tf_op jit(solution)/shard_map/ppermute | solution.py:23
  17.3 0.5 %collective-permute-start.9 = (f32[32,1024]{1,0:T(8,128)S(1)}, f32[32,1024]{1,0:T(8,128)S(1)}, u32[]{:S(2)}, u32[]{:S(2)}) collective-permute-start(f32[32,1024]{1,0:T(8,128)S(1)} %hold.5), channel_id=1, source_target_pairs={{0,17},{1,16},{2,19},{3,18},{4,21},{5,20},{6,23},{7,22},{8,25},{9,... | collective-permute-start | bytes 393224 | tf_op jit(solution)/shard_map/ppermute | solution.py:23
  17.8 0.3 %collective-permute-done.2 = f32[32,128]{1,0:T(8,128)S(1)} collective-permute-done((f32[32,128]{1,0:T(8,128)S(1)}, f32[32,128]{1,0:T(8,128)S(1)}, u32[]{:S(2)}, u32[]{:S(2)}) %collective-permute-start.2) | collective-permute-done | bytes 16416 | tf_op jit(solution)/shard_map/ppermute | solution.py:23
  18.1 1.9 %collective-permute-start.5 = (f32[32,128]{1,0:T(8,128)S(1)}, f32[32,128]{1,0:T(8,128)S(1)}, u32[]{:S(2)}, u32[]{:S(2)}) collective-permute-start(f32[32,128]{1,0:T(8,128)S(1)} %add.7.own_ref), channel_id=1, source_target_pairs={{0,5},{1,4},{2,7},{3,6},{4,1},{5,0},{6,3},{7,2},{8,13},{9,12},{10,... | collective-permute-start | bytes 49160 | tf_op jit(solution)/shard_map/ppermute | solution.py:23
  20.0 0.6 %arrange_examples.1 = (bf16[128,256]{1,0:T(8,128)(2,1)S(1)}, bf16[128,256]{1,0:T(8,128)(2,1)S(1)}, bf16[128,256]{1,0:T(8,128)(2,1)S(1)}) custom-call(f32[2,16,1024]{2,1,0:T(8,128)S(1)} %pad_maximum_fusion.2.blocks_ref), custom_call_target="tpu_custom_call" | custom-call | tf_op jit(solution)/shard_map/arrange_examples/pallas_call | solution.py:195
  20.6 0.8 %collective-permute-done.5.other_ref = f32[32,128]{1,0:T(8,128)S(1)} collective-permute-done((f32[32,128]{1,0:T(8,128)S(1)}, f32[32,128]{1,0:T(8,128)S(1)}, u32[]{:S(2)}, u32[]{:S(2)}) %collective-permute-start.5) | collective-permute-done | bytes 16416 | tf_op jit(solution)/shard_map/ppermute | solution.py:23
  21.4 2.5 %condition.1 = (bf16[4,64,256]{2,1,0:T(8,128)(2,1)S(1)}, f32[32,128]{1,0:T(8,128)S(1)}) custom-call(f32[32,128]{1,0:T(8,128)S(1)} %add.7.own_ref, f32[32,128]{1,0:T(8,128)S(1)} %collective-permute-done.5.other_ref, bf16[128,256]{1,0:T(8,128)(2,1)S(1)} %get-tuple-element.49.high_ref, bf16[128,256]{1,0:T(8,128)(2,1)S(1)} %get-tuple-element.50.middle_ref, ...), custom_call_target="tpu_custom_call" | custom-call | flops 4000000000 | bytes 1000000 | tf_op jit(solution)/shard_map/condition/pallas_call | solution.py:339
  24.0 0.2 collective-permute-done.9
  24.2 0.3 %score.1.kept_ref = f32[32,256]{1,0:T(8,128)S(1)} custom-call(bf16[4,64,256]{2,1,0:T(8,128)(2,1)S(1)} %get-tuple-element.54.both_ref, f32[32,128]{1,0:T(8,128)S(1)} %get-tuple-element.55.near_ref, f32[64,1024]{1,0:T(8,128)S(1)} %pad_maximum_fusion.refs_0_, f32[64,1024]{1,0:T(8,128)S(1)} %pad_maximum_fusion.1.refs_1_), custom_call_target="tpu_custom_call" | custom-call | tf_op jit(solution)/shard_map/score/pallas_call | solution.py:370
  24.6 0.5 %collective-permute-start.10 = (f32[32,256]{1,0:T(8,128)S(1)}, f32[32,256]{1,0:T(8,128)S(1)}, u32[]{:S(2)}, u32[]{:S(2)}) collective-permute-start(f32[32,256]{1,0:T(8,128)S(1)} %score.1.kept_ref), channel_id=1, source_target_pairs={{0,1},{1,0},{2,3},{3,2},{4,5},{5,4},{6,7},{7,6},{8,9},{9,8},{10,11... | collective-permute-start | bytes 98312 | tf_op jit(solution)/shard_map/ppermute | solution.py:23
  25.0 0.9 %collective-permute-done.10.received_ref = f32[32,256]{1,0:T(8,128)S(1)} collective-permute-done((f32[32,256]{1,0:T(8,128)S(1)}, f32[32,256]{1,0:T(8,128)S(1)}, u32[]{:S(2)}, u32[]{:S(2)}) %collective-permute-start.10) | collective-permute-done | bytes 32800 | tf_op jit(solution)/shard_map/ppermute | solution.py:23
  25.9 0.7 %place.1 = f32[32,512]{1,0:T(8,128)} custom-call(f32[32,256]{1,0:T(8,128)S(1)} %score.1.kept_ref, f32[32,256]{1,0:T(8,128)S(1)} %collective-permute-done.10.received_ref), custom_call_target="tpu_custom_call" | custom-call | tf_op jit(solution)/shard_map/place/pallas_call | solution.py:394
  (28 shorter events, 0.5 us)
Async XLA Ops:
  0.0 6.4 %copy-start.1 = (bf16[512,2048]{1,0:T(8,128)(2,1)S(1)}, bf16[512,2048]{1,0:T(8,128)(2,1)}, u32[]{:S(2)}) copy-start(bf16[512,2048]{1,0:T(8,128)(2,1)} %a_ref.1) | copy-start | bytes 6291460
  0.0 6.4 %copy-start = (bf16[512,7168]{1,0:T(8,128)(2,1)S(1)}, bf16[512,7168]{1,0:T(8,128)(2,1)}, u32[]{:S(2)}) copy-start(bf16[512,7168]{1,0:T(8,128)(2,1)} %g_ref.1) | copy-start | bytes 22020100
  0.0 6.4 %copy-start.4 = (bf16[2048,32]{0,1:T(8,128)(2,1)S(1)}, bf16[2048,32]{0,1:T(8,128)(2,1)}, u32[]{:S(2)}) copy-start(bf16[2048,32]{0,1:T(8,128)(2,1)} %param.8) | copy-start | bytes 393220
  0.0 6.4 %copy-start.3 = (bf16[7168,32]{0,1:T(8,128)(2,1)S(1)}, bf16[7168,32]{0,1:T(8,128)(2,1)}, u32[]{:S(2)}) copy-start(bf16[7168,32]{0,1:T(8,128)(2,1)} %param.9) | copy-start | bytes 1376260
  1.2 8.5 %copy-start.5 = (s32[1,17]{1,0:T(1,128)S(1)}, s32[1,17]{1,0:T(1,128)}, u32[]{:S(2)}) copy-start(s32[1,17]{1,0:T(1,128)} %lengths_ref.1) | copy-start | bytes 208
  1.2 14.7 %collective-permute-start.6 = (f32[32,1024]{1,0:T(8,128)S(1)}, f32[32,1024]{1,0:T(8,128)S(1)}, u32[]{:S(2)}, u32[]{:S(2)}) collective-permute-start(f32[32,1024]{1,0:T(8,128)S(1)} %get-tuple-element.56), channel_id=1, source_target_pairs={{0,9},{1,8},{2,11},{3,10},{4,13},{5,12},{6,15},{7,14},{8,1},{9,0},... | collective-permute-start | bytes 393224 | tf_op jit(solution)/shard_map/ppermute | solution.py:23
  4.7 12.5 %collective-permute-start.8 = (f32[32,1024]{1,0:T(8,128)S(1)}, f32[32,1024]{1,0:T(8,128)S(1)}, u32[]{:S(2)}, u32[]{:S(2)}) collective-permute-start(f32[32,1024]{1,0:T(8,128)S(1)} %get-tuple-element.56), channel_id=1, source_target_pairs={{0,13},{1,12},{2,15},{3,14},{4,9},{5,8},{6,11},{7,10},{8,5},{9,4},... | collective-permute-start | bytes 393224 | tf_op jit(solution)/shard_map/ppermute | solution.py:23
  9.0 1.4 %collective-permute-start = (f32[64,512]{1,0:T(8,128)S(1)}, f32[64,512]{1,0:T(8,128)S(1)}, u32[]{:S(2)}, u32[]{:S(2)}) collective-permute-start(f32[64,512]{1,0:T(8,128)S(1)} %project.1.after_ref.own_ref), channel_id=1, source_target_pairs={{0,1},{1,0},{2,3},{3,2},{4,5},{5,4},{6,7},{7,6},{8,9},{9,8},{10,11... | collective-permute-start | bytes 393224 | tf_op jit(solution)/shard_map/ppermute | solution.py:23
  9.2 11.3 %collective-permute-start.4 = (f32[64,1024]{1,0:T(8,128)S(1)}, f32[64,1024]{1,0:T(8,128)S(1)}, u32[]{:S(2)}, u32[]{:S(2)}) collective-permute-start(f32[64,1024]{1,0:T(8,128)S(1)} %get-tuple-element.45.after_ref), channel_id=1, source_target_pairs={{0,5},{1,4},{2,7},{3,6},{4,1},{5,0},{6,3},{7,2},{8,13},{9,12},{10,... | collective-permute-start | bytes 786440 | tf_op jit(solution)/shard_map/ppermute | solution.py:23
  10.7 3.2 %collective-permute-start.1 = (f32[32,128]{1,0:T(8,128)S(1)}, f32[32,128]{1,0:T(8,128)S(1)}, u32[]{:S(2)}, u32[]{:S(2)}) collective-permute-start(f32[32,128]{1,0:T(8,128)S(1)} %fisher.1.after_ref), channel_id=1, source_target_pairs={{0,3},{1,2},{2,1},{3,0},{4,7},{5,6},{6,5},{7,4},{8,11},{9,10},{10,... | collective-permute-start | bytes 49160 | tf_op jit(solution)/shard_map/ppermute | solution.py:23
  12.9 7.6 %copy-start.2 = (f32[1,128,1024]{2,1,0:T(8,128)S(1)}, f32[1,128,1024]{2,1,0:T(8,128)}, u32[]{:S(2)}) copy-start(f32[1,128,1024]{2,1,0:T(8,128)} %own_ref.1) | copy-start | bytes 1572868
  13.0 7.0 %collective-permute-start.3 = (f32[1,16,1024]{2,1,0:T(8,128)S(1)}, f32[1,16,1024]{2,1,0:T(8,128)S(1)}, u32[]{:S(2)}, u32[]{:S(2)}) collective-permute-start(f32[1,16,1024]{2,1,0:T(8,128)S(1)} %hold.3), channel_id=1, source_target_pairs={{0,3},{1,2},{2,1},{3,0},{4,7},{5,6},{6,5},{7,4},{8,11},{9,10},{10,... | collective-permute-start | bytes 196616 | tf_op jit(solution)/shard_map/ppermute | solution.py:23
  13.9 4.2 %collective-permute-start.2 = (f32[32,128]{1,0:T(8,128)S(1)}, f32[32,128]{1,0:T(8,128)S(1)}, u32[]{:S(2)}, u32[]{:S(2)}) collective-permute-start(f32[32,128]{1,0:T(8,128)S(1)} %add.6.after_ref), channel_id=1, source_target_pairs={{0,9},{1,8},{2,11},{3,10},{4,13},{5,12},{6,15},{7,14},{8,1},{9,0},... | collective-permute-start | bytes 49160 | tf_op jit(solution)/shard_map/ppermute | solution.py:23
  15.9 8.0 %collective-permute-start.7 = (f32[32,1024]{1,0:T(8,128)S(1)}, f32[32,1024]{1,0:T(8,128)S(1)}, u32[]{:S(2)}, u32[]{:S(2)}) collective-permute-start(f32[32,1024]{1,0:T(8,128)S(1)} %hold.4), channel_id=1, source_target_pairs={{0,17},{1,16},{2,19},{3,18},{4,21},{5,20},{6,23},{7,22},{8,25},{9,... | collective-permute-start | bytes 393224 | tf_op jit(solution)/shard_map/ppermute | solution.py:23
  17.3 7.0 %collective-permute-start.9 = (f32[32,1024]{1,0:T(8,128)S(1)}, f32[32,1024]{1,0:T(8,128)S(1)}, u32[]{:S(2)}, u32[]{:S(2)}) collective-permute-start(f32[32,1024]{1,0:T(8,128)S(1)} %hold.5), channel_id=1, source_target_pairs={{0,17},{1,16},{2,19},{3,18},{4,21},{5,20},{6,23},{7,22},{8,25},{9,... | collective-permute-start | bytes 393224 | tf_op jit(solution)/shard_map/ppermute | solution.py:23
  18.1 3.3 %collective-permute-start.5 = (f32[32,128]{1,0:T(8,128)S(1)}, f32[32,128]{1,0:T(8,128)S(1)}, u32[]{:S(2)}, u32[]{:S(2)}) collective-permute-start(f32[32,128]{1,0:T(8,128)S(1)} %add.7.own_ref), channel_id=1, source_target_pairs={{0,5},{1,4},{2,7},{3,6},{4,1},{5,0},{6,3},{7,2},{8,13},{9,12},{10,... | collective-permute-start | bytes 49160 | tf_op jit(solution)/shard_map/ppermute | solution.py:23
  24.6 1.3 %collective-permute-start.10 = (f32[32,256]{1,0:T(8,128)S(1)}, f32[32,256]{1,0:T(8,128)S(1)}, u32[]{:S(2)}, u32[]{:S(2)}) collective-permute-start(f32[32,256]{1,0:T(8,128)S(1)} %score.1.kept_ref), channel_id=1, source_target_pairs={{0,1},{1,0},{2,3},{3,2},{4,5},{5,4},{6,7},{7,6},{8,9},{9,8},{10,11... | collective-permute-start | bytes 98312 | tf_op jit(solution)/shard_map/ppermute | solution.py:23

commit v10 on v8

--- a/solution.py
+++ b/solution.py
@@ -135,7 +135,7 @@
     both = own_ref[...] + other_ref[...]
     inputs, outputs = both[0:width], both[width : 2 * width]
     member, divisor = member_ref[...], count_ref[:, 0:1]
-    group = 8
+    group = 16
     for first in range(0, width, group):
         outer = jnp.concatenate([outputs[i : i + 1] * inputs for i in range(first, first + group)], axis=0)
         total = None
@@ -430,7 +430,7 @@
     group_bits = [b * unit * n_dp for b in bits_of(groups)]
 
     half, piece = pick_queries(queries, groups)
-    fetched = [swap(piece, mesh, r * unit | core_bit) for r in range(2, n_dp)]
+    fetched = [swap(piece, mesh, r * unit | core_bit) for r in range(n_dp - 1, 1, -1)][::-1]
 
     own = project(activations, out_grads, proj_in, proj_out, half)
     half, own = lax.optimization_barrier((half, own))
@@ -452,7 +452,7 @@
             blocks = jnp.concatenate([blocks, swap(blocks, mesh, query_bits[i] | core_bit)], axis=0)
         if stage in Y_STAGES:
             first, end = (1, n_dp - 1)
-            for r in range(first, end):
+            for r in range(end - 1, first - 1, -1):
                 fetched[r] = hold(fetched[r], factor)
                 for bit in group_bits:
                     fetched[r] = jnp.concatenate([fetched[r], swap(fetched[r], mesh, bit)], axis=0)

time: 26.8 us -> 26.8 us (level)
  no operation moved by 1% of the time
where the time goes in v10:
time: 26.8 us; the launch traced here: 26.6 us
  starting transfers between devices  13.9 us (52%)
  Pallas kernels  9.34 us (35%)
  waiting for transfers between devices  3.22 us (12%)
    ppermute x11, starting transfers between devices, swap(): return lax.ppermute(value, AXES, [(i, i ^ mask) for i in range(count)])  13.9 us
    ppermute x11, waiting for transfers between devices, swap(): return lax.ppermute(value, AXES, [(i, i ^ mask) for i in range(count)])  3.22 us
    pallas_call x1, Pallas kernels, project(): pl.pallas_call(project_kernel, out_shape=jax.ShapeDtypeStruct((2 * proj_i...  2.6 us
    pallas_call x1, Pallas kernels, condition(): pl.pallas_call(condition_kernel, out_shape=(jax.ShapeDtypeStruct((columns...  2.54 us
    pallas_call x1, Pallas kernels, pick_queries(): pl.pallas_call(functools.partial(pick_kernel, groups), out_shape=tuple((j...  1.16 us
    pallas_call x1, Pallas kernels, example_grads(): pl.pallas_call(examples_kernel, out_shape=jax.ShapeDtypeStruct((member.sh...  0.96 us
    pallas_call x1, Pallas kernels, place(): pl.pallas_call(functools.partial(place_kernel, half), out_shape=jax.Shape...  0.72 us
    pallas_call x1, Pallas kernels, arrange_examples(): pl.pallas_call(functools.partial(arrange_examples_kernel, n_query), out_s...  0.56 us
  transfers between devices with their start and end apart: 11, of which 6 were waited for; matrix products, arithmetic and copies ran while one was open for 0% of the time, Pallas kernels for 27%

profile of v10, /device:TPU:0, one launch (start us, length us, event | category | flops | bytes accessed | tf_op | source)
XLA Modules:
  0.0 26.6 jit_solution(14868945528051969640)
XLA Ops:
  0.0 1.2 %pick_queries.1 = (f32[64,1024]{1,0:T(8,128)S(1)}, f32[32,1024]{1,0:T(8,128)S(1)}) custom-call(f32[1,128,1024]{2,1,0:T(8,128)} %own_ref.1), custom_call_target="tpu_custom_call" | custom-call | flops 4000000000 | bytes 1000000 | tf_op jit(solution)/shard_map/pick_queries/pallas_call | solution.py:46
  1.2 3.6 %collective-permute-start.6 = (f32[32,1024]{1,0:T(8,128)S(1)}, f32[32,1024]{1,0:T(8,128)S(1)}, u32[]{:S(2)}, u32[]{:S(2)}) collective-permute-start(f32[32,1024]{1,0:T(8,128)S(1)} %get-tuple-element.56), channel_id=1, source_target_pairs={{0,9},{1,8},{2,11},{3,10},{4,13},{5,12},{6,15},{7,14},{8,1},{9,0},... | collective-permute-start | bytes 393224 | tf_op jit(solution)/shard_map/ppermute | solution.py:23
  4.7 1.6 %collective-permute-start.8 = (f32[32,1024]{1,0:T(8,128)S(1)}, f32[32,1024]{1,0:T(8,128)S(1)}, u32[]{:S(2)}, u32[]{:S(2)}) collective-permute-start(f32[32,1024]{1,0:T(8,128)S(1)} %get-tuple-element.56), channel_id=1, source_target_pairs={{0,13},{1,12},{2,15},{3,14},{4,9},{5,8},{6,11},{7,10},{8,5},{9,4},... | collective-permute-start | bytes 393224 | tf_op jit(solution)/shard_map/ppermute | solution.py:23
  6.4 2.6 %project.1.after_ref.own_ref = f32[64,512]{1,0:T(8,128)S(1)} custom-call(bf16[512,2048]{1,0:T(8,128)(2,1)S(1)} %copy-done.1, bf16[512,7168]{1,0:T(8,128)(2,1)S(1)} %copy-done, bf16[32,2048]{1,0:T(8,128)(2,1)S(1)} %bitcast.4, bf16[32,7168]{1,0:T(8,128)(2,1)S(1)} %bitcast.3, f32[64,1024]{1,0:T(8,128)S(1)} %get-tuple-element.45.after_ref), custom_call_target="tpu_custom_call" | custom-call | tf_op jit(solution)/shard_map/project/pallas_call | solution.py:65
  9.0 0.2 collective-permute-start
  9.2 0.5 %collective-permute-start.4 = (f32[64,1024]{1,0:T(8,128)S(1)}, f32[64,1024]{1,0:T(8,128)S(1)}, u32[]{:S(2)}, u32[]{:S(2)}) collective-permute-start(f32[64,1024]{1,0:T(8,128)S(1)} %get-tuple-element.45.after_ref), channel_id=1, source_target_pairs={{0,5},{1,4},{2,7},{3,6},{4,1},{5,0},{6,3},{7,2},{8,13},{9,12},{10,... | collective-permute-start | bytes 786440 | tf_op jit(solution)/shard_map/ppermute | solution.py:23
  9.8 0.6 %collective-permute-done.other_ref = f32[64,512]{1,0:T(8,128)S(1)} collective-permute-done((f32[64,512]{1,0:T(8,128)S(1)}, f32[64,512]{1,0:T(8,128)S(1)}, u32[]{:S(2)}, u32[]{:S(2)}) %collective-permute-start) | collective-permute-done | bytes 131104 | tf_op jit(solution)/shard_map/ppermute | solution.py:23
  10.4 0.3 fisher.1.after_ref
  10.7 1.3 %collective-permute-start.1 = (f32[32,128]{1,0:T(8,128)S(1)}, f32[32,128]{1,0:T(8,128)S(1)}, u32[]{:S(2)}, u32[]{:S(2)}) collective-permute-start(f32[32,128]{1,0:T(8,128)S(1)} %fisher.1.after_ref), channel_id=1, source_target_pairs={{0,3},{1,2},{2,1},{3,0},{4,7},{5,6},{6,5},{7,4},{8,11},{9,10},{10,... | collective-permute-start | bytes 49160 | tf_op jit(solution)/shard_map/ppermute | solution.py:23
  12.0 1.0 %examples.1 = f32[16,1024]{1,0:T(8,128)S(1)} custom-call(bf16[16,512]{1,0:T(8,128)(2,1)S(1)} %get-tuple-element.38.member_ref, f32[16,128]{1,0:T(8,128)S(1)} %get-tuple-element.39.count_ref, f32[64,512]{1,0:T(8,128)S(1)} %project.1.after_ref.own_ref, f32[64,512]{1,0:T(8,128)S(1)} %collective-permute-done.other_ref), custom_call_target="tpu_custom_call" | custom-call | flops 2000000000 | bytes 1000000 | tf_op jit(solution)/shard_map/examples/pallas_call | solution.py:150
  13.0 0.6 %collective-permute-start.3 = (f32[1,16,1024]{2,1,0:T(8,128)S(1)}, f32[1,16,1024]{2,1,0:T(8,128)S(1)}, u32[]{:S(2)}, u32[]{:S(2)}) collective-permute-start(f32[1,16,1024]{2,1,0:T(8,128)S(1)} %hold.3), channel_id=1, source_target_pairs={{0,3},{1,2},{2,1},{3,0},{4,7},{5,6},{6,5},{7,4},{8,11},{9,10},{10,... | collective-permute-start | bytes 196616 | tf_op jit(solution)/shard_map/ppermute | solution.py:23
  13.5 0.4 %collective-permute-done.1 = f32[32,128]{1,0:T(8,128)S(1)} collective-permute-done((f32[32,128]{1,0:T(8,128)S(1)}, f32[32,128]{1,0:T(8,128)S(1)}, u32[]{:S(2)}, u32[]{:S(2)}) %collective-permute-start.1) | collective-permute-done | bytes 16416 | tf_op jit(solution)/shard_map/ppermute | solution.py:23
  13.9 2.0 %collective-permute-start.2 = (f32[32,128]{1,0:T(8,128)S(1)}, f32[32,128]{1,0:T(8,128)S(1)}, u32[]{:S(2)}, u32[]{:S(2)}) collective-permute-start(f32[32,128]{1,0:T(8,128)S(1)} %add.6.after_ref), channel_id=1, source_target_pairs={{0,9},{1,8},{2,11},{3,10},{4,13},{5,12},{6,15},{7,14},{8,1},{9,0},... | collective-permute-start | bytes 49160 | tf_op jit(solution)/shard_map/ppermute | solution.py:23
  15.9 1.6 %collective-permute-start.7 = (f32[32,1024]{1,0:T(8,128)S(1)}, f32[32,1024]{1,0:T(8,128)S(1)}, u32[]{:S(2)}, u32[]{:S(2)}) collective-permute-start(f32[32,1024]{1,0:T(8,128)S(1)} %hold.4), channel_id=1, source_target_pairs={{0,16},{1,17},{2,18},{3,19},{4,20},{5,21},{6,22},{7,23},{8,24},{9,... | collective-permute-start | bytes 393224 | tf_op jit(solution)/shard_map/ppermute | solution.py:23
  17.5 0.6 %collective-permute-start.9 = (f32[32,1024]{1,0:T(8,128)S(1)}, f32[32,1024]{1,0:T(8,128)S(1)}, u32[]{:S(2)}, u32[]{:S(2)}) collective-permute-start(f32[32,1024]{1,0:T(8,128)S(1)} %hold.5), channel_id=1, source_target_pairs={{0,16},{1,17},{2,18},{3,19},{4,20},{5,21},{6,22},{7,23},{8,24},{9,... | collective-permute-start | bytes 393224 | tf_op jit(solution)/shard_map/ppermute | solution.py:23
  18.1 1.6 %collective-permute-start.5 = (f32[32,128]{1,0:T(8,128)S(1)}, f32[32,128]{1,0:T(8,128)S(1)}, u32[]{:S(2)}, u32[]{:S(2)}) collective-permute-start(f32[32,128]{1,0:T(8,128)S(1)} %add.7.own_ref), channel_id=1, source_target_pairs={{0,5},{1,4},{2,7},{3,6},{4,1},{5,0},{6,3},{7,2},{8,13},{9,12},{10,... | collective-permute-start | bytes 49160 | tf_op jit(solution)/shard_map/ppermute | solution.py:23
  19.7 0.6 %arrange_examples.1 = (bf16[128,256]{1,0:T(8,128)(2,1)S(1)}, bf16[128,256]{1,0:T(8,128)(2,1)S(1)}, bf16[128,256]{1,0:T(8,128)(2,1)S(1)}) custom-call(f32[2,16,1024]{2,1,0:T(8,128)S(1)} %pad_maximum_fusion.2.blocks_ref), custom_call_target="tpu_custom_call" | custom-call | tf_op jit(solution)/shard_map/arrange_examples/pallas_call | solution.py:194
  20.4 0.9 %collective-permute-done.5.other_ref = f32[32,128]{1,0:T(8,128)S(1)} collective-permute-done((f32[32,128]{1,0:T(8,128)S(1)}, f32[32,128]{1,0:T(8,128)S(1)}, u32[]{:S(2)}, u32[]{:S(2)}) %collective-permute-start.5) | collective-permute-done | bytes 16416 | tf_op jit(solution)/shard_map/ppermute | solution.py:23
  21.3 2.5 %condition.1 = (bf16[4,64,256]{2,1,0:T(8,128)(2,1)S(1)}, f32[32,128]{1,0:T(8,128)S(1)}) custom-call(f32[32,128]{1,0:T(8,128)S(1)} %add.7.own_ref, f32[32,128]{1,0:T(8,128)S(1)} %collective-permute-done.5.other_ref, bf16[128,256]{1,0:T(8,128)(2,1)S(1)} %get-tuple-element.49.high_ref, bf16[128,256]{1,0:T(8,128)(2,1)S(1)} %get-tuple-element.50.middle_ref, ...), custom_call_target="tpu_custom_call" | custom-call | flops 4000000000 | bytes 1000000 | tf_op jit(solution)/shard_map/condition/pallas_call | solution.py:338
  23.9 0.4 %collective-permute-done.9 = f32[32,1024]{1,0:T(8,128)S(1)} collective-permute-done((f32[32,1024]{1,0:T(8,128)S(1)}, f32[32,1024]{1,0:T(8,128)S(1)}, u32[]{:S(2)}, u32[]{:S(2)}) %collective-permute-start.9) | collective-permute-done | bytes 131104 | tf_op jit(solution)/shard_map/ppermute | solution.py:23
  24.4 0.3 %score.1.kept_ref = f32[32,256]{1,0:T(8,128)S(1)} custom-call(bf16[4,64,256]{2,1,0:T(8,128)(2,1)S(1)} %get-tuple-element.54.both_ref, f32[32,128]{1,0:T(8,128)S(1)} %get-tuple-element.55.near_ref, f32[64,1024]{1,0:T(8,128)S(1)} %pad_maximum_fusion.refs_0_, f32[64,1024]{1,0:T(8,128)S(1)} %pad_maximum_fusion.1.refs_1_), custom_call_target="tpu_custom_call" | custom-call | tf_op jit(solution)/shard_map/score/pallas_call | solution.py:369
  24.7 0.4 %collective-permute-start.10 = (f32[32,256]{1,0:T(8,128)S(1)}, f32[32,256]{1,0:T(8,128)S(1)}, u32[]{:S(2)}, u32[]{:S(2)}) collective-permute-start(f32[32,256]{1,0:T(8,128)S(1)} %score.1.kept_ref), channel_id=1, source_target_pairs={{0,1},{1,0},{2,3},{3,2},{4,5},{5,4},{6,7},{7,6},{8,9},{9,8},{10,11... | collective-permute-start | bytes 98312 | tf_op jit(solution)/shard_map/ppermute | solution.py:23
  25.1 0.9 %collective-permute-done.10.received_ref = f32[32,256]{1,0:T(8,128)S(1)} collective-permute-done((f32[32,256]{1,0:T(8,128)S(1)}, f32[32,256]{1,0:T(8,128)S(1)}, u32[]{:S(2)}, u32[]{:S(2)}) %collective-permute-start.10) | collective-permute-done | bytes 32800 | tf_op jit(solution)/shard_map/ppermute | solution.py:23
  25.9 0.7 %place.1 = f32[32,512]{1,0:T(8,128)} custom-call(f32[32,256]{1,0:T(8,128)S(1)} %score.1.kept_ref, f32[32,256]{1,0:T(8,128)S(1)} %collective-permute-done.10.received_ref), custom_call_target="tpu_custom_call" | custom-call | tf_op jit(solution)/shard_map/place/pallas_call | solution.py:393
  (28 shorter events, 0.4 us)
Async XLA Ops:
  0.0 6.4 %copy-start.1 = (bf16[512,2048]{1,0:T(8,128)(2,1)S(1)}, bf16[512,2048]{1,0:T(8,128)(2,1)}, u32[]{:S(2)}) copy-start(bf16[512,2048]{1,0:T(8,128)(2,1)} %a_ref.1) | copy-start | bytes 6291460
  0.0 6.4 %copy-start = (bf16[512,7168]{1,0:T(8,128)(2,1)S(1)}, bf16[512,7168]{1,0:T(8,128)(2,1)}, u32[]{:S(2)}) copy-start(bf16[512,7168]{1,0:T(8,128)(2,1)} %g_ref.1) | copy-start | bytes 22020100
  0.0 6.4 %copy-start.4 = (bf16[2048,32]{0,1:T(8,128)(2,1)S(1)}, bf16[2048,32]{0,1:T(8,128)(2,1)}, u32[]{:S(2)}) copy-start(bf16[2048,32]{0,1:T(8,128)(2,1)} %param.8) | copy-start | bytes 393220
  0.0 6.4 %copy-start.3 = (bf16[7168,32]{0,1:T(8,128)(2,1)S(1)}, bf16[7168,32]{0,1:T(8,128)(2,1)}, u32[]{:S(2)}) copy-start(bf16[7168,32]{0,1:T(8,128)(2,1)} %param.9) | copy-start | bytes 1376260
  1.2 8.6 %copy-start.5 = (s32[1,17]{1,0:T(1,128)S(1)}, s32[1,17]{1,0:T(1,128)}, u32[]{:S(2)}) copy-start(s32[1,17]{1,0:T(1,128)} %lengths_ref.1) | copy-start | bytes 208
  1.2 14.7 %collective-permute-start.6 = (f32[32,1024]{1,0:T(8,128)S(1)}, f32[32,1024]{1,0:T(8,128)S(1)}, u32[]{:S(2)}, u32[]{:S(2)}) collective-permute-start(f32[32,1024]{1,0:T(8,128)S(1)} %get-tuple-element.56), channel_id=1, source_target_pairs={{0,9},{1,8},{2,11},{3,10},{4,13},{5,12},{6,15},{7,14},{8,1},{9,0},... | collective-permute-start | bytes 393224 | tf_op jit(solution)/shard_map/ppermute | solution.py:23
  4.7 12.7 %collective-permute-start.8 = (f32[32,1024]{1,0:T(8,128)S(1)}, f32[32,1024]{1,0:T(8,128)S(1)}, u32[]{:S(2)}, u32[]{:S(2)}) collective-permute-start(f32[32,1024]{1,0:T(8,128)S(1)} %get-tuple-element.56), channel_id=1, source_target_pairs={{0,13},{1,12},{2,15},{3,14},{4,9},{5,8},{6,11},{7,10},{8,5},{9,4},... | collective-permute-start | bytes 393224 | tf_op jit(solution)/shard_map/ppermute | solution.py:23
  9.0 1.4 %collective-permute-start = (f32[64,512]{1,0:T(8,128)S(1)}, f32[64,512]{1,0:T(8,128)S(1)}, u32[]{:S(2)}, u32[]{:S(2)}) collective-permute-start(f32[64,512]{1,0:T(8,128)S(1)} %project.1.after_ref.own_ref), channel_id=1, source_target_pairs={{0,1},{1,0},{2,3},{3,2},{4,5},{5,4},{6,7},{7,6},{8,9},{9,8},{10,11... | collective-permute-start | bytes 393224 | tf_op jit(solution)/shard_map/ppermute | solution.py:23
  9.2 11.1 %collective-permute-start.4 = (f32[64,1024]{1,0:T(8,128)S(1)}, f32[64,1024]{1,0:T(8,128)S(1)}, u32[]{:S(2)}, u32[]{:S(2)}) collective-permute-start(f32[64,1024]{1,0:T(8,128)S(1)} %get-tuple-element.45.after_ref), channel_id=1, source_target_pairs={{0,5},{1,4},{2,7},{3,6},{4,1},{5,0},{6,3},{7,2},{8,13},{9,12},{10,... | collective-permute-start | bytes 786440 | tf_op jit(solution)/shard_map/ppermute | solution.py:23
  10.7 3.2 %collective-permute-start.1 = (f32[32,128]{1,0:T(8,128)S(1)}, f32[32,128]{1,0:T(8,128)S(1)}, u32[]{:S(2)}, u32[]{:S(2)}) collective-permute-start(f32[32,128]{1,0:T(8,128)S(1)} %fisher.1.after_ref), channel_id=1, source_target_pairs={{0,3},{1,2},{2,1},{3,0},{4,7},{5,6},{6,5},{7,4},{8,11},{9,10},{10,... | collective-permute-start | bytes 49160 | tf_op jit(solution)/shard_map/ppermute | solution.py:23
  12.9 7.4 %copy-start.2 = (f32[1,128,1024]{2,1,0:T(8,128)S(1)}, f32[1,128,1024]{2,1,0:T(8,128)}, u32[]{:S(2)}) copy-start(f32[1,128,1024]{2,1,0:T(8,128)} %own_ref.1) | copy-start | bytes 1572868
  13.0 6.7 %collective-permute-start.3 = (f32[1,16,1024]{2,1,0:T(8,128)S(1)}, f32[1,16,1024]{2,1,0:T(8,128)S(1)}, u32[]{:S(2)}, u32[]{:S(2)}) collective-permute-start(f32[1,16,1024]{2,1,0:T(8,128)S(1)} %hold.3), channel_id=1, source_target_pairs={{0,3},{1,2},{2,1},{3,0},{4,7},{5,6},{6,5},{7,4},{8,11},{9,10},{10,... | collective-permute-start | bytes 196616 | tf_op jit(solution)/shard_map/ppermute | solution.py:23
  13.9 4.2 %collective-permute-start.2 = (f32[32,128]{1,0:T(8,128)S(1)}, f32[32,128]{1,0:T(8,128)S(1)}, u32[]{:S(2)}, u32[]{:S(2)}) collective-permute-start(f32[32,128]{1,0:T(8,128)S(1)} %add.6.after_ref), channel_id=1, source_target_pairs={{0,9},{1,8},{2,11},{3,10},{4,13},{5,12},{6,15},{7,14},{8,1},{9,0},... | collective-permute-start | bytes 49160 | tf_op jit(solution)/shard_map/ppermute | solution.py:23
  15.9 8.0 %collective-permute-start.7 = (f32[32,1024]{1,0:T(8,128)S(1)}, f32[32,1024]{1,0:T(8,128)S(1)}, u32[]{:S(2)}, u32[]{:S(2)}) collective-permute-start(f32[32,1024]{1,0:T(8,128)S(1)} %hold.4), channel_id=1, source_target_pairs={{0,16},{1,17},{2,18},{3,19},{4,20},{5,21},{6,22},{7,23},{8,24},{9,... | collective-permute-start | bytes 393224 | tf_op jit(solution)/shard_map/ppermute | solution.py:23
  17.5 6.8 %collective-permute-start.9 = (f32[32,1024]{1,0:T(8,128)S(1)}, f32[32,1024]{1,0:T(8,128)S(1)}, u32[]{:S(2)}, u32[]{:S(2)}) collective-permute-start(f32[32,1024]{1,0:T(8,128)S(1)} %hold.5), channel_id=1, source_target_pairs={{0,16},{1,17},{2,18},{3,19},{4,20},{5,21},{6,22},{7,23},{8,24},{9,... | collective-permute-start | bytes 393224 | tf_op jit(solution)/shard_map/ppermute | solution.py:23
  18.1 3.2 %collective-permute-start.5 = (f32[32,128]{1,0:T(8,128)S(1)}, f32[32,128]{1,0:T(8,128)S(1)}, u32[]{:S(2)}, u32[]{:S(2)}) collective-permute-start(f32[32,128]{1,0:T(8,128)S(1)} %add.7.own_ref), channel_id=1, source_target_pairs={{0,5},{1,4},{2,7},{3,6},{4,1},{5,0},{6,3},{7,2},{8,13},{9,12},{10,... | collective-permute-start | bytes 49160 | tf_op jit(solution)/shard_map/ppermute | solution.py:23
  24.7 1.2 %collective-permute-start.10 = (f32[32,256]{1,0:T(8,128)S(1)}, f32[32,256]{1,0:T(8,128)S(1)}, u32[]{:S(2)}, u32[]{:S(2)}) collective-permute-start(f32[32,256]{1,0:T(8,128)S(1)} %score.1.kept_ref), channel_id=1, source_target_pairs={{0,1},{1,0},{2,3},{3,2},{4,5},{5,4},{6,7},{7,6},{8,9},{9,8},{10,11... | collective-permute-start | bytes 98312 | tf_op jit(solution)/shard_map/ppermute | solution.py:23
